TPU v7x, 32 devices: a whole 2x2x4 slice. The times are simulated.
32 devices in a mesh: groups: 2 (over x), blk: 16 (over z, y, core).
Axes of the slice: x: 2, y: 2, z: 4, core: 2. Of those that a mesh axis runs over, the one named last changes fastest.
Arguments:
- fitted_slab: float32 [2048, 14400], P('blk', 'groups'), parts along dimension 1, may hold values from -0.8 to 0.8
- pair_list: int32 [16, 8], replicated, may hold values from -1 to 7, as said below
Outputs:
- exchange_band: float32 [4096, 1920], P(('groups', 'blk')), parts along dimension 0
There are 2 independent parts, one for each index of `groups`. A program takes and returns all parts, laid end to end along the dimension named above; an argument that names none is the same for every part. Nothing has to cross between parts.
Inputs may be any that keep to these rules, and one draw needn't show every extreme that they name: `pair_list`: each row lists distinct offsets in increasing order, then -1 padding; offset 0 is always listed; a + d < 16 for every listed offset d of row a; row 0 lists all offsets.
All inputs are finite; a program needn't handle non-finite values.
Results may differ from a plain program's by a relative error of at most 0.0003.
Values sent between devices are 32-bit elements; how exact they have to be, the bound alone decides.
No kernel may reach another device: no remote copies, remote signals or barrier semaphores. Data moves between devices by JAX's collectives and lax.ppermute only.
A program may use at most 128 MiB of HBM per device.

v0:
```python
import jax
import jax.numpy as jnp
from jax import lax
from jax.sharding import PartitionSpec as P


def passed_along(block, axis, distance):
    devices = range(lax.axis_size(axis))
    route = [(i - distance, i) for i in devices if i - distance in devices]
    return lax.ppermute(block, axis, route)


def send_back(pieces):
    results = []
    for offset_value, block in pieces:
        results.append(passed_along(block, "blk", offset_value))
    return results


def body(fitted_slab, pair_list):
    block_rows = fitted_slab.shape[0]
    max_offset = pair_list.shape[1] - 1
    my_index = lax.axis_index("blk")
    offset_range = jnp.arange(max_offset + 1, dtype=jnp.int32)
    present_all = jnp.any(pair_list[:, :, None] == offset_range[None, None, :], axis=1).astype(
        jnp.float32
    )
    present = lax.dynamic_index_in_dim(present_all, my_index, 0, keepdims=False)
    near_count = max_offset + 1
    pieces = [fitted_slab]
    for distance in range(1, max_offset + 1):
        pieces.append(passed_along(fitted_slab, "blk", -distance))
    stacked = jnp.stack(pieces)
    products = jnp.einsum("mk,jnk->jmn", fitted_slab, stacked, precision=lax.Precision.HIGHEST)
    own_band = products * present[:near_count, None, None]
    outgoing = [(distance, own_band[distance]) for distance in range(1, near_count)]
    lower_local = {}
    received = send_back(outgoing)
    upper_slots = {distance: own_band[distance] for distance in range(near_count)}
    lower_slots = dict(lower_local)
    for (offset_value, block), arrived in zip(outgoing, received):
        lower_slots[offset_value] = arrived.T
    ordered = [lower_slots[max_offset - slot] for slot in range(max_offset)]
    ordered = ordered + [upper_slots[distance] for distance in range(max_offset + 1)]
    band = jnp.stack(ordered, 0)
    return band.transpose(1, 0, 2).reshape(block_rows, (2 * max_offset + 1) * block_rows)


def solution(mesh):
    return jax.shard_map(
        body,
        mesh=mesh,
        in_specs=(P("blk", "groups"), P()),
        out_specs=P(("groups", "blk"), None),
        check_vma=False,
    )
```

profile of v0, /device:TPU:0, one launch (start us, length us, event | category | flops | bytes accessed | tf_op | source)
XLA Modules:
  0.0 788.5 jit_solution(16128709890858325098)
XLA Ops:
  0.0 1.3 collective-permute-start
  1.3 1.3 collective-permute-start.1
  2.6 1.3 collective-permute-start.2
  3.9 1.3 collective-permute-start.3
  5.2 1.3 collective-permute-start.4
  6.5 0.7 fusion.8
  7.2 0.2 dynamic-slice_reduce_fusion
  7.4 4.2 bitcast_dynamic-update-slice_fusion.7
  11.6 1.3 collective-permute-start.5
  12.9 4.1 bitcast_dynamic-update-slice_fusion.6
  17.1 145.8 %collective-permute-done.1 = f32[128,7200]{0,1:T(8,128)} collective-permute-done((f32[128,7200]{0,1:T(8,128)}, f32[128,7200]{0,1:T(8,128)}, u32[]{:S(2)}, u32[]{:S(2)}) %collective-permute-start.1) | collective-permute-done | bytes 3686432 | tf_op jit(solution)/shard_map/ppermute | solution.py:10
  162.9 1.3 collective-permute-start.6
  164.2 4.2 bitcast_dynamic-update-slice_fusion.5
  168.4 4.2 bitcast_dynamic-update-slice_fusion.4
  172.6 148.9 %collective-permute-done.3 = f32[128,7200]{0,1:T(8,128)} collective-permute-done((f32[128,7200]{0,1:T(8,128)}, f32[128,7200]{0,1:T(8,128)}, u32[]{:S(2)}, u32[]{:S(2)}) %collective-permute-start.3) | collective-permute-done | bytes 3686432 | tf_op jit(solution)/shard_map/ppermute | solution.py:10
  321.5 4.1 bitcast_dynamic-update-slice_fusion.3
  325.6 4.1 bitcast_dynamic-update-slice_fusion.2
  329.7 2.1 bitcast_dynamic-update-slice_fusion.1
  331.8 2.1 bitcast_dynamic-update-slice_fusion
  333.9 50.2 %fusion.5 = f32[8,128,128]{1,2,0:T(8,128)S(1)} fusion(f32[8,128,7200]{1,2,0:T(8,128)} %bitcast_dynamic-update-slice_fusion, f32[128,7200]{0,1:T(8,128)S(1)} %copy-done, f32[8]{0:T(128)S(1)} %dynamic-slice_reduce_fusion), kind=kOutput, calls=%fused_computation.11 | convolution fusion | flops 11324751872 | bytes 33701920 | tf_op jit(solution)/shard_map/mk,jnk->jmn/dot_general | solution.py:34
  384.2 0.1 copy.28
  384.3 80.0 %collective-permute-start.7 = (f32[128,128]{1,0:T(8,128)S(1)}, f32[128,128]{1,0:T(8,128)S(1)}, u32[]{:S(2)}, u32[]{:S(2)}) collective-permute-start(f32[128,128]{1,0:T(8,128)S(1)} %bitcast.71), channel_id=1, source_target_pairs={{0,7},{1,8},{2,9},{3,10},{4,11},{5,12},{6,13},{7,14},{8,15},{16,23... | collective-permute-start | bytes 196616 | tf_op jit(solution)/shard_map/ppermute | solution.py:10
  464.3 0.1 copy.29
  464.4 79.2 %collective-permute-start.8 = (f32[128,128]{1,0:T(8,128)S(1)}, f32[128,128]{1,0:T(8,128)S(1)}, u32[]{:S(2)}, u32[]{:S(2)}) collective-permute-start(f32[128,128]{1,0:T(8,128)S(1)} %bitcast.70), channel_id=1, source_target_pairs={{0,6},{1,7},{2,8},{3,9},{4,10},{5,11},{6,12},{7,13},{8,14},{9,15},... | collective-permute-start | bytes 196616 | tf_op jit(solution)/shard_map/ppermute | solution.py:10
  543.7 37.7 %collective-permute-start.9 = (f32[128,128]{1,0:T(8,128)S(1)}, f32[128,128]{1,0:T(8,128)S(1)}, u32[]{:S(2)}, u32[]{:S(2)}) collective-permute-start(f32[128,128]{1,0:T(8,128)S(1)} %bitcast.69), channel_id=1, source_target_pairs={{0,5},{1,6},{2,7},{3,8},{4,9},{5,10},{6,11},{7,12},{8,13},{9,14},{... | collective-permute-start | bytes 196616 | tf_op jit(solution)/shard_map/ppermute | solution.py:10
  581.5 160.3 %collective-permute-start.10 = (f32[128,128]{1,0:T(8,128)S(1)}, f32[128,128]{1,0:T(8,128)S(1)}, u32[]{:S(2)}, u32[]{:S(2)}) collective-permute-start(f32[128,128]{1,0:T(8,128)S(1)} %bitcast.68), channel_id=1, source_target_pairs={{0,4},{1,5},{2,6},{3,7},{4,8},{5,9},{6,10},{7,11},{8,12},{9,13},{1... | collective-permute-start | bytes 196616 | tf_op jit(solution)/shard_map/ppermute | solution.py:10
  741.9 40.2 %collective-permute-start.11 = (f32[128,128]{1,0:T(8,128)S(1)}, f32[128,128]{1,0:T(8,128)S(1)}, u32[]{:S(2)}, u32[]{:S(2)}) collective-permute-start(f32[128,128]{1,0:T(8,128)S(1)} %bitcast.67), channel_id=1, source_target_pairs={{0,3},{1,4},{2,5},{3,6},{4,7},{5,8},{6,9},{7,10},{8,11},{9,12},{10... | collective-permute-start | bytes 196616 | tf_op jit(solution)/shard_map/ppermute | solution.py:10
  782.2 0.1 copy.34
  782.3 1.3 collective-permute-start.12
  783.7 2.6 collective-permute-start.13
  786.4 0.8 collective-permute-done.13
  787.3 1.3 copy.27
  (27 shorter events, 0.5 us)
Async XLA Ops:
  0.0 11.6 %collective-permute-start = (f32[128,7200]{0,1:T(8,128)}, f32[128,7200]{0,1:T(8,128)}, u32[]{:S(2)}, u32[]{:S(2)}) collective-permute-start(f32[128,7200]{0,1:T(8,128)} %param.2), channel_id=1, source_target_pairs={{1,0},{2,1},{3,2},{4,3},{5,4},{6,5},{7,6},{8,7},{9,8},{10,9},{11,1... | collective-permute-start | bytes 11059208 | tf_op jit(solution)/shard_map/ppermute | solution.py:10
  1.3 161.6 %collective-permute-start.1 = (f32[128,7200]{0,1:T(8,128)}, f32[128,7200]{0,1:T(8,128)}, u32[]{:S(2)}, u32[]{:S(2)}) collective-permute-start(f32[128,7200]{0,1:T(8,128)} %param.2), channel_id=1, source_target_pairs={{2,0},{3,1},{4,2},{5,3},{6,4},{7,5},{8,6},{9,7},{10,8},{11,9},{12,... | collective-permute-start | bytes 11059208 | tf_op jit(solution)/shard_map/ppermute | solution.py:10
  2.6 165.8 %collective-permute-start.2 = (f32[128,7200]{0,1:T(8,128)}, f32[128,7200]{0,1:T(8,128)}, u32[]{:S(2)}, u32[]{:S(2)}) collective-permute-start(f32[128,7200]{0,1:T(8,128)} %param.2), channel_id=1, source_target_pairs={{3,0},{4,1},{5,2},{6,3},{7,4},{8,5},{9,6},{10,7},{11,8},{12,9},{13... | collective-permute-start | bytes 11059208 | tf_op jit(solution)/shard_map/ppermute | solution.py:10
  3.9 317.6 %collective-permute-start.3 = (f32[128,7200]{0,1:T(8,128)}, f32[128,7200]{0,1:T(8,128)}, u32[]{:S(2)}, u32[]{:S(2)}) collective-permute-start(f32[128,7200]{0,1:T(8,128)} %param.2), channel_id=1, source_target_pairs={{4,0},{5,1},{6,2},{7,3},{8,4},{9,5},{10,6},{11,7},{12,8},{13,9},{1... | collective-permute-start | bytes 11059208 | tf_op jit(solution)/shard_map/ppermute | solution.py:10
  5.2 320.4 %collective-permute-start.4 = (f32[128,7200]{0,1:T(8,128)}, f32[128,7200]{0,1:T(8,128)}, u32[]{:S(2)}, u32[]{:S(2)}) collective-permute-start(f32[128,7200]{0,1:T(8,128)} %param.2), channel_id=1, source_target_pairs={{5,0},{6,1},{7,2},{8,3},{9,4},{10,5},{11,6},{12,7},{13,8},{14,9},{... | collective-permute-start | bytes 11059208 | tf_op jit(solution)/shard_map/ppermute | solution.py:10
  7.4 326.5 %copy-start = (f32[128,7200]{0,1:T(8,128)S(1)}, f32[128,7200]{0,1:T(8,128)}, u32[]{:S(2)}) copy-start(f32[128,7200]{0,1:T(8,128)} %param.2) | copy-start | bytes 11059204
  11.6 318.1 %collective-permute-start.5 = (f32[128,7200]{0,1:T(8,128)}, f32[128,7200]{0,1:T(8,128)S(1)}, u32[]{:S(2)}, u32[]{:S(2)}) collective-permute-start(f32[128,7200]{0,1:T(8,128)} %param.2), channel_id=1, source_target_pairs={{6,0},{7,1},{8,2},{9,3},{10,4},{11,5},{12,6},{13,7},{14,8},{15,9},... | collective-permute-start | bytes 11059208 | tf_op jit(solution)/shard_map/ppermute | solution.py:10
  162.9 168.9 %collective-permute-start.6 = (f32[128,7200]{0,1:T(8,128)}, f32[128,7200]{0,1:T(8,128)S(1)}, u32[]{:S(2)}, u32[]{:S(2)}) collective-permute-start(f32[128,7200]{0,1:T(8,128)} %param.2), channel_id=1, source_target_pairs={{7,0},{8,1},{9,2},{10,3},{11,4},{12,5},{13,6},{14,7},{15,8},{23,16... | collective-permute-start | bytes 11059208 | tf_op jit(solution)/shard_map/ppermute | solution.py:10
  384.3 398.1 %collective-permute-start.7 = (f32[128,128]{1,0:T(8,128)S(1)}, f32[128,128]{1,0:T(8,128)S(1)}, u32[]{:S(2)}, u32[]{:S(2)}) collective-permute-start(f32[128,128]{1,0:T(8,128)S(1)} %bitcast.71), channel_id=1, source_target_pairs={{0,7},{1,8},{2,9},{3,10},{4,11},{5,12},{6,13},{7,14},{8,15},{16,23... | collective-permute-start | bytes 196616 | tf_op jit(solution)/shard_map/ppermute | solution.py:10
  464.4 319.3 %collective-permute-start.8 = (f32[128,128]{1,0:T(8,128)S(1)}, f32[128,128]{1,0:T(8,128)S(1)}, u32[]{:S(2)}, u32[]{:S(2)}) collective-permute-start(f32[128,128]{1,0:T(8,128)S(1)} %bitcast.70), channel_id=1, source_target_pairs={{0,6},{1,7},{2,8},{3,9},{4,10},{5,11},{6,12},{7,13},{8,14},{9,15},... | collective-permute-start | bytes 196616 | tf_op jit(solution)/shard_map/ppermute | solution.py:10
  543.7 242.7 %collective-permute-start.9 = (f32[128,128]{1,0:T(8,128)S(1)}, f32[128,128]{1,0:T(8,128)S(1)}, u32[]{:S(2)}, u32[]{:S(2)}) collective-permute-start(f32[128,128]{1,0:T(8,128)S(1)} %bitcast.69), channel_id=1, source_target_pairs={{0,5},{1,6},{2,7},{3,8},{4,9},{5,10},{6,11},{7,12},{8,13},{9,14},{... | collective-permute-start | bytes 196616 | tf_op jit(solution)/shard_map/ppermute | solution.py:10
  581.5 204.9 %collective-permute-start.10 = (f32[128,128]{1,0:T(8,128)S(1)}, f32[128,128]{1,0:T(8,128)S(1)}, u32[]{:S(2)}, u32[]{:S(2)}) collective-permute-start(f32[128,128]{1,0:T(8,128)S(1)} %bitcast.68), channel_id=1, source_target_pairs={{0,4},{1,5},{2,6},{3,7},{4,8},{5,9},{6,10},{7,11},{8,12},{9,13},{1... | collective-permute-start | bytes 196616 | tf_op jit(solution)/shard_map/ppermute | solution.py:10
  741.9 44.5 %collective-permute-start.11 = (f32[128,128]{1,0:T(8,128)S(1)}, f32[128,128]{1,0:T(8,128)S(1)}, u32[]{:S(2)}, u32[]{:S(2)}) collective-permute-start(f32[128,128]{1,0:T(8,128)S(1)} %bitcast.67), channel_id=1, source_target_pairs={{0,3},{1,4},{2,5},{3,6},{4,7},{5,8},{6,9},{7,10},{8,11},{9,12},{10... | collective-permute-start | bytes 196616 | tf_op jit(solution)/shard_map/ppermute | solution.py:10
  782.3 4.1 collective-permute-start.12
  783.7 3.5 collective-permute-start.13
where the time goes:
time: 791 us; the launch traced here: 789 us
  starting transfers between devices  410 us (52%)
  waiting for transfers between devices  296 us (37%)
  matrix products  50.2 us (6%)
  local copies, waits for them, and re-layouts  31.3 us (4%)
    ppermute x14, starting transfers between devices, passed_along(): return lax.ppermute(block, axis, route)  410 us
    ppermute x14, waiting for transfers between devices, passed_along(): return lax.ppermute(block, axis, route)  296 us
    dot_general x1, matrix products, body(): jnp.einsum('mk,jnk->jmn', fitted_slab, stacked, precision=lax.Precision.H...  50.2 us
    unnamed x23, local copies, waits for them, and re-layouts  27.7 us
  transfers between devices with their start and end apart: 14, of which 3 were waited for; matrix products, arithmetic and copies ran while one was open for 4% of the time, Pallas kernels for 0%

commit v1 on v0

v1 whole, which is shorter than its diff:
```python
import functools

import jax
import jax.numpy as jnp
from jax import lax
from jax.sharding import PartitionSpec as P

PLANE = 4


def body(count, fitted_slab, pair_list):
    rows, width = fitted_slab.shape
    reach = pair_list.shape[1] - 1
    slots = 2 * reach + 1
    me = lax.axis_index("blk")
    k = me % PLANE
    upper = k >= 2
    outer = (k == 0) | (k == 3)
    devices = range(count)

    def xor(block, t):
        return lax.ppermute(block, "blk", [(i, i ^ t) for i in devices])

    def some(block, t, sources):
        return lax.ppermute(block, "blk", [(i, i ^ t) for i in devices if i % PLANE in sources])

    def shift(block, step):
        return lax.ppermute(block, "blk", [(i, i + step) for i in devices if 0 <= i + step < count])

    up = functools.partial(shift, step=PLANE)
    down = functools.partial(shift, step=-PLANE)

    quarters = fitted_slab.T.reshape(PLANE, width // PLANE, rows)

    def quarter(index):
        return lax.dynamic_index_in_dim(quarters, index, 0, keepdims=False)

    own = quarter(k)
    cx = xor(quarter(k ^ 1), 1)
    q2, q3 = quarter(k ^ 2), quarter(k ^ 3)
    far_outer = some(q3, 3, (0, 3)) + some(q2, 2, (0, 3))
    far_inner = some(q3, 3, (1, 2)) + some(q2, 2, (1, 2))
    near_inner = jnp.where(outer, cx, own)
    near_outer = jnp.where(outer, own, cx)
    b0 = jnp.where(upper, far_outer, near_outer)
    b3 = jnp.where(upper, near_outer, far_outer)
    b1 = jnp.where(upper, far_inner, near_inner)
    b2 = jnp.where(upper, near_inner, far_inner)
    x2 = jnp.where(outer, far_inner, far_outer)
    x3 = jnp.where(outer, far_outer, far_inner)

    low_near, high_near = up(near_inner), down(near_inner)
    low3, high0 = up(b3), down(b0)
    low_far, high_far = up(far_inner), down(far_inner)
    low0, high3 = up(b0), down(b3)

    def dot(a, b):
        return lax.dot_general(a, b, (((0,), (0,)), ((), ())), precision=lax.Precision.HIGH)

    mine = jnp.concatenate([own, x2, cx, x3], 1)

    def core_sum(part):
        return part[: 2 * rows] + xor(part[2 * rows :], 1)

    first = core_sum(dot(mine, jnp.concatenate([b0, b1, b2, b3, low3, high0, low_near, high_near], 1)))
    first_in = xor(first[rows:], 2)
    done = first[:rows, : 6 * rows] + first_in[:, : 6 * rows]

    low1 = jnp.where(upper, low_far, low_near)
    low2 = jnp.where(upper, low_near, low_far)
    high1 = jnp.where(upper, high_far, high_near)
    high2 = jnp.where(upper, high_near, high_far)
    lows, highs = [low1, low2, low3], [high0, high1, high2]
    cross = dot(jnp.concatenate(lows, 1), jnp.concatenate(highs, 1))

    def at(i, j):
        return cross[(i - 1) * rows : i * rows, j * rows : (j + 1) * rows]

    packs = jnp.stack(
        [
            jnp.concatenate([at(i, m) if m < i else at(m + 1, i).T for m in range(PLANE - 1)], 1)
            for i in range(PLANE)
        ]
    )
    packs = jnp.concatenate([lax.dynamic_index_in_dim(packs, k ^ t, 0, keepdims=False) for t in (0, 2, 1, 3)], 0)
    second = core_sum(jnp.concatenate([packs, dot(mine, jnp.concatenate([low_far, high_far], 1))], 1))
    second_in = xor(second[rows:], 2)
    pack = second[:rows, : 3 * rows] + second_in[:, : 3 * rows]
    from_high, from_low = down(pack), up(pack)

    third = core_sum(dot(mine, jnp.concatenate([low0, high3], 1)))
    third = third[:rows] + xor(third[rows:], 2)

    def col(array, i):
        return array[:, i * rows : (i + 1) * rows]

    low_n = col(first[:rows], 6) + col(second_in, 3)
    high_n = col(first[:rows], 7) + col(second_in, 4)
    low_f = col(first_in, 6) + col(second[:rows], 3)
    high_f = col(first_in, 7) + col(second[:rows], 4)
    wide = [
        col(from_low, 0),
        col(from_low, 0),
        col(from_low, 1),
        col(from_low, 2),
        col(third, 0),
        jnp.where(upper, low_f, low_n),
        jnp.where(upper, low_n, low_f),
        col(done, 4),
        col(done, 0),
        col(done, 1),
        col(done, 2),
        col(done, 3),
        col(done, 5),
        jnp.where(upper, high_f, high_n),
        jnp.where(upper, high_n, high_f),
        col(third, 1),
        col(from_high, 0),
        col(from_high, 1),
        col(from_high, 2),
    ]
    band = lax.dynamic_slice_in_dim(jnp.concatenate(wide, 1), (k + 1) * rows, slots * rows, 1)

    offsets = jnp.arange(reach + 1, dtype=jnp.int32)
    present = jnp.any(pair_list[:, :, None] == offsets, axis=1)
    padded = jnp.pad(present, ((reach, 0), (0, 0)))
    window = lax.dynamic_slice_in_dim(padded, me, reach + 1, 0)
    lower = [window[reach - d, d] for d in range(reach, 0, -1)]
    mask = jnp.concatenate([jnp.stack(lower), window[reach]])
    return jnp.where(jnp.repeat(mask, rows)[None, :], band, 0.0)


def solution(mesh):
    return jax.shard_map(
        functools.partial(body, mesh.shape["blk"]),
        mesh=mesh,
        in_specs=(P("blk", "groups"), P()),
        out_specs=P(("groups", "blk"), None),
        check_vma=False,
    )
```

time: 791 us -> 201 us (0.25)
  starting transfers between devices: 410 us -> 41.7 us
  waiting for transfers between devices: 296 us -> 94.9 us
  matrix products: 50.2 us -> 18.4 us
  other arithmetic: 0.71 us -> 17.8 us
    ppermute x14 -> x21, starting transfers between devices: 410 us -> 41.7 us  [the longest x10 24.6 us: shift(): lax.ppermute(block, 'blk', [(i, i + step) for i in devices if 0 <= i + st...]
    ppermute x14 -> x21, waiting for transfers between devices: 296 us -> 94.9 us  [the longest x10 46 us: shift(): lax.ppermute(block, 'blk', [(i, i + step) for i in devices if 0 <= i + st...]
    dot_general x1 -> x4, matrix products: 50.2 us -> 18.4 us  [dot(): lax.dot_general(a, b, (((0,), (0,)), ((), ())), precision=lax.Precision.H...]
    unnamed x23 -> x40, local copies, waits for them, and re-layouts: 27.7 us -> 14 us
  transfers between devices with their start and end apart: 14 -> 21, of which waited for: 3 -> 12; matrix products, arithmetic and copies ran while one was open for 4% -> 24% of each run, Pallas kernels for 0% -> 0%
where the time goes in v1:
time: 201 us; the launch traced here: 200 us
  waiting for transfers between devices  94.9 us (47%)
  starting transfers between devices  41.7 us (21%)
  local copies, waits for them, and re-layouts  27.1 us (13%)
  matrix products  18.4 us (9%)
  other arithmetic  17.8 us (9%)
    ppermute x10, waiting for transfers between devices, shift(): lax.ppermute(block, 'blk', [(i, i + step) for i in devices if 0 <= i + st...  46 us
    ppermute x4, waiting for transfers between devices, some(): lax.ppermute(block, 'blk', [(i, i ^ t) for i in devices if i % PLANE in s...  29 us
    ppermute x10, starting transfers between devices, shift(): lax.ppermute(block, 'blk', [(i, i + step) for i in devices if 0 <= i + st...  24.6 us
    ppermute x7, waiting for transfers between devices, xor(): return lax.ppermute(block, 'blk', [(i, i ^ t) for i in devices])  19.9 us
    dot_general x4, matrix products, dot(): lax.dot_general(a, b, (((0,), (0,)), ((), ())), precision=lax.Precision.H...  18.4 us
    unnamed x40, local copies, waits for them, and re-layouts  14 us
    ppermute x4, starting transfers between devices, some(): lax.ppermute(block, 'blk', [(i, i ^ t) for i in devices if i % PLANE in s...  10.2 us
    ppermute x7, starting transfers between devices, xor(): return lax.ppermute(block, 'blk', [(i, i ^ t) for i in devices])  7.02 us
  transfers between devices with their start and end apart: 21, of which 12 were waited for; matrix products, arithmetic and copies ran while one was open for 24% of the time, Pallas kernels for 0%

profile of v1, /device:TPU:0, one launch (start us, length us, event | category | flops | bytes accessed | tf_op | source)
XLA Modules:
  0.0 200.4 jit_solution(1565709771390872995)
XLA Ops:
  0.0 2.8 %dynamic-slice_bitcast_fusion.2 = (f32[1800,128]{1,0:T(8,128)}, f32[1800,128]{1,0:T(8,128)S(1)}, f32[1800,128]{1,0:T(8,128)S(1)}) fusion(f32[4,1800,128]{2,1,0:T(8,128)} %bitcast.47, s32[]{:T(128)S(6)} %select_n.113, s32[]{:T(128)S(6)} %select_n.115, s32[]{:T(128)S(6)} %select_n.112), kind=kLoop, calls=%fused_computation.27 | loop fusion | bytes 5529612 | tf_op jit(solution)/shard_map/jit(dynamic_index_in_dim)/squeeze | solution.py:36
  3.3 5.3 %collective-permute-start.6 = (f32[1800,128]{1,0:T(8,128)}, f32[1800,128]{1,0:T(8,128)}, u32[]{:S(2)}, u32[]{:S(2)}) collective-permute-start(f32[1800,128]{1,0:T(8,128)} %get-tuple-element.14), channel_id=1, source_target_pairs={{0,2},{3,1},{4,6},{7,5},{8,10},{11,9},{12,14},{15,13},{16,18},{19,... | collective-permute-start | bytes 2764808 | tf_op jit(solution)/shard_map/ppermute | solution.py:25
  8.6 1.9 collective-permute-start.5
  13.5 9.4 %collective-permute-done.6 = f32[1800,128]{1,0:T(8,128)} collective-permute-done((f32[1800,128]{1,0:T(8,128)}, f32[1800,128]{1,0:T(8,128)}, u32[]{:S(2)}, u32[]{:S(2)}) %collective-permute-start.6) | collective-permute-done | bytes 921632 | tf_op jit(solution)/shard_map/ppermute | solution.py:25
  22.9 19.6 %collective-permute-done.5 = f32[1800,128]{1,0:T(8,128)} collective-permute-done((f32[1800,128]{1,0:T(8,128)S(1)}, f32[1800,128]{1,0:T(8,128)}, u32[]{:S(2)}, u32[]{:S(2)}) %collective-permute-start.5) | collective-permute-done | bytes 921632 | tf_op jit(solution)/shard_map/ppermute | solution.py:25
  42.5 2.9 %constant_dynamic-update-slice_fusion.5 = (f32[1800,1024]{1,0:T(8,128)S(1)}, f32[1800,128]{1,0:T(8,128)}, f32[1800,128]{1,0:T(8,128)S(1)}, f32[1800,128]{1,0:T(8,128)S(1)}) fusion(f32[1800,128]{1,0:T(8,128)S(1)} %collective-permute-done.3, pred[]{:T(512)S(6)} %or.5, pred[]{:T(512)S(6)} %ge.3, f32[4,1800,128]{2,1,0:T(8,128)} %bitcast.48, s32[]{:T(128)S(6)} %select_n.116, ...), kind=kLoop, calls=%fused_computation.73 | loop fusion | flops 691199 | bytes 7372806
  50.0 2.9 %copy-done.10 = f32[1800,1024]{1,0:T(8,128)} copy-done((f32[1800,1024]{1,0:T(8,128)}, f32[1800,1024]{1,0:T(8,128)S(1)}, u32[]{:S(2)}) %copy-start.10) | copy-done | bytes 7372824
  52.9 4.5 %collective-permute-start.7 = (f32[1800,128]{1,0:T(8,128)}, f32[1800,128]{1,0:T(8,128)}, u32[]{:S(2)}, u32[]{:S(2)}) collective-permute-start(f32[1800,128]{1,0:T(8,128)} %get-tuple-element.6), channel_id=1, source_target_pairs={{0,4},{1,5},{2,6},{3,7},{4,8},{5,9},{6,10},{7,11},{8,12},{9,13},{1... | collective-permute-start | bytes 2764808 | tf_op jit(solution)/shard_map/ppermute | solution.py:28
  58.6 5.5 %collective-permute-start.4 = (f32[1800,128]{1,0:T(8,128)}, f32[1800,128]{1,0:T(8,128)}, u32[]{:S(2)}, u32[]{:S(2)}) collective-permute-start(f32[1800,128]{1,0:T(8,128)} %copy-done), channel_id=1, source_target_pairs={{0,4},{1,5},{2,6},{3,7},{4,8},{5,9},{6,10},{7,11},{8,12},{9,13},{1... | collective-permute-start | bytes 2764808 | tf_op jit(solution)/shard_map/ppermute | solution.py:28
  64.1 2.6 %collective-permute-start.2 = (f32[1800,128]{1,0:T(8,128)S(1)}, f32[1800,128]{1,0:T(8,128)}, u32[]{:S(2)}, u32[]{:S(2)}) collective-permute-start(f32[1800,128]{1,0:T(8,128)S(1)} %get-tuple-element.9), channel_id=1, source_target_pairs={{0,4},{1,5},{2,6},{3,7},{4,8},{5,9},{6,10},{7,11},{8,12},{9,13},{1... | collective-permute-start | bytes 2764808 | tf_op jit(solution)/shard_map/ppermute | solution.py:28
  67.6 4.2 %concatenate.43 = pred[15]{0:T(512)(128)(4,1)S(1)} concatenate(pred[1]{0:T(512)(128)(4,1)} %bitcast, pred[1]{0:T(512)(128)(4,1)} %bitcast.1, pred[1]{0:T(512)(128)(4,1)} %bitcast.2, pred[1]{0:T(512)(128)(4,1)} %bitcast.3, pred[1]{0:T(512)(128)(4,1)} %bitcast.4, pred[1]{0:T(512)(128)(4,1)} %bitcast.5, pred[1]{0:T(512)(128)(4,1)} %bitcast.6, pred[8]{0:T(512)(128)(4,1)S(1)} %slice_reduce_fusion), dimensions={0} | concatenate | bytes 30 | tf_op jit(solution)/shard_map/concatenate | solution.py:129
  73.1 1.8 collective-permute-done.7
  76.2 2.2 %constant_dynamic-update-slice_fusion.3 = f32[1800,1024]{1,0:T(8,128)} fusion(f32[1800,1024]{1,0:T(8,128)} %copy-done.10, f32[1800,128]{1,0:T(8,128)} %collective-permute-done.7), kind=kLoop, calls=%fused_computation.71 | loop fusion | bytes 1843200
  78.5 2.1 %collective-permute-done.8 = f32[1800,128]{1,0:T(8,128)} collective-permute-done((f32[1800,128]{1,0:T(8,128)}, f32[1800,128]{1,0:T(8,128)}, u32[]{:S(2)}, u32[]{:S(2)}) %collective-permute-start.8) | collective-permute-done | bytes 921632 | tf_op jit(solution)/shard_map/ppermute | solution.py:28
  80.6 3.0 %collective-permute-start.14 = (f32[1800,128]{1,0:T(8,128)}, f32[1800,128]{1,0:T(8,128)S(1)}, u32[]{:S(2)}, u32[]{:S(2)}) collective-permute-start(f32[1800,128]{1,0:T(8,128)} %get-tuple-element.11), channel_id=1, source_target_pairs={{0,4},{1,5},{2,6},{3,7},{4,8},{5,9},{6,10},{7,11},{8,12},{9,13},{1... | collective-permute-start | bytes 2764808 | tf_op jit(solution)/shard_map/ppermute | solution.py:28
  83.5 2.2 %constant_dynamic-update-slice_fusion.2 = f32[1800,1024]{1,0:T(8,128)} fusion(f32[1800,1024]{1,0:T(8,128)} %constant_dynamic-update-slice_fusion.3, f32[1800,128]{1,0:T(8,128)} %collective-permute-done.8), kind=kLoop, calls=%fused_computation.70 | loop fusion | bytes 1843200
  85.8 8.9 %collective-permute-done.4 = f32[1800,128]{1,0:T(8,128)} collective-permute-done((f32[1800,128]{1,0:T(8,128)}, f32[1800,128]{1,0:T(8,128)}, u32[]{:S(2)}, u32[]{:S(2)}) %collective-permute-start.4) | collective-permute-done | bytes 921632 | tf_op jit(solution)/shard_map/ppermute | solution.py:28
  96.2 18.2 %collective-permute-done.2 = f32[1800,128]{1,0:T(8,128)} collective-permute-done((f32[1800,128]{1,0:T(8,128)S(1)}, f32[1800,128]{1,0:T(8,128)}, u32[]{:S(2)}, u32[]{:S(2)}) %collective-permute-start.2) | collective-permute-done | bytes 921632 | tf_op jit(solution)/shard_map/ppermute | solution.py:28
  114.3 2.6 %broadcast_select_fusion.9 = (f32[1800,128]{1,0:T(8,128)S(1)}, f32[1800,128]{1,0:T(8,128)S(1)}, f32[1800,1024]{1,0:T(8,128)}) fusion(f32[1800,128]{1,0:T(8,128)} %collective-permute-done.2, f32[1800,128]{1,0:T(8,128)} %collective-permute-done.4, pred[]{:T(512)S(6)} %ge.3, f32[1800,1024]{1,0:T(8,128)} %constant_dynamic-update-slice_fusion.2), kind=kLoop, calls=%fused_computation.41 | loop fusion | flops 460800 | bytes 4608001 | tf_op jit(solution)/shard_map/jit(_where)/select_n | solution.py:69
  117.0 3.0 %collective-permute-done.9 = f32[1800,128]{1,0:T(8,128)S(1)} collective-permute-done((f32[1800,128]{1,0:T(8,128)S(1)}, f32[1800,128]{1,0:T(8,128)S(1)}, u32[]{:S(2)}, u32[]{:S(2)}) %collective-permute-start.9) | collective-permute-done | bytes 921632 | tf_op jit(solution)/shard_map/ppermute | solution.py:28
  122.1 4.3 %fusion = f32[384,384]{1,0:T(8,128)S(1)} fusion(f32[1800,128]{1,0:T(8,128)} %collective-permute-done.7, f32[1800,128]{1,0:T(8,128)S(1)} %get-tuple-element.20, f32[1800,128]{1,0:T(8,128)S(1)} %get-tuple-element.19, f32[1800,128]{1,0:T(8,128)S(1)} %get-tuple-element.18, f32[1800,128]{1,0:T(8,128)S(1)} %get-tuple-element.17, ...), kind=kOutput, calls=%fused_computation.1 | convolution fusion | flops 1595289600 | bytes 6119424 | tf_op jit(solution)/shard_map/dot_general | solution.py:58
  127.8 6.4 %collective-permute-done.14 = f32[1800,128]{1,0:T(8,128)S(1)} collective-permute-done((f32[1800,128]{1,0:T(8,128)}, f32[1800,128]{1,0:T(8,128)S(1)}, u32[]{:S(2)}, u32[]{:S(2)}) %collective-permute-start.14) | collective-permute-done | bytes 921632 | tf_op jit(solution)/shard_map/ppermute | solution.py:28
  134.2 5.5 %collective-permute-done.15 = f32[1800,128]{1,0:T(8,128)S(1)} collective-permute-done((f32[1800,128]{1,0:T(8,128)}, f32[1800,128]{1,0:T(8,128)S(1)}, u32[]{:S(2)}, u32[]{:S(2)}) %collective-permute-start.15) | collective-permute-done | bytes 921632 | tf_op jit(solution)/shard_map/ppermute | solution.py:28
  139.7 1.9 fusion.15
  142.5 2.1 %collective-permute-start.16 = (f32[256,256]{0,1:T(8,128)}, f32[256,256]{0,1:T(8,128)}, u32[]{:S(2)}, u32[]{:S(2)}) collective-permute-start(f32[256,256]{0,1:T(8,128)} %slice.217), channel_id=1, source_target_pairs={{0,1},{1,0},{2,3},{3,2},{4,5},{5,4},{6,7},{7,6},{8,9},{9,8},{10,11... | collective-permute-start | bytes 786440 | tf_op jit(solution)/shard_map/ppermute | solution.py:22
  153.2 4.7 %fusion.11 = f32[512,256]{1,0:T(8,128)S(1)} fusion(f32[1800,128]{1,0:T(8,128)S(1)} %copy-done.3, f32[1800,128]{1,0:T(8,128)} %collective-permute-done.2, f32[1800,128]{1,0:T(8,128)S(1)} %copy-done.5, f32[1800,128]{1,0:T(8,128)S(1)} %collective-permute-done.3, f32[1800,128]{1,0:T(8,128)S(1)} %copy-done.7, f32[1800,128]{1,0:T(8,128)S(1)} %get-tuple-element.12), kind=kOutput, calls=%fused_computation.12 | convolution fusion | flops 1418803200 | bytes 6053888 | tf_op jit(solution)/shard_map/dot_general | solution.py:58
  158.2 7.5 %fusion.19 = f32[512,1024]{1,0:T(8,128)S(1)} fusion(f32[1800,1024]{1,0:T(8,128)S(1)} %bitcast.53, f32[1800,128]{1,0:T(8,128)S(1)} %copy-done.5, f32[1800,128]{1,0:T(8,128)S(1)} %collective-permute-done.3, f32[1800,128]{1,0:T(8,128)S(1)} %copy-done.7, f32[1800,128]{1,0:T(8,128)S(1)} %get-tuple-element.12), kind=kOutput, calls=%fused_computation.31 | convolution fusion | flops 5665075200 | bytes 13156352 | tf_op jit(solution)/shard_map/dot_general | solution.py:58
  168.1 1.8 collective-permute-start.17
  171.0 3.6 %collective-permute-done.17 = f32[128,256]{0,1:T(8,128)S(1)} collective-permute-done((f32[128,256]{0,1:T(8,128)}, f32[128,256]{0,1:T(8,128)S(1)}, u32[]{:S(2)}, u32[]{:S(2)}) %collective-permute-start.17) | collective-permute-done | bytes 131104 | tf_op jit(solution)/shard_map/ppermute | solution.py:22
  174.6 6.5 %collective-permute-done.12 = f32[128,640]{1,0:T(8,128)S(1)} collective-permute-done((f32[128,640]{1,0:T(8,128)}, f32[128,640]{1,0:T(8,128)S(1)}, u32[]{:S(2)}, u32[]{:S(2)}) %collective-permute-start.12) | collective-permute-done | bytes 327712 | tf_op jit(solution)/shard_map/ppermute | solution.py:22
  181.8 2.5 %collective-permute-start.13 = (f32[128,384]{1,0:T(8,128)}, f32[128,384]{1,0:T(8,128)S(1)}, u32[]{:S(2)}, u32[]{:S(2)}) collective-permute-start(f32[128,384]{1,0:T(8,128)} %slice_add_fusion.4), channel_id=1, source_target_pairs={{0,4},{1,5},{2,6},{3,7},{4,8},{5,9},{6,10},{7,11},{8,12},{9,13},{1... | collective-permute-start | bytes 589832 | tf_op jit(solution)/shard_map/ppermute | solution.py:28
  189.2 9.8 %collective-permute-done.19 = f32[128,1024]{1,0:T(8,128)S(1)} collective-permute-done((f32[128,1024]{1,0:T(8,128)S(1)}, f32[128,1024]{1,0:T(8,128)S(1)}, u32[]{:S(2)}, u32[]{:S(2)}) %collective-permute-start.19) | collective-permute-done | bytes 524320 | tf_op jit(solution)/shard_map/ppermute | solution.py:22
  (98 shorter events, 37.5 us)
Async XLA Ops:
  2.8 10.6 %collective-permute-start.3 = (f32[1800,128]{1,0:T(8,128)S(1)}, f32[1800,128]{1,0:T(8,128)S(1)}, u32[]{:S(2)}, u32[]{:S(2)}) collective-permute-start(f32[1800,128]{1,0:T(8,128)S(1)} %get-tuple-element.15), channel_id=1, source_target_pairs={{0,1},{1,0},{2,3},{3,2},{4,5},{5,4},{6,7},{7,6},{8,9},{9,8},{10,11... | collective-permute-start | bytes 2764808 | tf_op jit(solution)/shard_map/ppermute | solution.py:22
  3.3 19.6 %collective-permute-start.6 = (f32[1800,128]{1,0:T(8,128)}, f32[1800,128]{1,0:T(8,128)}, u32[]{:S(2)}, u32[]{:S(2)}) collective-permute-start(f32[1800,128]{1,0:T(8,128)} %get-tuple-element.14), channel_id=1, source_target_pairs={{0,2},{3,1},{4,6},{7,5},{8,10},{11,9},{12,14},{15,13},{16,18},{19,... | collective-permute-start | bytes 2764808 | tf_op jit(solution)/shard_map/ppermute | solution.py:25
  8.6 33.9 %collective-permute-start.5 = (f32[1800,128]{1,0:T(8,128)S(1)}, f32[1800,128]{1,0:T(8,128)}, u32[]{:S(2)}, u32[]{:S(2)}) collective-permute-start(f32[1800,128]{1,0:T(8,128)S(1)} %get-tuple-element.16), channel_id=1, source_target_pairs={{0,3},{3,0},{4,7},{7,4},{8,11},{11,8},{12,15},{15,12},{16,19},{19,... | collective-permute-start | bytes 2764808 | tf_op jit(solution)/shard_map/ppermute | solution.py:25
  10.5 34.9 %collective-permute-start.1 = (f32[1800,128]{1,0:T(8,128)}, f32[1800,128]{1,0:T(8,128)}, u32[]{:S(2)}, u32[]{:S(2)}) collective-permute-start(f32[1800,128]{1,0:T(8,128)} %get-tuple-element.14), channel_id=1, source_target_pairs={{1,3},{2,0},{5,7},{6,4},{9,11},{10,8},{13,15},{14,12},{17,19},{18,... | collective-permute-start | bytes 2764808 | tf_op jit(solution)/shard_map/ppermute | solution.py:25
  11.8 33.6 %collective-permute-start = (f32[1800,128]{1,0:T(8,128)S(1)}, f32[1800,128]{1,0:T(8,128)}, u32[]{:S(2)}, u32[]{:S(2)}) collective-permute-start(f32[1800,128]{1,0:T(8,128)S(1)} %get-tuple-element.16), channel_id=1, source_target_pairs={{1,2},{2,1},{5,6},{6,5},{9,10},{10,9},{13,14},{14,13},{17,18},{18,... | collective-permute-start | bytes 2764808 | tf_op jit(solution)/shard_map/ppermute | solution.py:25
  48.2 18.5 %copy-start.11 = (s32[16,8]{0,1:T(8,128)S(1)}, s32[16,8]{0,1:T(8,128)}, u32[]{:S(2)}) copy-start(s32[16,8]{0,1:T(8,128)} %param.3) | copy-start | bytes 1540
  50.0 2.9 %copy-start.10 = (f32[1800,1024]{1,0:T(8,128)}, f32[1800,1024]{1,0:T(8,128)S(1)}, u32[]{:S(2)}) copy-start(f32[1800,1024]{1,0:T(8,128)S(1)} %get-tuple-element.5) | copy-start | bytes 22118404
  52.9 22.1 %collective-permute-start.7 = (f32[1800,128]{1,0:T(8,128)}, f32[1800,128]{1,0:T(8,128)}, u32[]{:S(2)}, u32[]{:S(2)}) collective-permute-start(f32[1800,128]{1,0:T(8,128)} %get-tuple-element.6), channel_id=1, source_target_pairs={{0,4},{1,5},{2,6},{3,7},{4,8},{5,9},{6,10},{7,11},{8,12},{9,13},{1... | collective-permute-start | bytes 2764808 | tf_op jit(solution)/shard_map/ppermute | solution.py:28
  57.3 23.2 %collective-permute-start.8 = (f32[1800,128]{1,0:T(8,128)}, f32[1800,128]{1,0:T(8,128)}, u32[]{:S(2)}, u32[]{:S(2)}) collective-permute-start(f32[1800,128]{1,0:T(8,128)} %get-tuple-element.11), channel_id=1, source_target_pairs={{4,0},{5,1},{6,2},{7,3},{8,4},{9,5},{10,6},{11,7},{12,8},{13,9},{1... | collective-permute-start | bytes 2764808 | tf_op jit(solution)/shard_map/ppermute | solution.py:28
  58.6 36.0 %collective-permute-start.4 = (f32[1800,128]{1,0:T(8,128)}, f32[1800,128]{1,0:T(8,128)}, u32[]{:S(2)}, u32[]{:S(2)}) collective-permute-start(f32[1800,128]{1,0:T(8,128)} %copy-done), channel_id=1, source_target_pairs={{0,4},{1,5},{2,6},{3,7},{4,8},{5,9},{6,10},{7,11},{8,12},{9,13},{1... | collective-permute-start | bytes 2764808 | tf_op jit(solution)/shard_map/ppermute | solution.py:28
  64.1 50.2 %collective-permute-start.2 = (f32[1800,128]{1,0:T(8,128)S(1)}, f32[1800,128]{1,0:T(8,128)}, u32[]{:S(2)}, u32[]{:S(2)}) collective-permute-start(f32[1800,128]{1,0:T(8,128)S(1)} %get-tuple-element.9), channel_id=1, source_target_pairs={{0,4},{1,5},{2,6},{3,7},{4,8},{5,9},{6,10},{7,11},{8,12},{9,13},{1... | collective-permute-start | bytes 2764808 | tf_op jit(solution)/shard_map/ppermute | solution.py:28
  71.8 45.1 %collective-permute-start.10 = (f32[1800,128]{1,0:T(8,128)}, f32[1800,128]{1,0:T(8,128)S(1)}, u32[]{:S(2)}, u32[]{:S(2)}) collective-permute-start(f32[1800,128]{1,0:T(8,128)} %copy-done), channel_id=1, source_target_pairs={{4,0},{5,1},{6,2},{7,3},{8,4},{9,5},{10,6},{11,7},{12,8},{13,9},{1... | collective-permute-start | bytes 2764808 | tf_op jit(solution)/shard_map/ppermute | solution.py:28
  74.9 45.0 %collective-permute-start.9 = (f32[1800,128]{1,0:T(8,128)S(1)}, f32[1800,128]{1,0:T(8,128)S(1)}, u32[]{:S(2)}, u32[]{:S(2)}) collective-permute-start(f32[1800,128]{1,0:T(8,128)S(1)} %get-tuple-element.9), channel_id=1, source_target_pairs={{4,0},{5,1},{6,2},{7,3},{8,4},{9,5},{10,6},{11,7},{12,8},{13,9},{1... | collective-permute-start | bytes 2764808 | tf_op jit(solution)/shard_map/ppermute | solution.py:28
  80.6 53.6 %collective-permute-start.14 = (f32[1800,128]{1,0:T(8,128)}, f32[1800,128]{1,0:T(8,128)S(1)}, u32[]{:S(2)}, u32[]{:S(2)}) collective-permute-start(f32[1800,128]{1,0:T(8,128)} %get-tuple-element.11), channel_id=1, source_target_pairs={{0,4},{1,5},{2,6},{3,7},{4,8},{5,9},{6,10},{7,11},{8,12},{9,13},{1... | collective-permute-start | bytes 2764808 | tf_op jit(solution)/shard_map/ppermute | solution.py:28
  94.7 45.0 %collective-permute-start.15 = (f32[1800,128]{1,0:T(8,128)}, f32[1800,128]{1,0:T(8,128)S(1)}, u32[]{:S(2)}, u32[]{:S(2)}) collective-permute-start(f32[1800,128]{1,0:T(8,128)} %get-tuple-element.6), channel_id=1, source_target_pairs={{4,0},{5,1},{6,2},{7,3},{8,4},{9,5},{10,6},{11,7},{12,8},{13,9},{1... | collective-permute-start | bytes 2764808 | tf_op jit(solution)/shard_map/ppermute | solution.py:28
  122.1 17.6 %copy-start.4 = (f32[1800,128]{1,0:T(8,128)S(1)}, f32[1800,128]{1,0:T(8,128)}, u32[]{:S(2)}) copy-start(f32[1800,128]{1,0:T(8,128)} %get-tuple-element.25) | copy-start | bytes 2764804
  122.1 17.6 %copy-start.6 = (f32[1800,128]{1,0:T(8,128)S(1)}, f32[1800,128]{1,0:T(8,128)}, u32[]{:S(2)}) copy-start(f32[1800,128]{1,0:T(8,128)} %get-tuple-element.26) | copy-start | bytes 2764804
  141.7 2.9 %copy-start.8 = (f32[512,256]{0,1:T(8,128)}, f32[512,256]{0,1:T(8,128)S(1)}, u32[]{:S(2)}) copy-start(f32[512,256]{0,1:T(8,128)S(1)} %fusion.15) | copy-start | bytes 1572868
  142.5 10.7 %copy-start.3 = (f32[1800,128]{1,0:T(8,128)S(1)}, f32[1800,128]{1,0:T(8,128)}, u32[]{:S(2)}) copy-start(f32[1800,128]{1,0:T(8,128)} %copy-done.2) | copy-start | bytes 2764804
  142.5 23.8 %collective-permute-start.16 = (f32[256,256]{0,1:T(8,128)}, f32[256,256]{0,1:T(8,128)}, u32[]{:S(2)}, u32[]{:S(2)}) collective-permute-start(f32[256,256]{0,1:T(8,128)} %slice.217), channel_id=1, source_target_pairs={{0,1},{1,0},{2,3},{3,2},{4,5},{5,4},{6,7},{7,6},{8,9},{9,8},{10,11... | collective-permute-start | bytes 786440 | tf_op jit(solution)/shard_map/ppermute | solution.py:22
  151.0 2.2 %copy-start.7 = (f32[1800,128]{1,0:T(8,128)S(1)}, f32[1800,128]{1,0:T(8,128)}, u32[]{:S(2)}) copy-start(f32[1800,128]{1,0:T(8,128)} %get-tuple-element.26) | copy-start | bytes 2764804
  153.1 5.1 %slice-start = ((s8[7372800]{0:T(1024)(128)(4,1)}), s8[4194304]{0:T(1024)(128)(4,1)S(1)}, s32[]{:S(2)}) async-start(s8[7372800]{0:T(1024)(128)(4,1)} %bitcast.52), calls=%async_computation | async-start | bytes 8388608
  153.2 5.0 %slice-start.1 = ((s8[7372800]{0:T(1024)(128)(4,1)}), s8[3178496]{0:T(1024)(128)(4,1)S(1)}, s32[]{:S(2)}) async-start(s8[7372800]{0:T(1024)(128)(4,1)} %bitcast.52), calls=%async_computation.1 | async-start | bytes 6356992
  158.0 11.9 %collective-permute-start.11 = (f32[256,640]{1,0:T(8,128)S(1)}, f32[256,640]{1,0:T(8,128)S(1)}, u32[]{:S(2)}, u32[]{:S(2)}) collective-permute-start(f32[256,640]{1,0:T(8,128)S(1)} %slice.211), channel_id=1, source_target_pairs={{0,1},{1,0},{2,3},{3,2},{4,5},{5,4},{6,7},{7,6},{8,9},{9,8},{10,11... | collective-permute-start | bytes 1966088 | tf_op jit(solution)/shard_map/ppermute | solution.py:22
  158.2 8.1 %copy-start.9 = (f32[512,256]{0,1:T(8,128)S(1)}, f32[512,256]{0,1:T(8,128)}, u32[]{:S(2)}) copy-start(f32[512,256]{0,1:T(8,128)} %copy-done.8) | copy-start | bytes 1572868
  165.7 5.0 %copy-start.1 = (f32[512,1024]{1,0:T(8,128)}, f32[512,1024]{1,0:T(8,128)S(1)}, u32[]{:S(2)}) copy-start(f32[512,1024]{1,0:T(8,128)S(1)} %fusion.19) | copy-start | bytes 6291460
  165.8 18.5 %collective-permute-start.18 = (f32[256,1024]{1,0:T(8,128)S(1)}, f32[256,1024]{1,0:T(8,128)S(1)}, u32[]{:S(2)}, u32[]{:S(2)}) collective-permute-start(f32[256,1024]{1,0:T(8,128)S(1)} %slice.222), channel_id=1, source_target_pairs={{0,1},{1,0},{2,3},{3,2},{4,5},{5,4},{6,7},{7,6},{8,9},{9,8},{10,11... | collective-permute-start | bytes 3145736 | tf_op jit(solution)/shard_map/ppermute | solution.py:22
  168.1 6.5 %collective-permute-start.17 = (f32[128,256]{0,1:T(8,128)}, f32[128,256]{0,1:T(8,128)S(1)}, u32[]{:S(2)}, u32[]{:S(2)}) collective-permute-start(f32[128,256]{0,1:T(8,128)} %slice.219), channel_id=1, source_target_pairs={{0,2},{1,3},{2,0},{3,1},{4,6},{5,7},{6,4},{7,5},{8,10},{9,11},{10,... | collective-permute-start | bytes 393224 | tf_op jit(solution)/shard_map/ppermute | solution.py:22
  170.7 10.4 %collective-permute-start.12 = (f32[128,640]{1,0:T(8,128)}, f32[128,640]{1,0:T(8,128)S(1)}, u32[]{:S(2)}, u32[]{:S(2)}) collective-permute-start(f32[128,640]{1,0:T(8,128)} %slice.213), channel_id=1, source_target_pairs={{0,2},{1,3},{2,0},{3,1},{4,6},{5,7},{6,4},{7,5},{8,10},{9,11},{10,... | collective-permute-start | bytes 983048 | tf_op jit(solution)/shard_map/ppermute | solution.py:22
  181.8 7.3 %collective-permute-start.13 = (f32[128,384]{1,0:T(8,128)}, f32[128,384]{1,0:T(8,128)S(1)}, u32[]{:S(2)}, u32[]{:S(2)}) collective-permute-start(f32[128,384]{1,0:T(8,128)} %slice_add_fusion.4), channel_id=1, source_target_pairs={{0,4},{1,5},{2,6},{3,7},{4,8},{5,9},{6,10},{7,11},{8,12},{9,13},{1... | collective-permute-start | bytes 589832 | tf_op jit(solution)/shard_map/ppermute | solution.py:28
  185.8 13.2 %collective-permute-start.19 = (f32[128,1024]{1,0:T(8,128)S(1)}, f32[128,1024]{1,0:T(8,128)S(1)}, u32[]{:S(2)}, u32[]{:S(2)}) collective-permute-start(f32[128,1024]{1,0:T(8,128)S(1)} %slice.223), channel_id=1, source_target_pairs={{0,2},{1,3},{2,0},{3,1},{4,6},{5,7},{6,4},{7,5},{8,10},{9,11},{10,... | collective-permute-start | bytes 1572872 | tf_op jit(solution)/shard_map/ppermute | solution.py:22
  187.9 11.5 %collective-permute-start.20 = (f32[128,384]{1,0:T(8,128)}, f32[128,384]{1,0:T(8,128)S(1)}, u32[]{:S(2)}, u32[]{:S(2)}) collective-permute-start(f32[128,384]{1,0:T(8,128)} %slice_add_fusion.4), channel_id=1, source_target_pairs={{4,0},{5,1},{6,2},{7,3},{8,4},{9,5},{10,6},{11,7},{12,8},{13,9},{1... | collective-permute-start | bytes 589832 | tf_op jit(solution)/shard_map/ppermute | solution.py:28
  (3 other events, 4.0 us)

commit v2 on v0

v2 whole, which is shorter than its diff:
```python
import functools

import jax
import jax.numpy as jnp
from jax import lax
from jax.experimental import pallas as pl
from jax.experimental.pallas import tpu as pltpu
from jax.sharding import PartitionSpec as P

PLANE = 4
VMEM_BYTES = 44 * 2**20


def halves(value):
    high = value.astype(jnp.bfloat16)
    return high, (value - high.astype(jnp.float32)).astype(jnp.bfloat16)


def product(a, b):
    dot = functools.partial(
        lax.dot_general,
        dimension_numbers=(((0,), (0,)), ((), ())),
        preferred_element_type=jnp.float32,
    )
    (ah, al), (bh, bl) = halves(a), halves(b)
    return dot(ah, bh) + (dot(ah, bl) + dot(al, bh))


def side_by_side(*values):
    return jnp.concatenate(values, 1)


def block(index, size):
    if isinstance(index, int):
        return slice(index * size, (index + 1) * size)
    return pl.ds(pl.multiple_of(index * size, size), size)


def spread(value, keep, other, send):
    rows = keep.shape[0]
    keep[...] = value[:rows]
    other[...] = value[rows : 2 * rows]
    send[...] = value[2 * rows :]


def sides(odd, even_pair, odd_pair):
    first, second = even_pair[...], odd_pair[...]
    return jnp.where(odd, first, second), jnp.where(odd, second, first)


def first_kernel(at_ref, own, x2, cx, x3, e0, o0, keep, other, send):
    k, odd = at_ref[0], at_ref[1] == 1
    rows = own.shape[1]
    mine = side_by_side(own[...], x2[...], cx[...], x3[...])
    out = product(mine, side_by_side(mine, *sides(odd, e0, o0)))
    for ref, r in ((keep, 0), (other, rows), (send, 2 * rows)):
        size = ref.shape[0]
        for i, t in enumerate((0, 2, 1, 3)):
            ref[:, block(k ^ t, rows)] = out[r : r + size, block(i, rows)]
        ref[:, PLANE * rows :] = out[r : r + size, PLANE * rows :]


def cross_kernel(at_ref, e0, o0, e1, o1, e2, o2, keep, other, send, packs):
    k, odd = at_ref[0], at_ref[1] == 1
    rows = e0.shape[1]
    upper = k >= 2
    low, high = zip(sides(odd, e0, o0), sides(odd, e1, o1), sides(odd, e2, o2))
    swap = k == 1
    low_1 = jnp.where(upper, low[2], low[0])
    low_2 = jnp.where(upper, low[0], jnp.where(swap, low[1], low[2]))
    low_3 = jnp.where(swap, low[2], low[1])
    swap = k == 2
    high_0 = jnp.where(swap, high[2], high[1])
    high_1 = jnp.where(upper, jnp.where(swap, high[1], high[2]), high[0])
    high_2 = jnp.where(upper, high[0], high[2])
    cross = product(side_by_side(low_1, low_2, low_3), side_by_side(high_0, high_1, high_2))

    def at(i, j):
        return cross[block(i - 1, rows), block(j, rows)]

    for i in range(PLANE):
        t = i ^ k
        place = jnp.where(t == 1, 2, jnp.where(t == 2, 1, t))
        for m in range(PLANE - 1):
            value = at(i, m) if m < i else at(m + 1, i).T
            packs[block(place, rows), block(m, rows)] = value
    spread(packs[...], keep, other, send)


def second_kernel(at_ref, own, x2, cx, x3, e1, o1, e2, o2, keep, other, send):
    k, odd = at_ref[0], at_ref[1] == 1
    (low_1, high_1), (low_2, high_2) = sides(odd, e1, o1), sides(odd, e2, o2)
    columns = (
        jnp.where(k == 1, low_2, low_1),
        jnp.where(k == 1, low_1, low_2),
        jnp.where(k == 2, high_2, high_1),
        jnp.where(k == 2, high_1, high_2),
    )
    mine = side_by_side(own[...], x2[...], cx[...], x3[...])
    spread(product(mine, side_by_side(*columns)), keep, other, send)


def third_kernel(at_ref, own, x2, cx, x3, e3, o3, keep, other, send):
    odd = at_ref[1] == 1
    rows = own.shape[1]
    mine = side_by_side(own[...], x2[...], cx[...], x3[...])
    out = product(side_by_side(*sides(odd, e3, o3)), mine)
    keep[...] = out[:, :rows]
    other[...] = out[:, rows : 2 * rows]
    send[...] = out[:, 2 * rows :]


def final_kernel(reach, at_ref, pairs, k1, c1, y1, k2, c2, y2, k3, c3, y3, ez, oz, out):
    k, odd, me = at_ref[0], at_ref[1] == 1, at_ref[2]
    rows = out.shape[0]
    upper = k >= 2
    from_low, from_high = sides(odd, ez, oz)

    def near(keep, core, i):
        return keep[:, block(i, rows)] + core[:rows, block(i, rows)]

    def whole(keep, core, far, i):
        return near(keep, core, i) + far[:, block(i, rows)]

    def write(index, value):
        slot = index - k - 1
        offset = slot - reach
        row = me + jnp.minimum(offset, 0)
        wanted = jnp.abs(offset)
        found = pairs[jnp.maximum(row, 0), 0] == wanted
        for m in range(1, reach + 1):
            found = found | (pairs[jnp.maximum(row, 0), m] == wanted)
        factor = jnp.where(found & (row >= 0), 1.0, 0.0)

        @pl.when((slot >= 0) & (slot <= 2 * reach))
        def _():
            out[:, block(slot, rows)] = value * factor

    for m in range(PLANE - 1):
        write(m + 1, from_low[:, block(m, rows)])
        write(4 * PLANE + m, from_high[:, block(m, rows)])
    for i in range(PLANE):
        write(2 * PLANE + i, whole(k1, c1, y1, i))
    inner = jnp.where(upper, 1, 0)
    for plane, i, j in ((1, 4, 1), (3, 5, 3)):
        write(plane * PLANE + 1 + inner, near(k1, c1, i) + y2[:, block(j, rows)])
        write(plane * PLANE + 2 - inner, near(k2, c2, j) + y1[:, block(i, rows)])
    write(2 * PLANE - 1, whole(k2, c2, y2, 0))
    write(3 * PLANE, whole(k2, c2, y2, 2))
    third = k3[...] + c3[:, :rows] + y3[...]
    write(PLANE, third[:rows].T)
    write(4 * PLANE - 1, third[rows:].T)


def call(kernel, outs, scratch, scalars, arrays):
    return pl.pallas_call(
        kernel,
        cost_estimate=pl.CostEstimate(flops=1000, bytes_accessed=1000, transcendentals=0),
        in_specs=[pl.BlockSpec(memory_space=pltpu.SMEM)] * len(scalars)
        + [pl.BlockSpec(memory_space=pltpu.VMEM)] * len(arrays),
        out_specs=[pl.BlockSpec(memory_space=pltpu.VMEM)] * len(outs),
        out_shape=outs,
        scratch_shapes=scratch,
        compiler_params=pltpu.CompilerParams(vmem_limit_bytes=VMEM_BYTES),
    )(*scalars, *arrays)


def after(value, *others):
    return lax.optimization_barrier((value, *others))[0]


def body(count, fitted_slab, pair_list):
    rows, width = fitted_slab.shape
    depth = width // PLANE
    reach = pair_list.shape[1] - 1
    me = lax.axis_index("blk").astype(jnp.int32)
    k = me % PLANE
    odd = (me // PLANE) % 2
    place = jnp.stack([k, odd, me])
    upper = k >= 2
    outer = (k == 0) | (k == 3)
    flip = upper ^ (odd == 1)
    devices = range(count)

    def xor(value, t):
        return lax.ppermute(value, "blk", [(i, i ^ t) for i in devices])

    def along(value, parity):
        route = []
        for i in devices:
            j = i + (PLANE if i // PLANE % 2 == parity else -PLANE)
            if j in devices:
                route.append((i, j))
        return lax.ppermute(value, "blk", route)

    def both(to_even, to_odd):
        return along(to_even, 0), along(to_odd, 1)

    quarters = fitted_slab.T.reshape(PLANE, depth, rows)

    def quarter(index, *others):
        return lax.dynamic_index_in_dim(after(quarters, *others), index, 0, keepdims=False)

    q1 = quarter(k ^ 1)
    cx = xor(q1, 1)
    q3 = quarter(k ^ 3, q1)
    x3 = xor(q3, 3)
    own = quarter(k, q1)
    near_inner = jnp.where(outer, cx, own)
    e0, o0 = both(near_inner, near_inner)
    x2 = xor(quarter(k ^ 2, cx), 2)

    own_a, cx_a, x3_a, _ = lax.optimization_barrier((own, cx, x3, near_inner))
    near_outer = jnp.where(outer, own_a, cx_a)
    e1, o1 = both(jnp.where(flip, near_outer, x3_a), jnp.where(flip, x3_a, near_outer))

    own_b, cx_b, x3_b, x2_b, _, _ = lax.optimization_barrier((own_a, cx_a, x3_a, x2, e0, o0))
    far_inner = jnp.where(outer, x2_b, x3_b)
    e2, o2 = both(jnp.where(flip, far_inner, x2_b), jnp.where(flip, x2_b, far_inner))

    own_c, cx_c, x3_c, x2_c, _, _ = lax.optimization_barrier((own_b, cx_b, x3_b, x2_b, e1, o1))
    near_outer = jnp.where(outer, own_c, cx_c)
    far_outer = jnp.where(outer, x3_c, x2_c)
    e3, o3 = both(jnp.where(flip, far_outer, near_outer), jnp.where(flip, near_outer, far_outer))

    def f32(*shape):
        return jax.ShapeDtypeStruct(shape, jnp.float32)

    def parts(n):
        return [f32(rows, n * rows), f32(rows, n * rows), f32(2 * rows, n * rows)]

    def core_sum(other, send):
        core = xor(send, 1)
        return core, other + core[rows:]

    def fenced(function, *operands):
        shapes = jax.eval_shape(function, *operands)

        def never(*_):
            return jax.tree.map(lambda x: jnp.zeros(x.shape, x.dtype), shapes)

        return lax.cond(me >= 0, function, never, *operands)

    mine = (own, x2, cx, x3)

    def first_part(place, *operands):
        keep, other, send = call(first_kernel, parts(6), [], (place,), operands)
        return (keep, *core_sum(other, send))

    k1, c1, out1 = fenced(first_part, place, *mine, e0, o0)
    y1 = xor(out1, 2)

    def second_part(place, own, x2, cx, x3, *arrived):
        keep, other, send = call(
            cross_kernel, parts(3), [pltpu.VMEM((PLANE * rows, 3 * rows), jnp.float32)], (place,), arrived
        )
        core, out = core_sum(other, send)
        pack = keep + core[:rows] + xor(out, 2)
        place = after(place, keep)
        keep, other, send = call(second_kernel, parts(4), [], (place,), (own, x2, cx, x3, *arrived[2:]))
        return pack, keep, *core_sum(other, send)

    pack, k2, c2, out2 = fenced(second_part, place, *mine, e0, o0, e1, o1, e2, o2)
    ez, oz = both(pack, pack)
    y2 = xor(out2, 2)

    e3, o3, _, _ = lax.optimization_barrier((e3, o3, pack, y1))
    pair = f32(2 * rows, rows)
    k3, other, send = call(third_kernel, [pair, pair, f32(2 * rows, 2 * rows)], [], (place,), (*mine, e3, o3))
    c3 = xor(send, 1)
    y3 = xor(after(other + c3[:, rows:], y2), 2)

    return call(
        functools.partial(final_kernel, reach),
        [f32(rows, (2 * reach + 1) * rows)],
        [],
        (place, pair_list),
        (k1, c1, y1, k2, c2, y2, k3, c3, y3, ez, oz),
    )[0]


def solution(mesh):
    return jax.shard_map(
        functools.partial(body, mesh.shape["blk"]),
        mesh=mesh,
        in_specs=(P("blk", "groups"), P()),
        out_specs=P(("groups", "blk"), None),
        check_vma=False,
    )
```

time: 791 us -> 116 us (0.15)
  starting transfers between devices: 410 us -> 35.2 us
  waiting for transfers between devices: 296 us -> 40.7 us
  matrix products: 50.2 us -> 0 us
  Pallas kernels: 0 us -> 26 us
  local copies, waits for them, and re-layouts: 31.3 us -> 5.42 us
    ppermute x14 -> x21, starting transfers between devices: 410 us -> 35.2 us  [the longest x10 24.4 us: along(): return lax.ppermute(value, 'blk', route)]
    ppermute x14 -> x21, waiting for transfers between devices: 296 us -> 40.7 us  [the longest x11 38.3 us: xor(): return lax.ppermute(value, 'blk', [(i, i ^ t) for i in devices])]
    dot_general x1 -> x0, matrix products: 50.2 us -> none  [body(): jnp.einsum('mk,jnk->jmn', fitted_slab, stacked, precision=lax.Precision.H...]
    unnamed x23 -> x7, local copies, waits for them, and re-layouts: 27.7 us -> 0.77 us
    pallas_call x0 -> x5, Pallas kernels: none -> 26 us  [call(): pl.pallas_call(kernel, cost_estimate=pl.CostEstimate(flops=1000, bytes_ac...]
  transfers between devices with their start and end apart: 14 -> 21, of which waited for: 3 -> 9; matrix products, arithmetic and copies ran while one was open for 4% -> 10% of each run, Pallas kernels for 0% -> 17%
where the time goes in v2:
time: 116 us
  waiting for transfers between devices  40.7 us (35%)
  starting transfers between devices  35.2 us (30%)
  Pallas kernels  26 us (22%)
  other arithmetic  8.37 us (7%)
  local copies, waits for them, and re-layouts  5.42 us (5%)
    ppermute x11, waiting for transfers between devices, xor(): return lax.ppermute(value, 'blk', [(i, i ^ t) for i in devices])  38.3 us
    pallas_call x5, Pallas kernels, call(): pl.pallas_call(kernel, cost_estimate=pl.CostEstimate(flops=1000, bytes_ac...  26 us
    ppermute x10, starting transfers between devices, along(): return lax.ppermute(value, 'blk', route)  24.4 us
    ppermute x11, starting transfers between devices, xor(): return lax.ppermute(value, 'blk', [(i, i ^ t) for i in devices])  10.8 us
    squeeze x3, local copies, waits for them, and re-layouts, quarter(): lax.dynamic_index_in_dim(after(quarters, *others), index, 0, keepdims=False)  4.64 us
    add x3, other arithmetic, core_sum(): return (core, other + core[rows:])  2.85 us
    ppermute x10, waiting for transfers between devices, along(): return lax.ppermute(value, 'blk', route)  2.43 us
  transfers between devices with their start and end apart: 21, of which 9 were waited for; matrix products, arithmetic and copies ran while one was open for 10% of the time, Pallas kernels for 17%

profile of v2, /device:TPU:0, one launch (start us, length us, event | category | flops | bytes accessed | tf_op | source)
XLA Modules:
  0.0 115.9 jit_solution(14271641173332000792)
XLA Ops:
  0.0 2.2 %dynamic-slice_bitcast_fusion.3 = f32[1800,128]{1,0:T(8,128)} fusion(f32[4,1800,128]{2,1,0:T(8,128)} %bitcast.15, s32[]{:T(128)S(6)} %select_n.81), kind=kLoop, calls=%fused_computation.10 | loop fusion | bytes 1843204 | tf_op jit(solution)/shard_map/jit(dynamic_index_in_dim)/squeeze | solution.py:202
  3.9 2.7 %collective-permute-start.6 = (f32[1800,128]{1,0:T(8,128)S(1)}, f32[1800,128]{1,0:T(8,128)S(1)}, u32[]{:S(2)}, u32[]{:S(2)}) collective-permute-start(f32[1800,128]{1,0:T(8,128)S(1)} %dynamic-slice_bitcast_fusion), channel_id=1, source_target_pairs={{0,3},{1,2},{2,1},{3,0},{4,7},{5,6},{6,5},{7,4},{8,11},{9,10},{10,... | collective-permute-start | bytes 2764808 | tf_op jit(solution)/shard_map/ppermute | solution.py:186
  6.6 1.3 %broadcast_select_fusion.7 = (f32[1800,128]{1,0:T(8,128)S(1)}, f32[1800,128]{1,0:T(8,128)S(1)}) fusion(f32[1800,128]{1,0:T(8,128)S(1)} %collective-permute-done.4.cx, pred[]{:T(512)S(6)} %or.3, f32[4,1800,128]{2,1,0:T(8,128)} %bitcast.17, s32[]{:T(128)S(6)} %select_n.82), kind=kLoop, calls=%fused_computation.18 | loop fusion | flops 230400 | bytes 3686405 | tf_op jit(solution)/shard_map/jit(_where)/select_n | solution.py:209
  7.9 1.6 %collective-permute-start.8 = (f32[1800,128]{1,0:T(8,128)S(1)}, f32[1800,128]{1,0:T(8,128)}, u32[]{:S(2)}, u32[]{:S(2)}) collective-permute-start(f32[1800,128]{1,0:T(8,128)S(1)} %get-tuple-element.121), channel_id=1, source_target_pairs={{4,8},{5,9},{6,10},{7,11},{8,4},{9,5},{10,6},{11,7},{20,24},{21,25... | collective-permute-start | bytes 2764808 | tf_op jit(solution)/shard_map/ppermute | solution.py:194
  9.5 3.5 %collective-permute-start.7 = (f32[1800,128]{1,0:T(8,128)S(1)}, f32[1800,128]{1,0:T(8,128)}, u32[]{:S(2)}, u32[]{:S(2)}) collective-permute-start(f32[1800,128]{1,0:T(8,128)S(1)} %get-tuple-element.121), channel_id=1, source_target_pairs={{0,4},{1,5},{2,6},{3,7},{4,0},{5,1},{6,2},{7,3},{8,12},{9,13},{10,... | collective-permute-start | bytes 2764808 | tf_op jit(solution)/shard_map/ppermute | solution.py:194
  14.3 1.3 %collective-permute-start.5 = (f32[1800,128]{1,0:T(8,128)S(1)}, f32[1800,128]{1,0:T(8,128)S(1)}, u32[]{:S(2)}, u32[]{:S(2)}) collective-permute-start(f32[1800,128]{1,0:T(8,128)S(1)} %dynamic-slice_bitcast_fusion.1), channel_id=1, source_target_pairs={{0,2},{1,3},{2,0},{3,1},{4,6},{5,7},{6,4},{7,5},{8,10},{9,11},{10,... | collective-permute-start | bytes 2764808 | tf_op jit(solution)/shard_map/ppermute | solution.py:186
  15.6 11.8 %collective-permute-done.6.x3 = f32[1800,128]{1,0:T(8,128)S(1)} collective-permute-done((f32[1800,128]{1,0:T(8,128)S(1)}, f32[1800,128]{1,0:T(8,128)S(1)}, u32[]{:S(2)}, u32[]{:S(2)}) %collective-permute-start.6) | collective-permute-done | bytes 921632 | tf_op jit(solution)/shard_map/ppermute | solution.py:186
  27.7 1.6 %collective-permute-start.11 = (f32[1800,128]{1,0:T(8,128)S(1)}, f32[1800,128]{1,0:T(8,128)}, u32[]{:S(2)}, u32[]{:S(2)}) collective-permute-start(f32[1800,128]{1,0:T(8,128)S(1)} %get-tuple-element.125), channel_id=1, source_target_pairs={{4,8},{5,9},{6,10},{7,11},{8,4},{9,5},{10,6},{11,7},{20,24},{21,25... | collective-permute-start | bytes 2764808 | tf_op jit(solution)/shard_map/ppermute | solution.py:194
  29.3 3.5 %collective-permute-start.10 = (f32[1800,128]{1,0:T(8,128)S(1)}, f32[1800,128]{1,0:T(8,128)}, u32[]{:S(2)}, u32[]{:S(2)}) collective-permute-start(f32[1800,128]{1,0:T(8,128)S(1)} %get-tuple-element.126), channel_id=1, source_target_pairs={{0,4},{1,5},{2,6},{3,7},{4,0},{5,1},{6,2},{7,3},{8,12},{9,13},{10,... | collective-permute-start | bytes 2764808 | tf_op jit(solution)/shard_map/ppermute | solution.py:194
  32.8 14.5 %collective-permute-done.5.x2 = f32[1800,128]{1,0:T(8,128)S(1)} collective-permute-done((f32[1800,128]{1,0:T(8,128)S(1)}, f32[1800,128]{1,0:T(8,128)S(1)}, u32[]{:S(2)}, u32[]{:S(2)}) %collective-permute-start.5) | collective-permute-done | bytes 921632 | tf_op jit(solution)/shard_map/ppermute | solution.py:186
  47.3 1.5 %select_select_fusion = (f32[1800,128]{1,0:T(8,128)}, f32[1800,128]{1,0:T(8,128)}) fusion(f32[1800,128]{1,0:T(8,128)S(1)} %collective-permute-done.5.x2, f32[1800,128]{1,0:T(8,128)S(1)} %collective-permute-done.6.x3, pred[]{:T(512)S(6)} %xor.15, pred[]{:T(512)S(6)} %or.3), kind=kLoop, calls=%fused_computation.5 | loop fusion | flops 691200 | bytes 3686402 | tf_op jit(solution)/shard_map/jit(_where)/select_n | solution.py:219
  48.8 1.6 %collective-permute-start.13 = (f32[1800,128]{1,0:T(8,128)}, f32[1800,128]{1,0:T(8,128)}, u32[]{:S(2)}, u32[]{:S(2)}) collective-permute-start(f32[1800,128]{1,0:T(8,128)} %get-tuple-element.127), channel_id=1, source_target_pairs={{4,8},{5,9},{6,10},{7,11},{8,4},{9,5},{10,6},{11,7},{20,24},{21,25... | collective-permute-start | bytes 2764808 | tf_op jit(solution)/shard_map/ppermute | solution.py:194
  50.4 3.6 %collective-permute-start.12 = (f32[1800,128]{1,0:T(8,128)}, f32[1800,128]{1,0:T(8,128)}, u32[]{:S(2)}, u32[]{:S(2)}) collective-permute-start(f32[1800,128]{1,0:T(8,128)} %get-tuple-element.128), channel_id=1, source_target_pairs={{0,4},{1,5},{2,6},{3,7},{4,0},{5,1},{6,2},{7,3},{8,12},{9,13},{10,... | collective-permute-start | bytes 2764808 | tf_op jit(solution)/shard_map/ppermute | solution.py:194
  54.1 1.5 %broadcast_select_fusion = (f32[1800,128]{1,0:T(8,128)}, f32[1800,128]{1,0:T(8,128)}) fusion(pred[]{:T(512)S(6)} %xor.15, f32[1800,128]{1,0:T(8,128)S(1)} %collective-permute-done.6.x3, f32[1800,128]{1,0:T(8,128)S(1)} %collective-permute-done.5.x2, pred[]{:T(512)S(6)} %or.3, f32[1800,128]{1,0:T(8,128)S(1)} %get-tuple-element.112.own, ...), kind=kLoop, calls=%fused_computation.11 | loop fusion | flops 921600 | bytes 5529602 | tf_op jit(solution)/shard_map/jit(_where)/select_n | solution.py:224
  56.4 3.8 %collective-permute-start.15 = (f32[1800,128]{1,0:T(8,128)}, f32[1800,128]{1,0:T(8,128)S(1)}, u32[]{:S(2)}, u32[]{:S(2)}) collective-permute-start(f32[1800,128]{1,0:T(8,128)} %get-tuple-element.124), channel_id=1, source_target_pairs={{0,4},{1,5},{2,6},{3,7},{4,0},{5,1},{6,2},{7,3},{8,12},{9,13},{10,... | collective-permute-start | bytes 2764808 | tf_op jit(solution)/shard_map/ppermute | solution.py:194
  60.2 12.3 %conditional.2 = (f32[128,768]{1,0:T(8,128)}, f32[256,768]{1,0:T(8,128)}, f32[128,768]{1,0:T(8,128)}) conditional(s32[]{:T(128)} %convert_element_type.4, () %tuple.29, (s32[3]{0:T(128)S(1)}, f32[1800,128]{1,0:T(8,128)}, f32[1800,128]{1,0:T(8,128)}, f32[1800,128]{1,0:T(8,128)S(1)}, f32[1800,128]{1,0:T(8,128)}, /*index=5*/f32[1800,128]{1,0:T(8,128)}, ...), branch_computations={%region_0.1_spmd, %region_1.2_spmd} | conditional | flops 99304 | bytes 4326440 | solution.py:242
  60.2 8.0 %branch_1_fun.3 = (f32[128,768]{1,0:T(8,128)}, f32[128,768]{1,0:T(8,128)S(1)}, f32[256,768]{1,0:T(8,128)S(1)}) custom-call(s32[3]{0:T(128)S(1)} %get-tuple-element.41.at_ref, f32[1800,128]{1,0:T(8,128)} %get-tuple-element.42.own, f32[1800,128]{1,0:T(8,128)} %get-tuple-element.43.x2, f32[1800,128]{1,0:T(8,128)S(1)} %get-tuple-element.44.cx, ...), custom_call_target="tpu_custom_call" | custom-call | flops 1000 | bytes 1000 | tf_op jit(solution)/shard_map/cond/branch_1_fun/pallas_call | solution.py:156
  68.3 2.4 %collective-permute-done = f32[256,768]{1,0:T(8,128)} collective-permute-done((f32[256,768]{1,0:T(8,128)S(1)}, f32[256,768]{1,0:T(8,128)}, u32[]{:S(2)}, u32[]{:S(2)}) %collective-permute-start) | collective-permute-done | bytes 786464 | tf_op jit(solution)/shard_map/cond/branch_1_fun/ppermute | solution.py:186
  70.7 1.8 %slice_add_fusion = f32[128,768]{1,0:T(8,128)} fusion(f32[128,768]{1,0:T(8,128)S(1)} %get-tuple-element.50, f32[256,768]{1,0:T(8,128)} %collective-permute-done), kind=kLoop, calls=%fused_computation | loop fusion | flops 98304 | bytes 1179648 | tf_op jit(solution)/shard_map/cond/branch_1_fun/add | solution.py:234
  73.5 2.2 %collective-permute-done.12 = f32[1800,128]{1,0:T(8,128)} collective-permute-done((f32[1800,128]{1,0:T(8,128)}, f32[1800,128]{1,0:T(8,128)}, u32[]{:S(2)}, u32[]{:S(2)}) %collective-permute-start.12) | collective-permute-done | bytes 921632 | tf_op jit(solution)/shard_map/ppermute | solution.py:194
  75.7 19.6 %conditional.3 = (f32[128,384]{1,0:T(8,128)}, f32[128,512]{1,0:T(8,128)S(1)}, f32[256,512]{1,0:T(8,128)}, f32[128,512]{1,0:T(8,128)S(1)}) conditional(s32[]{:T(128)} %convert_element_type.4, () %tuple.33, (s32[3]{0:T(128)S(1)}, f32[1800,128]{1,0:T(8,128)}, f32[1800,128]{1,0:T(8,128)}, f32[1800,128]{1,0:T(8,128)}, f32[1800,128]{1,0:T(8,128)}, ...), branch_computations={%region_2.3_spmd, %region_3.4_spmd} | conditional | flops 214992 | bytes 17680572 | solution.py:242
  75.7 5.8 %branch_1_fun.4 = (f32[128,384]{1,0:T(8,128)S(1)}, f32[128,384]{1,0:T(8,128)S(1)}, f32[256,384]{1,0:T(8,128)S(1)}) custom-call(s32[3]{0:T(128)S(1)} %get-tuple-element.61.at_ref, f32[1800,128]{1,0:T(8,128)} %get-tuple-element.52.e0, f32[1800,128]{1,0:T(8,128)} %get-tuple-element.53.o0, f32[1800,128]{1,0:T(8,128)} %get-tuple-element.54.e1, ...), custom_call_target="tpu_custom_call" | custom-call | flops 1000 | bytes 1000 | tf_op jit(solution)/shard_map/cond/branch_1_fun/pallas_call | solution.py:156
  81.6 5.5 %branch_1_fun.5 = (f32[128,512]{1,0:T(8,128)S(1)}, f32[128,512]{1,0:T(8,128)S(1)}, f32[256,512]{1,0:T(8,128)S(1)}) custom-call(s32[3]{0:T(128)S(1)} %get-tuple-element.61.at_ref, f32[1800,128]{1,0:T(8,128)S(1)} %copy-done.3, f32[1800,128]{1,0:T(8,128)S(1)} %copy-done.5, f32[1800,128]{1,0:T(8,128)S(1)} %get-tuple-element.64.cx, f32[1800,128]{1,0:T(8,128)S(1)} %copy-done.1, ...), custom_call_target="tpu_custom_call" | custom-call | flops 1000 | bytes 1000 | tf_op jit(solution)/shard_map/cond/branch_1_fun/pallas_call | solution.py:156
  87.7 1.6 %collective-permute-start.2 = (f32[128,384]{1,0:T(8,128)S(1)}, f32[128,384]{1,0:T(8,128)S(1)}, u32[]{:S(2)}, u32[]{:S(2)}) collective-permute-start(f32[128,384]{1,0:T(8,128)S(1)} %slice_add_fusion.2), channel_id=1, source_target_pairs={{0,2},{1,3},{2,0},{3,1},{4,6},{5,7},{6,4},{7,5},{8,10},{9,11},{10,... | collective-permute-start | bytes 589832 | tf_op jit(solution)/shard_map/cond/branch_1_fun/ppermute | solution.py:186
  90.3 4.3 %collective-permute-done.2 = f32[128,384]{1,0:T(8,128)S(1)} collective-permute-done((f32[128,384]{1,0:T(8,128)S(1)}, f32[128,384]{1,0:T(8,128)S(1)}, u32[]{:S(2)}, u32[]{:S(2)}) %collective-permute-start.2) | collective-permute-done | bytes 196640 | tf_op jit(solution)/shard_map/cond/branch_1_fun/ppermute | solution.py:186
  95.4 3.7 %shard_map.28 = (f32[256,128]{1,0:T(8,128)S(1)}, f32[256,128]{1,0:T(8,128)S(1)}, f32[256,256]{1,0:T(8,128)S(1)}) custom-call(s32[3]{0:T(128)S(1)} %pad_add_fusion.at_ref, f32[1800,128]{1,0:T(8,128)} %copy-done.2, f32[1800,128]{1,0:T(8,128)} %copy-done.4, f32[1800,128]{1,0:T(8,128)S(1)} %collective-permute-done.4.cx, f32[1800,128]{1,0:T(8,128)} %copy-done, ...), custom_call_target="tpu_custom_call" | custom-call | flops 1000 | bytes 1000 | tf_op jit(solution)/shard_map/pallas_call | solution.py:156
  99.1 1.6 %collective-permute-start.14 = (f32[128,512]{1,0:T(8,128)S(1)}, f32[128,512]{1,0:T(8,128)S(1)}, u32[]{:S(2)}, u32[]{:S(2)}) collective-permute-start(f32[128,512]{1,0:T(8,128)S(1)} %get-tuple-element.107), channel_id=1, source_target_pairs={{0,2},{1,3},{2,0},{3,1},{4,6},{5,7},{6,4},{7,5},{8,10},{9,11},{10,... | collective-permute-start | bytes 786440 | tf_op jit(solution)/shard_map/ppermute | solution.py:186
  101.4 3.8 %collective-permute-start.19 = (f32[128,384]{1,0:T(8,128)}, f32[128,384]{1,0:T(8,128)S(1)}, u32[]{:S(2)}, u32[]{:S(2)}) collective-permute-start(f32[128,384]{1,0:T(8,128)} %get-tuple-element.114), channel_id=1, source_target_pairs={{0,4},{1,5},{2,6},{3,7},{4,0},{5,1},{6,2},{7,3},{8,12},{9,13},{10,... | collective-permute-start | bytes 589832 | tf_op jit(solution)/shard_map/ppermute | solution.py:194
  105.2 2.7 %collective-permute-done.14.y2 = f32[128,512]{1,0:T(8,128)S(1)} collective-permute-done((f32[128,512]{1,0:T(8,128)S(1)}, f32[128,512]{1,0:T(8,128)S(1)}, u32[]{:S(2)}, u32[]{:S(2)}) %collective-permute-start.14) | collective-permute-done | bytes 262176 | tf_op jit(solution)/shard_map/ppermute | solution.py:186
  107.8 1.5 %collective-permute-start.18 = (f32[256,128]{1,0:T(8,128)S(1)}, f32[256,128]{1,0:T(8,128)S(1)}, u32[]{:S(2)}, u32[]{:S(2)}) collective-permute-start(f32[256,128]{1,0:T(8,128)S(1)} %slice_add_fusion.4), channel_id=1, source_target_pairs={{0,2},{1,3},{2,0},{3,1},{4,6},{5,7},{6,4},{7,5},{8,10},{9,11},{10,... | collective-permute-start | bytes 393224 | tf_op jit(solution)/shard_map/ppermute | solution.py:186
  110.3 2.6 %collective-permute-done.18.y3 = f32[256,128]{1,0:T(8,128)S(1)} collective-permute-done((f32[256,128]{1,0:T(8,128)S(1)}, f32[256,128]{1,0:T(8,128)S(1)}, u32[]{:S(2)}, u32[]{:S(2)}) %collective-permute-start.18) | collective-permute-done | bytes 131104 | tf_op jit(solution)/shard_map/ppermute | solution.py:186
  112.9 3.0 %shard_map.29 = f32[128,1920]{1,0:T(8,128)} custom-call(s32[3]{0:T(128)S(1)} %pad_add_fusion.at_ref, s32[16,8]{1,0:T(8,128)S(1)} %copy.3.pairs, f32[128,768]{1,0:T(8,128)} %get-tuple-element.97.k1, f32[256,768]{1,0:T(8,128)} %get-tuple-element.98.c1, f32[128,768]{1,0:T(8,128)S(1)} %collective-permute-done.9.y1, f32[128,512]{1,0:T(8,128)S(1)} %get-tuple-element.105.k2, ...), custom_call_target="tpu_custom_call" | custom-call | flops 1000 | bytes 1000 | tf_op jit(solution)/shard_map/pallas_call | solution.py:156
  (43 shorter events, 9.2 us)
Async XLA Ops:
  2.2 4.4 %collective-permute-start.4 = (f32[1800,128]{1,0:T(8,128)}, f32[1800,128]{1,0:T(8,128)S(1)}, u32[]{:S(2)}, u32[]{:S(2)}) collective-permute-start(f32[1800,128]{1,0:T(8,128)} %dynamic-slice_bitcast_fusion.3), channel_id=1, source_target_pairs={{0,1},{1,0},{2,3},{3,2},{4,5},{5,4},{6,7},{7,6},{8,9},{9,8},{10,11... | collective-permute-start | bytes 2764808 | tf_op jit(solution)/shard_map/ppermute | solution.py:186
  3.9 23.5 %collective-permute-start.6 = (f32[1800,128]{1,0:T(8,128)S(1)}, f32[1800,128]{1,0:T(8,128)S(1)}, u32[]{:S(2)}, u32[]{:S(2)}) collective-permute-start(f32[1800,128]{1,0:T(8,128)S(1)} %dynamic-slice_bitcast_fusion), channel_id=1, source_target_pairs={{0,3},{1,2},{2,1},{3,0},{4,7},{5,6},{6,5},{7,4},{8,11},{9,10},{10,... | collective-permute-start | bytes 2764808 | tf_op jit(solution)/shard_map/ppermute | solution.py:186
  7.9 46.2 %copy-start.2 = (f32[1800,128]{1,0:T(8,128)}, f32[1800,128]{1,0:T(8,128)S(1)}, u32[]{:S(2)}) copy-start(f32[1800,128]{1,0:T(8,128)S(1)} %get-tuple-element.112.own) | copy-start | bytes 2764804
  7.9 39.4 %collective-permute-start.8 = (f32[1800,128]{1,0:T(8,128)S(1)}, f32[1800,128]{1,0:T(8,128)}, u32[]{:S(2)}, u32[]{:S(2)}) collective-permute-start(f32[1800,128]{1,0:T(8,128)S(1)} %get-tuple-element.121), channel_id=1, source_target_pairs={{4,8},{5,9},{6,10},{7,11},{8,4},{9,5},{10,6},{11,7},{20,24},{21,25... | collective-permute-start | bytes 2764808 | tf_op jit(solution)/shard_map/ppermute | solution.py:194
  9.5 37.8 %collective-permute-start.7 = (f32[1800,128]{1,0:T(8,128)S(1)}, f32[1800,128]{1,0:T(8,128)}, u32[]{:S(2)}, u32[]{:S(2)}) collective-permute-start(f32[1800,128]{1,0:T(8,128)S(1)} %get-tuple-element.121), channel_id=1, source_target_pairs={{0,4},{1,5},{2,6},{3,7},{4,0},{5,1},{6,2},{7,3},{8,12},{9,13},{10,... | collective-permute-start | bytes 2764808 | tf_op jit(solution)/shard_map/ppermute | solution.py:194
  14.3 33.0 %collective-permute-start.5 = (f32[1800,128]{1,0:T(8,128)S(1)}, f32[1800,128]{1,0:T(8,128)S(1)}, u32[]{:S(2)}, u32[]{:S(2)}) collective-permute-start(f32[1800,128]{1,0:T(8,128)S(1)} %dynamic-slice_bitcast_fusion.1), channel_id=1, source_target_pairs={{0,2},{1,3},{2,0},{3,1},{4,6},{5,7},{6,4},{7,5},{8,10},{9,11},{10,... | collective-permute-start | bytes 2764808 | tf_op jit(solution)/shard_map/ppermute | solution.py:186
  27.4 26.7 %copy-start = (f32[1800,128]{1,0:T(8,128)}, f32[1800,128]{1,0:T(8,128)S(1)}, u32[]{:S(2)}) copy-start(f32[1800,128]{1,0:T(8,128)S(1)} %collective-permute-done.6.x3) | copy-start | bytes 2764804
  27.7 26.4 %collective-permute-start.11 = (f32[1800,128]{1,0:T(8,128)S(1)}, f32[1800,128]{1,0:T(8,128)}, u32[]{:S(2)}, u32[]{:S(2)}) collective-permute-start(f32[1800,128]{1,0:T(8,128)S(1)} %get-tuple-element.125), channel_id=1, source_target_pairs={{4,8},{5,9},{6,10},{7,11},{8,4},{9,5},{10,6},{11,7},{20,24},{21,25... | collective-permute-start | bytes 2764808 | tf_op jit(solution)/shard_map/ppermute | solution.py:194
  29.3 24.8 %collective-permute-start.10 = (f32[1800,128]{1,0:T(8,128)S(1)}, f32[1800,128]{1,0:T(8,128)}, u32[]{:S(2)}, u32[]{:S(2)}) collective-permute-start(f32[1800,128]{1,0:T(8,128)S(1)} %get-tuple-element.126), channel_id=1, source_target_pairs={{0,4},{1,5},{2,6},{3,7},{4,0},{5,1},{6,2},{7,3},{8,12},{9,13},{10,... | collective-permute-start | bytes 2764808 | tf_op jit(solution)/shard_map/ppermute | solution.py:194
  47.3 8.3 %copy-start.4 = (f32[1800,128]{1,0:T(8,128)}, f32[1800,128]{1,0:T(8,128)S(1)}, u32[]{:S(2)}) copy-start(f32[1800,128]{1,0:T(8,128)S(1)} %collective-permute-done.5.x2) | copy-start | bytes 2764804
  48.8 24.7 %collective-permute-start.13 = (f32[1800,128]{1,0:T(8,128)}, f32[1800,128]{1,0:T(8,128)}, u32[]{:S(2)}, u32[]{:S(2)}) collective-permute-start(f32[1800,128]{1,0:T(8,128)} %get-tuple-element.127), channel_id=1, source_target_pairs={{4,8},{5,9},{6,10},{7,11},{8,4},{9,5},{10,6},{11,7},{20,24},{21,25... | collective-permute-start | bytes 2764808 | tf_op jit(solution)/shard_map/ppermute | solution.py:194
  50.4 25.3 %collective-permute-start.12 = (f32[1800,128]{1,0:T(8,128)}, f32[1800,128]{1,0:T(8,128)}, u32[]{:S(2)}, u32[]{:S(2)}) collective-permute-start(f32[1800,128]{1,0:T(8,128)} %get-tuple-element.128), channel_id=1, source_target_pairs={{0,4},{1,5},{2,6},{3,7},{4,0},{5,1},{6,2},{7,3},{8,12},{9,13},{10,... | collective-permute-start | bytes 2764808 | tf_op jit(solution)/shard_map/ppermute | solution.py:194
  55.6 39.7 %collective-permute-start.16 = (f32[1800,128]{1,0:T(8,128)}, f32[1800,128]{1,0:T(8,128)S(1)}, u32[]{:S(2)}, u32[]{:S(2)}) collective-permute-start(f32[1800,128]{1,0:T(8,128)} %get-tuple-element.123), channel_id=1, source_target_pairs={{4,8},{5,9},{6,10},{7,11},{8,4},{9,5},{10,6},{11,7},{20,24},{21,25... | collective-permute-start | bytes 2764808 | tf_op jit(solution)/shard_map/ppermute | solution.py:194
  56.4 39.0 %collective-permute-start.15 = (f32[1800,128]{1,0:T(8,128)}, f32[1800,128]{1,0:T(8,128)S(1)}, u32[]{:S(2)}, u32[]{:S(2)}) collective-permute-start(f32[1800,128]{1,0:T(8,128)} %get-tuple-element.124), channel_id=1, source_target_pairs={{0,4},{1,5},{2,6},{3,7},{4,0},{5,1},{6,2},{7,3},{8,12},{9,13},{10,... | collective-permute-start | bytes 2764808 | tf_op jit(solution)/shard_map/ppermute | solution.py:194
  68.3 2.4 %collective-permute-start = (f32[256,768]{1,0:T(8,128)S(1)}, f32[256,768]{1,0:T(8,128)}, u32[]{:S(2)}, u32[]{:S(2)}) collective-permute-start(f32[256,768]{1,0:T(8,128)S(1)} %get-tuple-element.49), channel_id=1, source_target_pairs={{0,1},{1,0},{2,3},{3,2},{4,5},{5,4},{6,7},{7,6},{8,9},{9,8},{10,11... | collective-permute-start | bytes 2359304 | tf_op jit(solution)/shard_map/cond/branch_1_fun/ppermute | solution.py:186
  72.5 22.8 %collective-permute-start.9 = (f32[128,768]{1,0:T(8,128)}, f32[128,768]{1,0:T(8,128)S(1)}, u32[]{:S(2)}, u32[]{:S(2)}) collective-permute-start(f32[128,768]{1,0:T(8,128)} %get-tuple-element.99), channel_id=1, source_target_pairs={{0,2},{1,3},{2,0},{3,1},{4,6},{5,7},{6,4},{7,5},{8,10},{9,11},{10,... | collective-permute-start | bytes 1179656 | tf_op jit(solution)/shard_map/ppermute | solution.py:186
  75.7 5.9 %copy-start.1 = (f32[1800,128]{1,0:T(8,128)S(1)}, f32[1800,128]{1,0:T(8,128)}, u32[]{:S(2)}) copy-start(f32[1800,128]{1,0:T(8,128)} %get-tuple-element.65.x3) | copy-start | bytes 2764804 | tf_op jit(solution)/shard_map/cond
  75.7 5.9 %copy-start.3 = (f32[1800,128]{1,0:T(8,128)S(1)}, f32[1800,128]{1,0:T(8,128)}, u32[]{:S(2)}) copy-start(f32[1800,128]{1,0:T(8,128)} %get-tuple-element.62.own) | copy-start | bytes 2764804 | tf_op jit(solution)/shard_map/cond
  75.7 5.9 %copy-start.5 = (f32[1800,128]{1,0:T(8,128)S(1)}, f32[1800,128]{1,0:T(8,128)}, u32[]{:S(2)}) copy-start(f32[1800,128]{1,0:T(8,128)} %get-tuple-element.63.x2) | copy-start | bytes 2764804 | tf_op jit(solution)/shard_map/cond
  81.5 6.2 %collective-permute-start.1 = (f32[256,384]{1,0:T(8,128)S(1)}, f32[256,384]{1,0:T(8,128)S(1)}, u32[]{:S(2)}, u32[]{:S(2)}) collective-permute-start(f32[256,384]{1,0:T(8,128)S(1)} %get-tuple-element.59), channel_id=1, source_target_pairs={{0,1},{1,0},{2,3},{3,2},{4,5},{5,4},{6,7},{7,6},{8,9},{9,8},{10,11... | collective-permute-start | bytes 1179656 | tf_op jit(solution)/shard_map/cond/branch_1_fun/ppermute | solution.py:186
  87.2 2.2 %collective-permute-start.3 = (f32[256,512]{1,0:T(8,128)S(1)}, f32[256,512]{1,0:T(8,128)}, u32[]{:S(2)}, u32[]{:S(2)}) collective-permute-start(f32[256,512]{1,0:T(8,128)S(1)} %get-tuple-element.67), channel_id=1, source_target_pairs={{0,1},{1,0},{2,3},{3,2},{4,5},{5,4},{6,7},{7,6},{8,9},{9,8},{10,11... | collective-permute-start | bytes 1572872 | tf_op jit(solution)/shard_map/cond/branch_1_fun/ppermute | solution.py:186
  87.7 6.9 %collective-permute-start.2 = (f32[128,384]{1,0:T(8,128)S(1)}, f32[128,384]{1,0:T(8,128)S(1)}, u32[]{:S(2)}, u32[]{:S(2)}) collective-permute-start(f32[128,384]{1,0:T(8,128)S(1)} %slice_add_fusion.2), channel_id=1, source_target_pairs={{0,2},{1,3},{2,0},{3,1},{4,6},{5,7},{6,4},{7,5},{8,10},{9,11},{10,... | collective-permute-start | bytes 589832 | tf_op jit(solution)/shard_map/cond/branch_1_fun/ppermute | solution.py:186
  99.0 6.1 %collective-permute-start.17 = (f32[256,256]{1,0:T(8,128)S(1)}, f32[256,256]{1,0:T(8,128)S(1)}, u32[]{:S(2)}, u32[]{:S(2)}) collective-permute-start(f32[256,256]{1,0:T(8,128)S(1)} %get-tuple-element.118), channel_id=1, source_target_pairs={{0,1},{1,0},{2,3},{3,2},{4,5},{5,4},{6,7},{7,6},{8,9},{9,8},{10,11... | collective-permute-start | bytes 786440 | tf_op jit(solution)/shard_map/ppermute | solution.py:186
  99.1 8.7 %collective-permute-start.14 = (f32[128,512]{1,0:T(8,128)S(1)}, f32[128,512]{1,0:T(8,128)S(1)}, u32[]{:S(2)}, u32[]{:S(2)}) collective-permute-start(f32[128,512]{1,0:T(8,128)S(1)} %get-tuple-element.107), channel_id=1, source_target_pairs={{0,2},{1,3},{2,0},{3,1},{4,6},{5,7},{6,4},{7,5},{8,10},{9,11},{10,... | collective-permute-start | bytes 786440 | tf_op jit(solution)/shard_map/ppermute | solution.py:186
  100.7 9.4 %collective-permute-start.20 = (f32[128,384]{1,0:T(8,128)}, f32[128,384]{1,0:T(8,128)S(1)}, u32[]{:S(2)}, u32[]{:S(2)}) collective-permute-start(f32[128,384]{1,0:T(8,128)} %get-tuple-element.114), channel_id=1, source_target_pairs={{4,8},{5,9},{6,10},{7,11},{8,4},{9,5},{10,6},{11,7},{20,24},{21,25... | collective-permute-start | bytes 589832 | tf_op jit(solution)/shard_map/ppermute | solution.py:194
  101.4 9.0 %collective-permute-start.19 = (f32[128,384]{1,0:T(8,128)}, f32[128,384]{1,0:T(8,128)S(1)}, u32[]{:S(2)}, u32[]{:S(2)}) collective-permute-start(f32[128,384]{1,0:T(8,128)} %get-tuple-element.114), channel_id=1, source_target_pairs={{0,4},{1,5},{2,6},{3,7},{4,0},{5,1},{6,2},{7,3},{8,12},{9,13},{10,... | collective-permute-start | bytes 589832 | tf_op jit(solution)/shard_map/ppermute | solution.py:194
  107.8 5.1 %collective-permute-start.18 = (f32[256,128]{1,0:T(8,128)S(1)}, f32[256,128]{1,0:T(8,128)S(1)}, u32[]{:S(2)}, u32[]{:S(2)}) collective-permute-start(f32[256,128]{1,0:T(8,128)S(1)} %slice_add_fusion.4), channel_id=1, source_target_pairs={{0,2},{1,3},{2,0},{3,1},{4,6},{5,7},{6,4},{7,5},{8,10},{9,11},{10,... | collective-permute-start | bytes 393224 | tf_op jit(solution)/shard_map/ppermute | solution.py:186

commit v3 on v2

v3 whole, which is shorter than its diff:
```python
import functools

import jax
import jax.numpy as jnp
from jax import lax
from jax.experimental import pallas as pl
from jax.experimental.pallas import tpu as pltpu
from jax.sharding import PartitionSpec as P

PLANE = 4
VMEM_BYTES = 44 * 2**20


def halves(value):
    high = value.astype(jnp.bfloat16)
    return high, (value - high.astype(jnp.float32)).astype(jnp.bfloat16)


def product(a, b):
    dot = functools.partial(
        lax.dot_general,
        dimension_numbers=(((0,), (0,)), ((), ())),
        preferred_element_type=jnp.float32,
    )
    (ah, al), (bh, bl) = halves(a), halves(b)
    return dot(ah, bh) + (dot(ah, bl) + dot(al, bh))


def side_by_side(*values):
    return jnp.concatenate(values, 1)


def block(index, size):
    if isinstance(index, int):
        return slice(index * size, (index + 1) * size)
    return pl.ds(pl.multiple_of(index * size, size), size)


def spread(value, keep, other, send):
    rows = keep.shape[0]
    keep[...] = value[:rows]
    other[...] = value[rows : 2 * rows]
    send[...] = value[2 * rows :]


def place_columns(value, keep, other, send, places):
    rows = keep.shape[0]
    for ref, r in ((keep, 0), (other, rows), (send, 2 * rows)):
        for i, index in enumerate(places):
            ref[:, block(index, rows)] = value[r : r + ref.shape[0], block(i, rows)]


def clear_column(keep, other, send, index):
    rows = keep.shape[0]
    for ref in (keep, other, send):
        ref[:, block(index, rows)] = jnp.zeros((ref.shape[0], rows), ref.dtype)


def first_kernel(at_ref, own, x2, cx, x3, e0, o0, e1, o1, keep, other, send):
    k, flip = at_ref[0], at_ref[2] == 1
    mine = side_by_side(own[...], x2[...], cx[...], x3[...])
    out = product(mine, side_by_side(mine, e0[...], o0[...], e1[...], o1[...]))
    first = jnp.where((k == 1) | (k == 2), 8, 7)
    even = jnp.where(flip, first, 6)
    place_columns(out, keep, other, send, (k, k ^ 2, k ^ 1, k ^ 3, 4, 5, even, 6 + first - even))
    clear_column(keep, other, send, 15 - first)


def add_kernel(a, b, out):
    out[...] = a[...] + b[...]


def cross_kernel(at_ref, e0, o0, e1, o1, e2, o2, keep, other, send, cross, packs):
    k, odd = at_ref[0], at_ref[1] == 1
    rows = e0.shape[1]
    cross[...] = product(side_by_side(e0[...], e1[...], e2[...]), side_by_side(o0[...], o1[...], o2[...]))
    upper = k >= 2
    low_2 = jnp.where(upper, 0, jnp.where(k == 1, 1, 2))
    low = (None, jnp.where(upper, 2, 0), low_2, jnp.where(k == 1, 2, 1))
    high_1 = jnp.where(upper, jnp.where(k == 2, 1, 2), 0)
    high = (jnp.where(k == 2, 2, 1), high_1, jnp.where(upper, 0, 2))

    def put(owner, m, value):
        t = owner ^ k
        place = jnp.where(t == 1, 2, jnp.where(t == 2, 1, t))
        packs[block(place, rows), block(m, rows)] = value

    for i in range(1, PLANE):
        for j in range(i):
            r, c = jnp.where(odd, low[i], high[j]), jnp.where(odd, high[j], low[i])
            value = cross[block(r, rows), block(c, rows)]
            turned = value.T
            put(i, j, jnp.where(odd, value, turned))
            put(j, i - 1, jnp.where(odd, turned, value))
    spread(packs[...], keep, other, send)


def second_kernel(at_ref, own, x2, cx, x3, e2, o2, keep, other, send):
    k, flip = at_ref[0], at_ref[2] == 1
    mine = side_by_side(own[...], x2[...], cx[...], x3[...])
    out = product(mine, side_by_side(e2[...], o2[...]))
    last = jnp.where((k == 1) | (k == 2), 0, 1)
    even = jnp.where(flip, last, 2)
    place_columns(out, keep, other, send, (even, 2 + last - even))
    clear_column(keep, other, send, 1 - last)


def third_kernel(own, x2, cx, x3, e3, o3, keep, other, send):
    rows = own.shape[1]
    mine = side_by_side(own[...], x2[...], cx[...], x3[...])
    out = product(side_by_side(e3[...], o3[...]), mine)
    keep[...] = out[:, :rows]
    other[...] = out[:, rows : 2 * rows]
    send[...] = out[:, 2 * rows :]


def wanted(pairs, me, offset, reach):
    row = me + jnp.minimum(offset, 0)
    distance = jnp.abs(offset)
    found = pairs[jnp.maximum(row, 0), 0] == distance
    for m in range(1, reach + 1):
        found = found | (pairs[jnp.maximum(row, 0), m] == distance)
    return jnp.where(found & (row >= 0), 1.0, 0.0)


def band_kernel(reach, at_ref, pairs, t1, y1, t2, y2, out):
    k, flip, me = at_ref[0], at_ref[2], at_ref[3]
    rows = out.shape[0]
    upper = k >= 2

    def write(index, *terms):
        slot = index - k - 1
        total = functools.reduce(jnp.add, [ref[:, block(i, rows)] for ref, i in terms])
        out[:, block(slot, rows)] = total * wanted(pairs, me, slot - reach, reach)

    for i in range(PLANE):
        write(2 * PLANE + i, (t1, i), (y1, i))
    low, high = PLANE, 3 * PLANE
    here, there = jnp.where(upper, high, low), jnp.where(upper, low, high)
    near = jnp.where(upper, 2, 1)
    this, that = 5 - flip, 4 + flip
    write(here + near, (t1, this), (y2, 2))
    write(there + near, (t1, that), (y2, 1), (y1, 8))
    write(here + 3 - near, (t2, 1), (t1, 8), (y1, this))
    write(there + 3 - near, (t2, 2), (y1, that))
    write(jnp.where(upper, high, low + 3), (t2, 0), (t1, 7), (y1, 6))
    write(jnp.where(upper, low + 3, high), (t1, 6), (y1, 7), (y2, 0))


def final_kernel(reach, at_ref, pairs, k3, c3, y3, ez, oz, band, out, parts, sems):
    del band
    k, odd, me = at_ref[0], at_ref[1] == 1, at_ref[3]
    rows = y3.shape[1]
    copies = []

    def write(index, value):
        slot, i = index - k - 1, len(copies)
        parts[i] = value * wanted(pairs, me, slot - reach, reach)
        copies.append(pltpu.make_async_copy(parts.at[i], out.at[:, block(slot, rows)], sems.at[i]))
        copies[-1].start()

    for m in range(PLANE - 1):
        behind = m >= k
        value = jnp.where(behind == odd, ez[:, block(m, rows)], oz[:, block(m, rows)])
        write(jnp.where(behind, m + 1, 4 * PLANE + m), value)
    third = k3[...] + c3[:, :rows] + y3[...]
    write(jnp.where(odd, PLANE, 4 * PLANE - 1), third[:rows].T)
    write(jnp.where(odd, 4 * PLANE - 1, PLANE), third[rows:].T)
    for copy in copies:
        copy.wait()


def call(kernel, outs, scratch, scalars, arrays, flops=1000):
    return pl.pallas_call(
        kernel,
        cost_estimate=pl.CostEstimate(flops=flops, bytes_accessed=1000, transcendentals=0),
        in_specs=[pl.BlockSpec(memory_space=pltpu.SMEM)] * len(scalars)
        + [pl.BlockSpec(memory_space=pltpu.VMEM)] * len(arrays),
        out_specs=[pl.BlockSpec(memory_space=pltpu.VMEM)] * len(outs),
        out_shape=outs,
        scratch_shapes=scratch,
        compiler_params=pltpu.CompilerParams(vmem_limit_bytes=VMEM_BYTES),
    )(*scalars, *arrays)


def after(value, *others):
    return lax.optimization_barrier((value, *others))[0]


def body(count, fitted_slab, pair_list):
    rows, width = fitted_slab.shape
    depth = width // PLANE
    reach = pair_list.shape[1] - 1
    me = lax.axis_index("blk").astype(jnp.int32)
    k = me % PLANE
    odd = (me // PLANE) % 2
    upper = k >= 2
    outer = (k == 0) | (k == 3)
    flip = upper ^ (odd == 1)
    place = jnp.stack([k, odd, flip.astype(jnp.int32), me])
    devices = range(count)

    def xor(value, t):
        return lax.ppermute(value, "blk", [(i, i ^ t) for i in devices])

    def along(value, parity):
        route = []
        for i in devices:
            j = i + (PLANE if i // PLANE % 2 == parity else -PLANE)
            if j in devices:
                route.append((i, j))
        return lax.ppermute(value, "blk", route)

    def both(to_even, to_odd):
        return along(to_even, 0), along(to_odd, 1)

    quarters = fitted_slab.T.reshape(PLANE, depth, rows)

    def quarter(index, *others):
        return lax.dynamic_index_in_dim(after(quarters, *others), index, 0, keepdims=False)

    q1 = quarter(k ^ 1)
    cx = xor(q1, 1)
    q3 = quarter(k ^ 3, q1)
    x3 = xor(q3, 3)
    own = quarter(k, q1)
    near_inner = jnp.where(outer, cx, own)
    e0, o0 = both(near_inner, near_inner)
    x2 = xor(quarter(k ^ 2, cx), 2)

    own_a, cx_a, x3_a, _ = lax.optimization_barrier((own, cx, x3, near_inner))
    near_outer = jnp.where(outer, own_a, cx_a)
    e1, o1 = both(jnp.where(flip, near_outer, x3_a), jnp.where(flip, x3_a, near_outer))

    own_b, cx_b, x3_b, x2_b, _, _ = lax.optimization_barrier((own_a, cx_a, x3_a, x2, e0, o0))
    far_inner = jnp.where(outer, x2_b, x3_b)
    e2, o2 = both(jnp.where(flip, far_inner, x2_b), jnp.where(flip, x2_b, far_inner))

    own_c, cx_c, x3_c, x2_c, _, _ = lax.optimization_barrier((own_b, cx_b, x3_b, x2_b, e1, o1))
    near_outer = jnp.where(outer, own_c, cx_c)
    far_outer = jnp.where(outer, x3_c, x2_c)
    e3, o3 = both(jnp.where(flip, far_outer, near_outer), jnp.where(flip, near_outer, far_outer))

    def f32(*shape):
        return jax.ShapeDtypeStruct(shape, jnp.float32)

    def parts(n):
        return [f32(rows, n * rows), f32(rows, n * rows), f32(2 * rows, n * rows)]

    def core_sum(keep, other, send):
        core = xor(send, 1)
        return keep + core[:rows], other + core[rows:]

    def fenced(function, *operands):
        shapes = jax.eval_shape(function, *operands)

        def never(*_):
            return jax.tree.map(lambda x: jnp.zeros(x.shape, x.dtype), shapes)

        return lax.cond(me >= 0, function, never, *operands)

    mine = (own, x2, cx, x3)

    def first_part(place, *operands):
        return core_sum(*call(first_kernel, parts(9), [], (place,), operands))

    t1, out1 = fenced(first_part, place, *mine, e0, o0, e1, o1)
    y1 = xor(out1, 2)

    def second_part(place, own, x2, cx, x3, *arrived):
        square, tall = (pltpu.VMEM((n * rows, 3 * rows), jnp.float32) for n in (PLANE - 1, PLANE))
        keep, other, send = call(cross_kernel, parts(3), [square, tall], (place,), arrived)
        half, out = core_sum(keep, other, send)
        far = xor(out, 2)
        pack = call(add_kernel, [f32(rows, 3 * rows)], [], (), (half, far), flops=10**11)[0]
        place = after(place, keep)
        return pack, *core_sum(*call(second_kernel, parts(3), [], (place,), (own, x2, cx, x3, *arrived[4:])))

    pack, t2, out2 = fenced(second_part, place, *mine, e0, o0, e1, o1, e2, o2)
    ez, oz = both(pack, pack)
    y2 = xor(out2, 2)

    e3, o3, _, _ = lax.optimization_barrier((e3, o3, pack, y1))
    pair = f32(2 * rows, rows)
    k3, other, send = call(third_kernel, [pair, pair, f32(2 * rows, 2 * rows)], [], (), (*mine, e3, o3))
    c3 = xor(after(send, y2), 1)
    y3 = xor(other + c3[:, rows:], 2)

    whole = f32(rows, (2 * reach + 1) * rows)
    band = call(functools.partial(band_kernel, reach), [whole], [], (place, pair_list), (t1, y1, t2, y2))[0]
    late = (k3, c3, y3, ez, oz)
    return pl.pallas_call(
        functools.partial(final_kernel, reach),
        in_specs=[pl.BlockSpec(memory_space=pltpu.SMEM)] * 2
        + [pl.BlockSpec(memory_space=pltpu.VMEM)] * len(late)
        + [pl.BlockSpec(memory_space=pl.ANY)],
        out_specs=pl.BlockSpec(memory_space=pl.ANY),
        out_shape=whole,
        scratch_shapes=[pltpu.VMEM((PLANE + 1, rows, rows), jnp.float32), pltpu.SemaphoreType.DMA((PLANE + 1,))],
        input_output_aliases={2 + len(late): 0},
        compiler_params=pltpu.CompilerParams(vmem_limit_bytes=VMEM_BYTES),
    )(place, pair_list, *late, band)


def solution(mesh):
    return jax.shard_map(
        functools.partial(body, mesh.shape["blk"]),
        mesh=mesh,
        in_specs=(P("blk", "groups"), P()),
        out_specs=P(("groups", "blk"), None),
        check_vma=False,
    )
```

time: 116 us -> 111 us (0.957)
  other arithmetic: 8.37 us -> 5.99 us
  starting transfers between devices: 35.2 us -> 33.5 us
  waiting for transfers between devices: 40.7 us -> 39 us
    add x5 -> x4, other arithmetic: 3.6 us -> 1.06 us  [the longest x3 1.04 us: core_sum(): return (keep + core[:rows], other + core[rows:])]
    ppermute x11, waiting for transfers between devices: 38.3 us -> 36.5 us  [xor(): return lax.ppermute(value, 'blk', [(i, i ^ t) for i in devices])]
    pallas_call x5 -> x7, Pallas kernels: 26 us -> 26.7 us  [the longest x6 25.3 us: call(): pl.pallas_call(kernel, cost_estimate=pl.CostEstimate(flops=flops, bytes_a...]
  transfers between devices with their start and end apart: 21 -> 21, of which waited for: 9 -> 7; matrix products, arithmetic and copies ran while one was open for 10% -> 8% of each run, Pallas kernels for 17% -> 23%
where the time goes in v3:
time: 111 us
  waiting for transfers between devices  39 us (35%)
  starting transfers between devices  33.5 us (30%)
  Pallas kernels  26.7 us (24%)
  other arithmetic  5.99 us (5%)
  local copies, waits for them, and re-layouts  5.44 us (5%)
    ppermute x11, waiting for transfers between devices, xor(): return lax.ppermute(value, 'blk', [(i, i ^ t) for i in devices])  36.5 us
    pallas_call x6, Pallas kernels, call(): pl.pallas_call(kernel, cost_estimate=pl.CostEstimate(flops=flops, bytes_a...  25.3 us
    ppermute x10, starting transfers between devices, along(): return lax.ppermute(value, 'blk', route)  23.6 us
    ppermute x11, starting transfers between devices, xor(): return lax.ppermute(value, 'blk', [(i, i ^ t) for i in devices])  9.86 us
    squeeze x3, local copies, waits for them, and re-layouts, quarter(): lax.dynamic_index_in_dim(after(quarters, *others), index, 0, keepdims=False)  4.64 us
    ppermute x10, waiting for transfers between devices, along(): return lax.ppermute(value, 'blk', route)  2.49 us
  transfers between devices with their start and end apart: 21, of which 7 were waited for; matrix products, arithmetic and copies ran while one was open for 8% of the time, Pallas kernels for 23%

profile of v3, /device:TPU:0, one launch (start us, length us, event | category | flops | bytes accessed | tf_op | source)
XLA Modules:
  0.0 110.8 jit_solution(16340774581860132035)
XLA Ops:
  0.0 2.2 %dynamic-slice_bitcast_fusion.3 = f32[1800,128]{1,0:T(8,128)} fusion(f32[4,1800,128]{2,1,0:T(8,128)} %bitcast.16, s32[]{:T(128)S(6)} %select_n.81), kind=kLoop, calls=%fused_computation.11 | loop fusion | bytes 1843204 | tf_op jit(solution)/shard_map/jit(dynamic_index_in_dim)/squeeze | solution.py:220
  2.6 1.2 %dynamic-slice_bitcast_fusion = f32[1800,128]{1,0:T(8,128)S(1)} fusion(f32[4,1800,128]{2,1,0:T(8,128)} %bitcast.17, s32[]{:T(128)S(6)} %select_n.84), kind=kLoop, calls=%fused_computation.8 | loop fusion | bytes 1843204 | tf_op jit(solution)/shard_map/jit(dynamic_index_in_dim)/squeeze | solution.py:220
  3.9 2.7 %collective-permute-start.6 = (f32[1800,128]{1,0:T(8,128)S(1)}, f32[1800,128]{1,0:T(8,128)S(1)}, u32[]{:S(2)}, u32[]{:S(2)}) collective-permute-start(f32[1800,128]{1,0:T(8,128)S(1)} %dynamic-slice_bitcast_fusion), channel_id=1, source_target_pairs={{0,3},{1,2},{2,1},{3,0},{4,7},{5,6},{6,5},{7,4},{8,11},{9,10},{10,... | collective-permute-start | bytes 2764808 | tf_op jit(solution)/shard_map/ppermute | solution.py:204
  6.6 1.6 %broadcast_select_fusion.3 = (f32[1800,128]{1,0:T(8,128)S(1)}, f32[1800,128]{1,0:T(8,128)S(1)}) fusion(f32[1800,128]{1,0:T(8,128)S(1)} %collective-permute-done.4.cx, pred[]{:T(512)S(6)} %or.3, f32[4,1800,128]{2,1,0:T(8,128)} %bitcast.18, s32[]{:T(128)S(6)} %select_n.82), kind=kLoop, calls=%fused_computation.15 | loop fusion | flops 230400 | bytes 3686405 | tf_op jit(solution)/shard_map/jit(_where)/select_n | solution.py:227
  8.2 1.6 %collective-permute-start.8 = (f32[1800,128]{1,0:T(8,128)S(1)}, f32[1800,128]{1,0:T(8,128)}, u32[]{:S(2)}, u32[]{:S(2)}) collective-permute-start(f32[1800,128]{1,0:T(8,128)S(1)} %get-tuple-element.123), channel_id=1, source_target_pairs={{4,8},{5,9},{6,10},{7,11},{8,4},{9,5},{10,6},{11,7},{20,24},{21,25... | collective-permute-start | bytes 2764808 | tf_op jit(solution)/shard_map/ppermute | solution.py:212
  9.8 3.5 %collective-permute-start.7 = (f32[1800,128]{1,0:T(8,128)S(1)}, f32[1800,128]{1,0:T(8,128)}, u32[]{:S(2)}, u32[]{:S(2)}) collective-permute-start(f32[1800,128]{1,0:T(8,128)S(1)} %get-tuple-element.123), channel_id=1, source_target_pairs={{0,4},{1,5},{2,6},{3,7},{4,0},{5,1},{6,2},{7,3},{8,12},{9,13},{10,... | collective-permute-start | bytes 2764808 | tf_op jit(solution)/shard_map/ppermute | solution.py:212
  13.3 1.2 %dynamic-slice_bitcast_fusion.1 = f32[1800,128]{1,0:T(8,128)S(1)} fusion(f32[4,1800,128]{2,1,0:T(8,128)} %bitcast.19, s32[]{:T(128)S(6)} %select_n.83), kind=kLoop, calls=%fused_computation.9 | loop fusion | bytes 1843204 | tf_op jit(solution)/shard_map/jit(dynamic_index_in_dim)/squeeze | solution.py:220
  14.6 1.3 %collective-permute-start.5 = (f32[1800,128]{1,0:T(8,128)S(1)}, f32[1800,128]{1,0:T(8,128)S(1)}, u32[]{:S(2)}, u32[]{:S(2)}) collective-permute-start(f32[1800,128]{1,0:T(8,128)S(1)} %dynamic-slice_bitcast_fusion.1), channel_id=1, source_target_pairs={{0,2},{1,3},{2,0},{3,1},{4,6},{5,7},{6,4},{7,5},{8,10},{9,11},{10,... | collective-permute-start | bytes 2764808 | tf_op jit(solution)/shard_map/ppermute | solution.py:204
  15.9 11.4 %collective-permute-done.6.x3 = f32[1800,128]{1,0:T(8,128)S(1)} collective-permute-done((f32[1800,128]{1,0:T(8,128)S(1)}, f32[1800,128]{1,0:T(8,128)S(1)}, u32[]{:S(2)}, u32[]{:S(2)}) %collective-permute-start.6) | collective-permute-done | bytes 921632 | tf_op jit(solution)/shard_map/ppermute | solution.py:204
  27.6 1.7 %collective-permute-start.10 = (f32[1800,128]{1,0:T(8,128)S(1)}, f32[1800,128]{1,0:T(8,128)}, u32[]{:S(2)}, u32[]{:S(2)}) collective-permute-start(f32[1800,128]{1,0:T(8,128)S(1)} %get-tuple-element.133), channel_id=1, source_target_pairs={{4,8},{5,9},{6,10},{7,11},{8,4},{9,5},{10,6},{11,7},{20,24},{21,25... | collective-permute-start | bytes 2764808 | tf_op jit(solution)/shard_map/ppermute | solution.py:212
  29.3 3.4 %collective-permute-start.9 = (f32[1800,128]{1,0:T(8,128)S(1)}, f32[1800,128]{1,0:T(8,128)}, u32[]{:S(2)}, u32[]{:S(2)}) collective-permute-start(f32[1800,128]{1,0:T(8,128)S(1)} %get-tuple-element.134), channel_id=1, source_target_pairs={{0,4},{1,5},{2,6},{3,7},{4,0},{5,1},{6,2},{7,3},{8,12},{9,13},{10,... | collective-permute-start | bytes 2764808 | tf_op jit(solution)/shard_map/ppermute | solution.py:212
  32.7 14.6 %collective-permute-done.5.x2 = f32[1800,128]{1,0:T(8,128)S(1)} collective-permute-done((f32[1800,128]{1,0:T(8,128)S(1)}, f32[1800,128]{1,0:T(8,128)S(1)}, u32[]{:S(2)}, u32[]{:S(2)}) %collective-permute-start.5) | collective-permute-done | bytes 921632 | tf_op jit(solution)/shard_map/ppermute | solution.py:204
  47.3 1.5 %select_select_fusion = (f32[1800,128]{1,0:T(8,128)}, f32[1800,128]{1,0:T(8,128)}) fusion(f32[1800,128]{1,0:T(8,128)S(1)} %collective-permute-done.5.x2, f32[1800,128]{1,0:T(8,128)S(1)} %collective-permute-done.6.x3, pred[]{:T(512)S(6)} %or.3, pred[]{:T(512)S(6)} %xor.12), kind=kLoop, calls=%fused_computation.6 | loop fusion | flops 691200 | bytes 3686402 | tf_op jit(solution)/shard_map/jit(_where)/select_n | solution.py:237
  48.8 1.6 %collective-permute-start.14 = (f32[1800,128]{1,0:T(8,128)}, f32[1800,128]{1,0:T(8,128)}, u32[]{:S(2)}, u32[]{:S(2)}) collective-permute-start(f32[1800,128]{1,0:T(8,128)} %get-tuple-element.135), channel_id=1, source_target_pairs={{4,8},{5,9},{6,10},{7,11},{8,4},{9,5},{10,6},{11,7},{20,24},{21,25... | collective-permute-start | bytes 2764808 | tf_op jit(solution)/shard_map/ppermute | solution.py:212
  50.4 3.6 %collective-permute-start.13 = (f32[1800,128]{1,0:T(8,128)}, f32[1800,128]{1,0:T(8,128)}, u32[]{:S(2)}, u32[]{:S(2)}) collective-permute-start(f32[1800,128]{1,0:T(8,128)} %get-tuple-element.136), channel_id=1, source_target_pairs={{0,4},{1,5},{2,6},{3,7},{4,0},{5,1},{6,2},{7,3},{8,12},{9,13},{10,... | collective-permute-start | bytes 2764808 | tf_op jit(solution)/shard_map/ppermute | solution.py:212
  54.0 1.5 %broadcast_select_fusion.4 = (f32[1800,128]{1,0:T(8,128)}, f32[1800,128]{1,0:T(8,128)}) fusion(pred[]{:T(512)S(6)} %xor.12, f32[1800,128]{1,0:T(8,128)S(1)} %collective-permute-done.6.x3, f32[1800,128]{1,0:T(8,128)S(1)} %collective-permute-done.5.x2, pred[]{:T(512)S(6)} %or.3, f32[1800,128]{1,0:T(8,128)S(1)} %get-tuple-element.110.own, ...), kind=kLoop, calls=%fused_computation.16 | loop fusion | flops 921600 | bytes 5529602 | tf_op jit(solution)/shard_map/jit(_where)/select_n | solution.py:242
  56.3 3.8 %collective-permute-start.11 = (f32[1800,128]{1,0:T(8,128)}, f32[1800,128]{1,0:T(8,128)S(1)}, u32[]{:S(2)}, u32[]{:S(2)}) collective-permute-start(f32[1800,128]{1,0:T(8,128)} %get-tuple-element.132), channel_id=1, source_target_pairs={{0,4},{1,5},{2,6},{3,7},{4,0},{5,1},{6,2},{7,3},{8,12},{9,13},{10,... | collective-permute-start | bytes 2764808 | tf_op jit(solution)/shard_map/ppermute | solution.py:212
  60.1 13.4 %conditional.3 = (f32[128,1152]{1,0:T(8,128)S(1)}, f32[128,1152]{1,0:T(8,128)}) conditional(s32[]{:T(128)} %convert_element_type.2, () %tuple.36, (s32[4]{0:T(128)S(1)}, f32[1800,128]{1,0:T(8,128)}, f32[1800,128]{1,0:T(8,128)}, f32[1800,128]{1,0:T(8,128)S(1)}, f32[1800,128]{1,0:T(8,128)}, /*index=5*/f32[1800,128]{1,0:T(8,128)}, ...), branch_computations={%region_2.3_spmd, %region_3.4_spmd} | conditional | flops 295912 | bytes 8258592 | solution.py:260
  60.1 9.6 %branch_1_fun.7 = (f32[128,1152]{1,0:T(8,128)S(1)}, f32[128,1152]{1,0:T(8,128)S(1)}, f32[256,1152]{1,0:T(8,128)S(1)}) custom-call(s32[4]{0:T(128)S(1)} %get-tuple-element.63.at_ref, f32[1800,128]{1,0:T(8,128)} %get-tuple-element.64.own, f32[1800,128]{1,0:T(8,128)} %get-tuple-element.65.x2, f32[1800,128]{1,0:T(8,128)S(1)} %get-tuple-element.66.cx, ...), custom_call_target="tpu_custom_call" | custom-call | flops 1000 | bytes 1000 | tf_op jit(solution)/shard_map/cond/branch_1_fun/pallas_call | solution.py:174
  69.8 2.8 %collective-permute-done.3 = f32[256,1152]{1,0:T(8,128)S(1)} collective-permute-done((f32[256,1152]{1,0:T(8,128)S(1)}, f32[256,1152]{1,0:T(8,128)S(1)}, u32[]{:S(2)}, u32[]{:S(2)}) %collective-permute-start.3) | collective-permute-done | bytes 1179680 | tf_op jit(solution)/shard_map/cond/branch_1_fun/ppermute | solution.py:204
  75.7 18.4 %conditional.2 = (f32[128,384]{1,0:T(8,128)}, f32[128,384]{1,0:T(8,128)S(1)}, f32[128,384]{1,0:T(8,128)S(1)}) conditional(s32[]{:T(128)} %convert_element_type.2, () %tuple.34, (s32[4]{0:T(128)S(1)}, f32[1800,128]{1,0:T(8,128)}, f32[1800,128]{1,0:T(8,128)}, f32[1800,128]{1,0:T(8,128)}, f32[1800,128]{1,0:T(8,128)}, /*index=5*/f32[1800,128]{1,0:T(8,128)}, ...), branch_computations={%region_0.1_spmd, %region_1.2_spmd} | conditional | flops 100000194560 | bytes 17353884 | solution.py:260
  75.7 5.5 %branch_1_fun.4 = (f32[128,384]{1,0:T(8,128)S(1)}, f32[128,384]{1,0:T(8,128)S(1)}, f32[256,384]{1,0:T(8,128)S(1)}) custom-call(s32[4]{0:T(128)S(1)} %get-tuple-element.55.at_ref, f32[1800,128]{1,0:T(8,128)} %get-tuple-element.46.e0, f32[1800,128]{1,0:T(8,128)} %get-tuple-element.47.o0, f32[1800,128]{1,0:T(8,128)} %get-tuple-element.48.e1, ...), custom_call_target="tpu_custom_call" | custom-call | flops 1000 | bytes 1000 | tf_op jit(solution)/shard_map/cond/branch_1_fun/pallas_call | solution.py:174
  81.4 3.3 %branch_1_fun.6 = (f32[128,384]{1,0:T(8,128)S(1)}, f32[128,384]{1,0:T(8,128)S(1)}, f32[256,384]{1,0:T(8,128)S(1)}) custom-call(s32[4]{0:T(128)S(1)} %get-tuple-element.55.at_ref, f32[1800,128]{1,0:T(8,128)S(1)} %copy-done.4, f32[1800,128]{1,0:T(8,128)S(1)} %copy-done.6, f32[1800,128]{1,0:T(8,128)S(1)} %get-tuple-element.58.cx, f32[1800,128]{1,0:T(8,128)S(1)} %copy-done.2, ...), custom_call_target="tpu_custom_call" | custom-call | flops 1000 | bytes 1000 | tf_op jit(solution)/shard_map/cond/branch_1_fun/pallas_call | solution.py:174
  85.3 1.6 %collective-permute-start.1 = (f32[128,384]{1,0:T(8,128)S(1)}, f32[128,384]{1,0:T(8,128)S(1)}, u32[]{:S(2)}, u32[]{:S(2)}) collective-permute-start(f32[128,384]{1,0:T(8,128)S(1)} %get-tuple-element.127), channel_id=1, source_target_pairs={{0,2},{1,3},{2,0},{3,1},{4,6},{5,7},{6,4},{7,5},{8,10},{9,11},{10,... | collective-permute-start | bytes 589832 | tf_op jit(solution)/shard_map/cond/branch_1_fun/ppermute | solution.py:204
  86.9 6.4 %collective-permute-done.1.b = f32[128,384]{1,0:T(8,128)S(1)} collective-permute-done((f32[128,384]{1,0:T(8,128)S(1)}, f32[128,384]{1,0:T(8,128)S(1)}, u32[]{:S(2)}, u32[]{:S(2)}) %collective-permute-start.1) | collective-permute-done | bytes 196640 | tf_op jit(solution)/shard_map/cond/branch_1_fun/ppermute | solution.py:204
  95.0 3.9 %shard_map.28 = (f32[256,128]{1,0:T(8,128)S(1)}, f32[256,128]{1,0:T(8,128)S(1)}, f32[256,256]{1,0:T(8,128)S(1)}) custom-call(f32[1800,128]{1,0:T(8,128)} %copy-done.3, f32[1800,128]{1,0:T(8,128)} %copy-done.5, f32[1800,128]{1,0:T(8,128)} %copy-done, f32[1800,128]{1,0:T(8,128)} %copy-done.1, f32[1800,128]{1,0:T(8,128)S(1)} %collective-permute-done.11.e3, ...), custom_call_target="tpu_custom_call" | custom-call | flops 1000 | bytes 1000 | tf_op jit(solution)/shard_map/pallas_call | solution.py:174
  98.9 1.2 %collective-permute-done.16.y2 = f32[128,384]{1,0:T(8,128)S(1)} collective-permute-done((f32[128,384]{1,0:T(8,128)S(1)}, f32[128,384]{1,0:T(8,128)S(1)}, u32[]{:S(2)}, u32[]{:S(2)}) %collective-permute-start.16) | collective-permute-done | bytes 196640 | tf_op jit(solution)/shard_map/ppermute | solution.py:204
  100.8 3.0 %collective-permute-start.19 = (f32[128,384]{1,0:T(8,128)}, f32[128,384]{1,0:T(8,128)S(1)}, u32[]{:S(2)}, u32[]{:S(2)}) collective-permute-start(f32[128,384]{1,0:T(8,128)} %get-tuple-element.112), channel_id=1, source_target_pairs={{0,4},{1,5},{2,6},{3,7},{4,0},{5,1},{6,2},{7,3},{8,12},{9,13},{10,... | collective-permute-start | bytes 589832 | tf_op jit(solution)/shard_map/ppermute | solution.py:212
  103.9 1.1 %collective-permute-start.18 = (f32[256,128]{1,0:T(8,128)S(1)}, f32[256,128]{1,0:T(8,128)S(1)}, u32[]{:S(2)}, u32[]{:S(2)}) collective-permute-start(f32[256,128]{1,0:T(8,128)S(1)} %slice_add_fusion.6), channel_id=1, source_target_pairs={{0,2},{1,3},{2,0},{3,1},{4,6},{5,7},{6,4},{7,5},{8,10},{9,11},{10,... | collective-permute-start | bytes 393224 | tf_op jit(solution)/shard_map/ppermute | solution.py:204
  105.7 2.2 %shard_map.29.band = f32[128,1920]{1,0:T(8,128)} custom-call(s32[4]{0:T(128)S(1)} %pad_add_fusion.at_ref, s32[16,8]{1,0:T(8,128)S(1)} %copy.5.pairs, f32[128,1152]{1,0:T(8,128)} %copy-done.7, f32[128,1152]{1,0:T(8,128)S(1)} %collective-permute-done.15.y1, f32[128,384]{1,0:T(8,128)S(1)} %get-tuple-element.122.t2, f32[128,384]{1,0:T(8,128)S(1)} %collective-permute-done.16.y2), custom_call_target="tpu_custom_call" | custom-call | flops 1000 | bytes 1000 | tf_op jit(solution)/shard_map/pallas_call | solution.py:174
  108.0 1.3 %collective-permute-done.19.ez = f32[128,384]{1,0:T(8,128)S(1)} collective-permute-done((f32[128,384]{1,0:T(8,128)}, f32[128,384]{1,0:T(8,128)S(1)}, u32[]{:S(2)}, u32[]{:S(2)}) %collective-permute-start.19) | collective-permute-done | bytes 196640 | tf_op jit(solution)/shard_map/ppermute | solution.py:212
  109.3 1.5 %shard_map.30 = f32[128,1920]{1,0:T(8,128)} custom-call(s32[4]{0:T(128)S(1)} %pad_add_fusion.at_ref, s32[16,8]{1,0:T(8,128)S(1)} %copy.5.pairs, f32[256,128]{1,0:T(8,128)S(1)} %get-tuple-element.116.k3, f32[256,256]{1,0:T(8,128)S(1)} %collective-permute-done.17.c3, f32[256,128]{1,0:T(8,128)S(1)} %collective-permute-done.18.y3, ...), custom_call_target="tpu_custom_call", output_to_operand_aliasing={{}: (7, {})} | custom-call | tf_op jit(solution)/shard_map/pallas_call | solution.py:292
  (48 shorter events, 8.5 us)
Async XLA Ops:
  2.2 4.4 %collective-permute-start.4 = (f32[1800,128]{1,0:T(8,128)}, f32[1800,128]{1,0:T(8,128)S(1)}, u32[]{:S(2)}, u32[]{:S(2)}) collective-permute-start(f32[1800,128]{1,0:T(8,128)} %dynamic-slice_bitcast_fusion.3), channel_id=1, source_target_pairs={{0,1},{1,0},{2,3},{3,2},{4,5},{5,4},{6,7},{7,6},{8,9},{9,8},{10,11... | collective-permute-start | bytes 2764808 | tf_op jit(solution)/shard_map/ppermute | solution.py:204
  3.9 23.5 %collective-permute-start.6 = (f32[1800,128]{1,0:T(8,128)S(1)}, f32[1800,128]{1,0:T(8,128)S(1)}, u32[]{:S(2)}, u32[]{:S(2)}) collective-permute-start(f32[1800,128]{1,0:T(8,128)S(1)} %dynamic-slice_bitcast_fusion), channel_id=1, source_target_pairs={{0,3},{1,2},{2,1},{3,0},{4,7},{5,6},{6,5},{7,4},{8,11},{9,10},{10,... | collective-permute-start | bytes 2764808 | tf_op jit(solution)/shard_map/ppermute | solution.py:204
  6.6 69.1 %copy-start = (f32[1800,128]{1,0:T(8,128)}, f32[1800,128]{1,0:T(8,128)S(1)}, u32[]{:S(2)}) copy-start(f32[1800,128]{1,0:T(8,128)S(1)} %collective-permute-done.4.cx) | copy-start | bytes 2764804
  8.2 45.8 %copy-start.3 = (f32[1800,128]{1,0:T(8,128)}, f32[1800,128]{1,0:T(8,128)S(1)}, u32[]{:S(2)}) copy-start(f32[1800,128]{1,0:T(8,128)S(1)} %get-tuple-element.110.own) | copy-start | bytes 2764804
  8.2 39.1 %collective-permute-start.8 = (f32[1800,128]{1,0:T(8,128)S(1)}, f32[1800,128]{1,0:T(8,128)}, u32[]{:S(2)}, u32[]{:S(2)}) collective-permute-start(f32[1800,128]{1,0:T(8,128)S(1)} %get-tuple-element.123), channel_id=1, source_target_pairs={{4,8},{5,9},{6,10},{7,11},{8,4},{9,5},{10,6},{11,7},{20,24},{21,25... | collective-permute-start | bytes 2764808 | tf_op jit(solution)/shard_map/ppermute | solution.py:212
  9.8 37.5 %collective-permute-start.7 = (f32[1800,128]{1,0:T(8,128)S(1)}, f32[1800,128]{1,0:T(8,128)}, u32[]{:S(2)}, u32[]{:S(2)}) collective-permute-start(f32[1800,128]{1,0:T(8,128)S(1)} %get-tuple-element.123), channel_id=1, source_target_pairs={{0,4},{1,5},{2,6},{3,7},{4,0},{5,1},{6,2},{7,3},{8,12},{9,13},{10,... | collective-permute-start | bytes 2764808 | tf_op jit(solution)/shard_map/ppermute | solution.py:212
  14.6 32.7 %collective-permute-start.5 = (f32[1800,128]{1,0:T(8,128)S(1)}, f32[1800,128]{1,0:T(8,128)S(1)}, u32[]{:S(2)}, u32[]{:S(2)}) collective-permute-start(f32[1800,128]{1,0:T(8,128)S(1)} %dynamic-slice_bitcast_fusion.1), channel_id=1, source_target_pairs={{0,2},{1,3},{2,0},{3,1},{4,6},{5,7},{6,4},{7,5},{8,10},{9,11},{10,... | collective-permute-start | bytes 2764808 | tf_op jit(solution)/shard_map/ppermute | solution.py:204
  27.4 26.6 %copy-start.1 = (f32[1800,128]{1,0:T(8,128)}, f32[1800,128]{1,0:T(8,128)S(1)}, u32[]{:S(2)}) copy-start(f32[1800,128]{1,0:T(8,128)S(1)} %collective-permute-done.6.x3) | copy-start | bytes 2764804
  27.6 26.4 %collective-permute-start.10 = (f32[1800,128]{1,0:T(8,128)S(1)}, f32[1800,128]{1,0:T(8,128)}, u32[]{:S(2)}, u32[]{:S(2)}) collective-permute-start(f32[1800,128]{1,0:T(8,128)S(1)} %get-tuple-element.133), channel_id=1, source_target_pairs={{4,8},{5,9},{6,10},{7,11},{8,4},{9,5},{10,6},{11,7},{20,24},{21,25... | collective-permute-start | bytes 2764808 | tf_op jit(solution)/shard_map/ppermute | solution.py:212
  29.3 24.7 %collective-permute-start.9 = (f32[1800,128]{1,0:T(8,128)S(1)}, f32[1800,128]{1,0:T(8,128)}, u32[]{:S(2)}, u32[]{:S(2)}) collective-permute-start(f32[1800,128]{1,0:T(8,128)S(1)} %get-tuple-element.134), channel_id=1, source_target_pairs={{0,4},{1,5},{2,6},{3,7},{4,0},{5,1},{6,2},{7,3},{8,12},{9,13},{10,... | collective-permute-start | bytes 2764808 | tf_op jit(solution)/shard_map/ppermute | solution.py:212
  47.3 8.2 %copy-start.5 = (f32[1800,128]{1,0:T(8,128)}, f32[1800,128]{1,0:T(8,128)S(1)}, u32[]{:S(2)}) copy-start(f32[1800,128]{1,0:T(8,128)S(1)} %collective-permute-done.5.x2) | copy-start | bytes 2764804
  48.8 25.8 %collective-permute-start.14 = (f32[1800,128]{1,0:T(8,128)}, f32[1800,128]{1,0:T(8,128)}, u32[]{:S(2)}, u32[]{:S(2)}) collective-permute-start(f32[1800,128]{1,0:T(8,128)} %get-tuple-element.135), channel_id=1, source_target_pairs={{4,8},{5,9},{6,10},{7,11},{8,4},{9,5},{10,6},{11,7},{20,24},{21,25... | collective-permute-start | bytes 2764808 | tf_op jit(solution)/shard_map/ppermute | solution.py:212
  50.4 25.3 %collective-permute-start.13 = (f32[1800,128]{1,0:T(8,128)}, f32[1800,128]{1,0:T(8,128)}, u32[]{:S(2)}, u32[]{:S(2)}) collective-permute-start(f32[1800,128]{1,0:T(8,128)} %get-tuple-element.136), channel_id=1, source_target_pairs={{0,4},{1,5},{2,6},{3,7},{4,0},{5,1},{6,2},{7,3},{8,12},{9,13},{10,... | collective-permute-start | bytes 2764808 | tf_op jit(solution)/shard_map/ppermute | solution.py:212
  55.6 39.5 %collective-permute-start.12 = (f32[1800,128]{1,0:T(8,128)}, f32[1800,128]{1,0:T(8,128)S(1)}, u32[]{:S(2)}, u32[]{:S(2)}) collective-permute-start(f32[1800,128]{1,0:T(8,128)} %get-tuple-element.131), channel_id=1, source_target_pairs={{4,8},{5,9},{6,10},{7,11},{8,4},{9,5},{10,6},{11,7},{20,24},{21,25... | collective-permute-start | bytes 2764808 | tf_op jit(solution)/shard_map/ppermute | solution.py:212
  56.3 38.8 %collective-permute-start.11 = (f32[1800,128]{1,0:T(8,128)}, f32[1800,128]{1,0:T(8,128)S(1)}, u32[]{:S(2)}, u32[]{:S(2)}) collective-permute-start(f32[1800,128]{1,0:T(8,128)} %get-tuple-element.132), channel_id=1, source_target_pairs={{0,4},{1,5},{2,6},{3,7},{4,0},{5,1},{6,2},{7,3},{8,12},{9,13},{10,... | collective-permute-start | bytes 2764808 | tf_op jit(solution)/shard_map/ppermute | solution.py:212
  69.7 2.9 %collective-permute-start.3 = (f32[256,1152]{1,0:T(8,128)S(1)}, f32[256,1152]{1,0:T(8,128)S(1)}, u32[]{:S(2)}, u32[]{:S(2)}) collective-permute-start(f32[256,1152]{1,0:T(8,128)S(1)} %get-tuple-element.73), channel_id=1, source_target_pairs={{0,1},{1,0},{2,3},{3,2},{4,5},{5,4},{6,7},{7,6},{8,9},{9,8},{10,11... | collective-permute-start | bytes 3538952 | tf_op jit(solution)/shard_map/cond/branch_1_fun/ppermute | solution.py:204
  73.5 2.1 %copy-start.7 = (f32[128,1152]{1,0:T(8,128)}, f32[128,1152]{1,0:T(8,128)S(1)}, u32[]{:S(2)}) copy-start(f32[128,1152]{1,0:T(8,128)S(1)} %get-tuple-element.121.t1) | copy-start | bytes 1769476
  73.5 21.5 %collective-permute-start.15 = (f32[128,1152]{1,0:T(8,128)}, f32[128,1152]{1,0:T(8,128)S(1)}, u32[]{:S(2)}, u32[]{:S(2)}) collective-permute-start(f32[128,1152]{1,0:T(8,128)} %get-tuple-element.113), channel_id=1, source_target_pairs={{0,2},{1,3},{2,0},{3,1},{4,6},{5,7},{6,4},{7,5},{8,10},{9,11},{10,... | collective-permute-start | bytes 1769480 | tf_op jit(solution)/shard_map/ppermute | solution.py:204
  75.7 5.7 %copy-start.2 = (f32[1800,128]{1,0:T(8,128)S(1)}, f32[1800,128]{1,0:T(8,128)}, u32[]{:S(2)}) copy-start(f32[1800,128]{1,0:T(8,128)} %get-tuple-element.59.x3) | copy-start | bytes 2764804 | tf_op jit(solution)/shard_map/cond
  75.7 5.7 %copy-start.4 = (f32[1800,128]{1,0:T(8,128)S(1)}, f32[1800,128]{1,0:T(8,128)}, u32[]{:S(2)}) copy-start(f32[1800,128]{1,0:T(8,128)} %get-tuple-element.56.own) | copy-start | bytes 2764804 | tf_op jit(solution)/shard_map/cond
  75.7 5.7 %copy-start.6 = (f32[1800,128]{1,0:T(8,128)S(1)}, f32[1800,128]{1,0:T(8,128)}, u32[]{:S(2)}) copy-start(f32[1800,128]{1,0:T(8,128)} %get-tuple-element.57.x2) | copy-start | bytes 2764804 | tf_op jit(solution)/shard_map/cond
  81.3 4.0 %collective-permute-start = (f32[256,384]{1,0:T(8,128)S(1)}, f32[256,384]{1,0:T(8,128)S(1)}, u32[]{:S(2)}, u32[]{:S(2)}) collective-permute-start(f32[256,384]{1,0:T(8,128)S(1)} %get-tuple-element.53), channel_id=1, source_target_pairs={{0,1},{1,0},{2,3},{3,2},{4,5},{5,4},{6,7},{7,6},{8,9},{9,8},{10,11... | collective-permute-start | bytes 1179656 | tf_op jit(solution)/shard_map/cond/branch_1_fun/ppermute | solution.py:204
  84.7 2.2 %collective-permute-start.2 = (f32[256,384]{1,0:T(8,128)S(1)}, f32[256,384]{1,0:T(8,128)S(1)}, u32[]{:S(2)}, u32[]{:S(2)}) collective-permute-start(f32[256,384]{1,0:T(8,128)S(1)} %get-tuple-element.61), channel_id=1, source_target_pairs={{0,1},{1,0},{2,3},{3,2},{4,5},{5,4},{6,7},{7,6},{8,9},{9,8},{10,11... | collective-permute-start | bytes 1179656 | tf_op jit(solution)/shard_map/cond/branch_1_fun/ppermute | solution.py:204
  85.3 8.0 %collective-permute-start.1 = (f32[128,384]{1,0:T(8,128)S(1)}, f32[128,384]{1,0:T(8,128)S(1)}, u32[]{:S(2)}, u32[]{:S(2)}) collective-permute-start(f32[128,384]{1,0:T(8,128)S(1)} %get-tuple-element.127), channel_id=1, source_target_pairs={{0,2},{1,3},{2,0},{3,1},{4,6},{5,7},{6,4},{7,5},{8,10},{9,11},{10,... | collective-permute-start | bytes 589832 | tf_op jit(solution)/shard_map/cond/branch_1_fun/ppermute | solution.py:204
  94.0 6.1 %collective-permute-start.16 = (f32[128,384]{1,0:T(8,128)S(1)}, f32[128,384]{1,0:T(8,128)S(1)}, u32[]{:S(2)}, u32[]{:S(2)}) collective-permute-start(f32[128,384]{1,0:T(8,128)S(1)} %get-tuple-element.118), channel_id=1, source_target_pairs={{0,2},{1,3},{2,0},{3,1},{4,6},{5,7},{6,4},{7,5},{8,10},{9,11},{10,... | collective-permute-start | bytes 589832 | tf_op jit(solution)/shard_map/ppermute | solution.py:204
  100.2 3.7 %collective-permute-start.17 = (f32[256,256]{1,0:T(8,128)S(1)}, f32[256,256]{1,0:T(8,128)S(1)}, u32[]{:S(2)}, u32[]{:S(2)}) collective-permute-start(f32[256,256]{1,0:T(8,128)S(1)} %get-tuple-element.119), channel_id=1, source_target_pairs={{0,1},{1,0},{2,3},{3,2},{4,5},{5,4},{6,7},{7,6},{8,9},{9,8},{10,11... | collective-permute-start | bytes 786440 | tf_op jit(solution)/shard_map/ppermute | solution.py:204
  100.2 7.8 %collective-permute-start.20 = (f32[128,384]{1,0:T(8,128)}, f32[128,384]{1,0:T(8,128)S(1)}, u32[]{:S(2)}, u32[]{:S(2)}) collective-permute-start(f32[128,384]{1,0:T(8,128)} %get-tuple-element.112), channel_id=1, source_target_pairs={{4,8},{5,9},{6,10},{7,11},{8,4},{9,5},{10,6},{11,7},{20,24},{21,25... | collective-permute-start | bytes 589832 | tf_op jit(solution)/shard_map/ppermute | solution.py:212
  100.8 8.5 %collective-permute-start.19 = (f32[128,384]{1,0:T(8,128)}, f32[128,384]{1,0:T(8,128)S(1)}, u32[]{:S(2)}, u32[]{:S(2)}) collective-permute-start(f32[128,384]{1,0:T(8,128)} %get-tuple-element.112), channel_id=1, source_target_pairs={{0,4},{1,5},{2,6},{3,7},{4,0},{5,1},{6,2},{7,3},{8,12},{9,13},{10,... | collective-permute-start | bytes 589832 | tf_op jit(solution)/shard_map/ppermute | solution.py:212
  103.9 5.5 %collective-permute-start.18 = (f32[256,128]{1,0:T(8,128)S(1)}, f32[256,128]{1,0:T(8,128)S(1)}, u32[]{:S(2)}, u32[]{:S(2)}) collective-permute-start(f32[256,128]{1,0:T(8,128)S(1)} %slice_add_fusion.6), channel_id=1, source_target_pairs={{0,2},{1,3},{2,0},{3,1},{4,6},{5,7},{6,4},{7,5},{8,10},{9,11},{10,... | collective-permute-start | bytes 393224 | tf_op jit(solution)/shard_map/ppermute | solution.py:204

commit v4 on v3

--- a/solution.py
+++ b/solution.py
@@ -8,7 +8,7 @@
 from jax.sharding import PartitionSpec as P
 
 PLANE = 4
-VMEM_BYTES = 44 * 2**20
+VMEM_BYTES = 22 * 2**20
 
 
 def halves(value):
@@ -64,6 +64,10 @@
     even = jnp.where(flip, first, 6)
     place_columns(out, keep, other, send, (k, k ^ 2, k ^ 1, k ^ 3, 4, 5, even, 6 + first - even))
     clear_column(keep, other, send, 15 - first)
+
+
+def copy_kernel(a, out):
+    out[...] = a[...]
 
 
 def add_kernel(a, b, out):
@@ -95,7 +99,7 @@
     spread(packs[...], keep, other, send)
 
 
-def second_kernel(at_ref, own, x2, cx, x3, e2, o2, keep, other, send):
+def second_kernel(at_ref, own, x2, cx, x3, e2, o2, early_keep, early_other, keep, other, send):
     k, flip = at_ref[0], at_ref[2] == 1
     mine = side_by_side(own[...], x2[...], cx[...], x3[...])
     out = product(mine, side_by_side(e2[...], o2[...]))
@@ -103,15 +107,21 @@
     even = jnp.where(flip, last, 2)
     place_columns(out, keep, other, send, (even, 2 + last - even))
     clear_column(keep, other, send, 1 - last)
-
-
-def third_kernel(own, x2, cx, x3, e3, o3, keep, other, send):
+    early = early_keep.shape[1]
+    keep[:, :early] += early_keep[...]
+    other[:, :early] += early_other[...]
+
+
+def turn_kernel(own, x2, cx, x3, high, low):
     rows = own.shape[1]
-    mine = side_by_side(own[...], x2[...], cx[...], x3[...])
-    out = product(side_by_side(e3[...], o3[...]), mine)
-    keep[...] = out[:, :rows]
-    other[...] = out[:, rows : 2 * rows]
-    send[...] = out[:, 2 * rows :]
+    for i, ref in enumerate((own, x2, cx, x3)):
+        high[block(i, rows)], low[block(i, rows)] = halves(ref[...].T)
+
+
+def third_kernel(high, low, e3, o3, keep, other, send):
+    ch, cl = halves(side_by_side(e3[...], o3[...]))
+    dot = functools.partial(jnp.dot, preferred_element_type=jnp.float32)
+    spread(dot(high[...], ch) + (dot(high[...], cl) + dot(low[...], ch)), keep, other, send)
 
 
 def wanted(pairs, me, offset, reach):
@@ -140,17 +150,17 @@
     near = jnp.where(upper, 2, 1)
     this, that = 5 - flip, 4 + flip
     write(here + near, (t1, this), (y2, 2))
-    write(there + near, (t1, that), (y2, 1), (y1, 8))
-    write(here + 3 - near, (t2, 1), (t1, 8), (y1, this))
+    write(there + near, (t1, that), (y2, 1))
+    write(here + 3 - near, (t2, 1), (y1, this))
     write(there + 3 - near, (t2, 2), (y1, that))
-    write(jnp.where(upper, high, low + 3), (t2, 0), (t1, 7), (y1, 6))
-    write(jnp.where(upper, low + 3, high), (t1, 6), (y1, 7), (y2, 0))
+    write(jnp.where(upper, high, low + 3), (t2, 0), (y1, 6))
+    write(jnp.where(upper, low + 3, high), (t1, 6), (y2, 0))
 
 
 def final_kernel(reach, at_ref, pairs, k3, c3, y3, ez, oz, band, out, parts, sems):
     del band
     k, odd, me = at_ref[0], at_ref[1] == 1, at_ref[3]
-    rows = y3.shape[1]
+    rows = y3.shape[0]
     copies = []
 
     def write(index, value):
@@ -163,9 +173,9 @@
         behind = m >= k
         value = jnp.where(behind == odd, ez[:, block(m, rows)], oz[:, block(m, rows)])
         write(jnp.where(behind, m + 1, 4 * PLANE + m), value)
-    third = k3[...] + c3[:, :rows] + y3[...]
-    write(jnp.where(odd, PLANE, 4 * PLANE - 1), third[:rows].T)
-    write(jnp.where(odd, 4 * PLANE - 1, PLANE), third[rows:].T)
+    third = k3[...] + c3[:rows] + y3[...]
+    write(jnp.where(odd, PLANE, 4 * PLANE - 1), third[:, :rows])
+    write(jnp.where(odd, 4 * PLANE - 1, PLANE), third[:, rows:])
     for copy in copies:
         copy.wait()
 
@@ -173,7 +183,7 @@
 def call(kernel, outs, scratch, scalars, arrays, flops=1000):
     return pl.pallas_call(
         kernel,
-        cost_estimate=pl.CostEstimate(flops=flops, bytes_accessed=1000, transcendentals=0),
+        cost_estimate=pl.CostEstimate(flops=flops, bytes_accessed=sum(a.size * 4 for a in arrays), transcendentals=0),
         in_specs=[pl.BlockSpec(memory_space=pltpu.SMEM)] * len(scalars)
         + [pl.BlockSpec(memory_space=pltpu.VMEM)] * len(arrays),
         out_specs=[pl.BlockSpec(memory_space=pltpu.VMEM)] * len(outs),
@@ -226,9 +236,10 @@
     own = quarter(k, q1)
     near_inner = jnp.where(outer, cx, own)
     e0, o0 = both(near_inner, near_inner)
-    x2 = xor(quarter(k ^ 2, cx), 2)
-
-    own_a, cx_a, x3_a, _ = lax.optimization_barrier((own, cx, x3, near_inner))
+    q2 = quarter(k ^ 2, cx)
+    x2 = xor(q2, 2)
+
+    own_a, cx_a, x3_a, _, _ = lax.optimization_barrier((own, cx, x3, near_inner, q2))
     near_outer = jnp.where(outer, own_a, cx_a)
     e1, o1 = both(jnp.where(flip, near_outer, x3_a), jnp.where(flip, x3_a, near_outer))
 
@@ -262,29 +273,35 @@
     mine = (own, x2, cx, x3)
 
     def first_part(place, *operands):
-        return core_sum(*call(first_kernel, parts(9), [], (place,), operands))
-
-    t1, out1 = fenced(first_part, place, *mine, e0, o0, e1, o1)
+        total, out = core_sum(*call(first_kernel, parts(9), [], (place,), operands))
+        cut = 7 * rows
+        return total[:, :cut], out[:, :cut], total[:, cut:], out[:, cut:]
+
+    t1, out1, *early = fenced(first_part, place, *mine, e0, o0, e1, o1)
     y1 = xor(out1, 2)
 
-    def second_part(place, own, x2, cx, x3, *arrived):
+    def second_part(place, own, x2, cx, x3, early_keep, early_other, *arrived):
         square, tall = (pltpu.VMEM((n * rows, 3 * rows), jnp.float32) for n in (PLANE - 1, PLANE))
         keep, other, send = call(cross_kernel, parts(3), [square, tall], (place,), arrived)
         half, out = core_sum(keep, other, send)
         far = xor(out, 2)
+        place = after(place, out)
+        k2, other, send = call(second_kernel, parts(3), [], (place,), (own, x2, cx, x3, *arrived[4:], early_keep, early_other))
+        turned = [jax.ShapeDtypeStruct((PLANE * rows, depth), jnp.bfloat16)] * 2
+        high, low = call(turn_kernel, turned, [], (), (after(own, k2), x2, cx, x3))
+        half = after(half, high)
         pack = call(add_kernel, [f32(rows, 3 * rows)], [], (), (half, far), flops=10**11)[0]
-        place = after(place, keep)
-        return pack, *core_sum(*call(second_kernel, parts(3), [], (place,), (own, x2, cx, x3, *arrived[4:])))
-
-    pack, t2, out2 = fenced(second_part, place, *mine, e0, o0, e1, o1, e2, o2)
+        return pack, high, low, *core_sum(k2, other, send)
+
+    pack, high, low, t2, out2 = fenced(second_part, place, *mine, *early, e0, o0, e1, o1, e2, o2)
     ez, oz = both(pack, pack)
     y2 = xor(out2, 2)
 
     e3, o3, _, _ = lax.optimization_barrier((e3, o3, pack, y1))
-    pair = f32(2 * rows, rows)
-    k3, other, send = call(third_kernel, [pair, pair, f32(2 * rows, 2 * rows)], [], (), (*mine, e3, o3))
-    c3 = xor(after(send, y2), 1)
-    y3 = xor(other + c3[:, rows:], 2)
+    k3, other, send = call(third_kernel, parts(2), [], (), (high, low, e3, o3))
+    c3 = xor(send, 1)
+    y2 = call(copy_kernel, [f32(rows, 3 * rows)], [], (), (y2,), flops=5 * 10**9)[0]
+    y3 = xor(after(other + c3[rows:], y2), 2)
 
     whole = f32(rows, (2 * reach + 1) * rows)
     band = call(functools.partial(band_kernel, reach), [whole], [], (place, pair_list), (t1, y1, t2, y2))[0]

time: 111 us -> 106 us (0.955)
  starting transfers between devices: 33.5 us -> 26.1 us
  waiting for transfers between devices: 39 us -> 42.3 us
  Pallas kernels: 26.7 us -> 25.5 us
    ppermute x10, starting transfers between devices: 23.6 us -> 16.4 us  [along(): return lax.ppermute(value, 'blk', route)]
    ppermute x11, waiting for transfers between devices: 36.5 us -> 42.3 us  [xor(): return lax.ppermute(value, 'blk', [(i, i ^ t) for i in devices])]
    ppermute x10, waiting for transfers between devices: 2.49 us -> 0.03 us  [along(): return lax.ppermute(value, 'blk', route)]
    pallas_call x6 -> x8, Pallas kernels: 25.3 us -> 24 us  [call(): pl.pallas_call(kernel, cost_estimate=pl.CostEstimate(flops=flops, bytes_a...]
  transfers between devices with their start and end apart: 21 -> 21, of which waited for: 7 -> 7; matrix products, arithmetic and copies ran while one was open for 8% -> 7% of each run, Pallas kernels for 23% -> 23%
where the time goes in v4:
time: 106 us
  waiting for transfers between devices  42.3 us (40%)
  starting transfers between devices  26.1 us (25%)
  Pallas kernels  25.5 us (24%)
  local copies, waits for them, and re-layouts  6.29 us (6%)
  other arithmetic  5.13 us (5%)
    ppermute x11, waiting for transfers between devices, xor(): return lax.ppermute(value, 'blk', [(i, i ^ t) for i in devices])  42.3 us
    pallas_call x8, Pallas kernels, call(): pl.pallas_call(kernel, cost_estimate=pl.CostEstimate(flops=flops, bytes_a...  24 us
    ppermute x10, starting transfers between devices, along(): return lax.ppermute(value, 'blk', route)  16.4 us
    ppermute x11, starting transfers between devices, xor(): return lax.ppermute(value, 'blk', [(i, i ^ t) for i in devices])  9.73 us
    squeeze x3, local copies, waits for them, and re-layouts, quarter(): lax.dynamic_index_in_dim(after(quarters, *others), index, 0, keepdims=False)  4.65 us
  transfers between devices with their start and end apart: 21, of which 7 were waited for; matrix products, arithmetic and copies ran while one was open for 7% of the time, Pallas kernels for 23%

profile of v4, /device:TPU:0, one launch (start us, length us, event | category | flops | bytes accessed | tf_op | source)
XLA Modules:
  0.0 105.6 jit_solution(17944175519750008823)
XLA Ops:
  0.0 2.2 %dynamic-slice_bitcast_fusion.3 = f32[1800,128]{1,0:T(8,128)} fusion(f32[4,1800,128]{2,1,0:T(8,128)} %bitcast.16, s32[]{:T(128)S(6)} %select_n.82), kind=kLoop, calls=%fused_computation.11 | loop fusion | bytes 1843204 | tf_op jit(solution)/shard_map/jit(dynamic_index_in_dim)/squeeze | solution.py:230
  2.6 1.2 %dynamic-slice_bitcast_fusion.1 = f32[1800,128]{1,0:T(8,128)S(1)} fusion(f32[4,1800,128]{2,1,0:T(8,128)} %bitcast.17, s32[]{:T(128)S(6)} %select_n.86), kind=kLoop, calls=%fused_computation.9 | loop fusion | bytes 1843204 | tf_op jit(solution)/shard_map/jit(dynamic_index_in_dim)/squeeze | solution.py:230
  3.9 2.7 %collective-permute-start.7 = (f32[1800,128]{1,0:T(8,128)S(1)}, f32[1800,128]{1,0:T(8,128)S(1)}, u32[]{:S(2)}, u32[]{:S(2)}) collective-permute-start(f32[1800,128]{1,0:T(8,128)S(1)} %dynamic-slice_bitcast_fusion.1), channel_id=1, source_target_pairs={{0,3},{1,2},{2,1},{3,0},{4,7},{5,6},{6,5},{7,4},{8,11},{9,10},{10,... | collective-permute-start | bytes 2764808 | tf_op jit(solution)/shard_map/ppermute | solution.py:214
  6.6 1.3 %broadcast_select_fusion.7 = (f32[1800,128]{1,0:T(8,128)S(1)}, f32[1800,128]{1,0:T(8,128)S(1)}) fusion(f32[1800,128]{1,0:T(8,128)S(1)} %collective-permute-done.4, pred[]{:T(512)S(6)} %or.3, f32[4,1800,128]{2,1,0:T(8,128)} %bitcast.18, s32[]{:T(128)S(6)} %select_n.83), kind=kLoop, calls=%fused_computation.19 | loop fusion | flops 230400 | bytes 3686405 | tf_op jit(solution)/shard_map/jit(_where)/select_n | solution.py:237
  7.9 1.6 %collective-permute-start.5 = (f32[1800,128]{1,0:T(8,128)S(1)}, f32[1800,128]{1,0:T(8,128)}, u32[]{:S(2)}, u32[]{:S(2)}) collective-permute-start(f32[1800,128]{1,0:T(8,128)S(1)} %get-tuple-element.141), channel_id=1, source_target_pairs={{0,4},{1,5},{2,6},{3,7},{4,0},{5,1},{6,2},{7,3},{8,12},{9,13},{10,... | collective-permute-start | bytes 2764808 | tf_op jit(solution)/shard_map/ppermute | solution.py:222
  10.2 1.2 %dynamic-slice_bitcast_fusion = f32[1800,128]{1,0:T(8,128)S(1)} fusion(f32[4,1800,128]{2,1,0:T(8,128)} %bitcast.19, s32[]{:T(128)S(6)} %select_n.87), kind=kLoop, calls=%fused_computation.8 | loop fusion | bytes 1843204 | tf_op jit(solution)/shard_map/jit(dynamic_index_in_dim)/squeeze | solution.py:230
  11.5 1.3 %collective-permute-start.10 = (f32[1800,128]{1,0:T(8,128)S(1)}, f32[1800,128]{1,0:T(8,128)S(1)}, u32[]{:S(2)}, u32[]{:S(2)}) collective-permute-start(f32[1800,128]{1,0:T(8,128)S(1)} %dynamic-slice_bitcast_fusion), channel_id=1, source_target_pairs={{0,2},{1,3},{2,0},{3,1},{4,6},{5,7},{6,4},{7,5},{8,10},{9,11},{10,... | collective-permute-start | bytes 2764808 | tf_op jit(solution)/shard_map/ppermute | solution.py:214
  12.8 14.6 %collective-permute-done.7 = f32[1800,128]{1,0:T(8,128)S(1)} collective-permute-done((f32[1800,128]{1,0:T(8,128)S(1)}, f32[1800,128]{1,0:T(8,128)S(1)}, u32[]{:S(2)}, u32[]{:S(2)}) %collective-permute-start.7) | collective-permute-done | bytes 921632 | tf_op jit(solution)/shard_map/ppermute | solution.py:214
  27.6 1.6 %collective-permute-start.8 = (f32[1800,128]{1,0:T(8,128)S(1)}, f32[1800,128]{1,0:T(8,128)}, u32[]{:S(2)}, u32[]{:S(2)}) collective-permute-start(f32[1800,128]{1,0:T(8,128)S(1)} %get-tuple-element.152), channel_id=1, source_target_pairs={{0,4},{1,5},{2,6},{3,7},{4,0},{5,1},{6,2},{7,3},{8,12},{9,13},{10,... | collective-permute-start | bytes 2764808 | tf_op jit(solution)/shard_map/ppermute | solution.py:222
  29.3 1.6 %collective-permute-start.9 = (f32[1800,128]{1,0:T(8,128)S(1)}, f32[1800,128]{1,0:T(8,128)}, u32[]{:S(2)}, u32[]{:S(2)}) collective-permute-start(f32[1800,128]{1,0:T(8,128)S(1)} %get-tuple-element.151), channel_id=1, source_target_pairs={{4,8},{5,9},{6,10},{7,11},{8,4},{9,5},{10,6},{11,7},{20,24},{21,25... | collective-permute-start | bytes 2764808 | tf_op jit(solution)/shard_map/ppermute | solution.py:222
  30.9 16.5 %collective-permute-done.10 = f32[1800,128]{1,0:T(8,128)S(1)} collective-permute-done((f32[1800,128]{1,0:T(8,128)S(1)}, f32[1800,128]{1,0:T(8,128)S(1)}, u32[]{:S(2)}, u32[]{:S(2)}) %collective-permute-start.10) | collective-permute-done | bytes 921632 | tf_op jit(solution)/shard_map/ppermute | solution.py:214
  47.3 1.5 %select_select_fusion = (f32[1800,128]{1,0:T(8,128)}, f32[1800,128]{1,0:T(8,128)}) fusion(f32[1800,128]{1,0:T(8,128)S(1)} %collective-permute-done.10, f32[1800,128]{1,0:T(8,128)S(1)} %collective-permute-done.7, pred[]{:T(512)S(6)} %xor.12, pred[]{:T(512)S(6)} %or.3), kind=kLoop, calls=%fused_computation.6 | loop fusion | flops 691200 | bytes 3686402 | tf_op jit(solution)/shard_map/jit(_where)/select_n | solution.py:248
  48.8 1.7 %collective-permute-start.11 = (f32[1800,128]{1,0:T(8,128)}, f32[1800,128]{1,0:T(8,128)}, u32[]{:S(2)}, u32[]{:S(2)}) collective-permute-start(f32[1800,128]{1,0:T(8,128)} %get-tuple-element.154), channel_id=1, source_target_pairs={{0,4},{1,5},{2,6},{3,7},{4,0},{5,1},{6,2},{7,3},{8,12},{9,13},{10,... | collective-permute-start | bytes 2764808 | tf_op jit(solution)/shard_map/ppermute | solution.py:222
  50.5 1.6 %collective-permute-start.12 = (f32[1800,128]{1,0:T(8,128)}, f32[1800,128]{1,0:T(8,128)}, u32[]{:S(2)}, u32[]{:S(2)}) collective-permute-start(f32[1800,128]{1,0:T(8,128)} %get-tuple-element.153), channel_id=1, source_target_pairs={{4,8},{5,9},{6,10},{7,11},{8,4},{9,5},{10,6},{11,7},{20,24},{21,25... | collective-permute-start | bytes 2764808 | tf_op jit(solution)/shard_map/ppermute | solution.py:222
  52.1 1.7 %broadcast_select_fusion = (f32[1800,128]{1,0:T(8,128)}, f32[1800,128]{1,0:T(8,128)}) fusion(pred[]{:T(512)S(6)} %xor.12, f32[1800,128]{1,0:T(8,128)S(1)} %collective-permute-done.7, f32[1800,128]{1,0:T(8,128)S(1)} %collective-permute-done.10, pred[]{:T(512)S(6)} %or.3, f32[1800,128]{1,0:T(8,128)S(1)} %get-tuple-element.128, ...), kind=kLoop, calls=%fused_computation.12 | loop fusion | flops 921600 | bytes 5529602 | tf_op jit(solution)/shard_map/jit(_where)/select_n | solution.py:253
  53.8 3.5 %collective-permute-start.13 = (f32[1800,128]{1,0:T(8,128)}, f32[1800,128]{1,0:T(8,128)S(1)}, u32[]{:S(2)}, u32[]{:S(2)}) collective-permute-start(f32[1800,128]{1,0:T(8,128)} %get-tuple-element.150), channel_id=1, source_target_pairs={{0,4},{1,5},{2,6},{3,7},{4,0},{5,1},{6,2},{7,3},{8,12},{9,13},{10,... | collective-permute-start | bytes 2764808 | tf_op jit(solution)/shard_map/ppermute | solution.py:222
  58.1 12.8 %conditional.2 = (f32[128,896]{1,0:T(8,128)S(1)}, f32[128,896]{1,0:T(8,128)S(1)}, f32[128,256]{1,0:T(8,128)S(1)}, f32[128,256]{1,0:T(8,128)S(1)}) conditional(s32[]{:T(128)} %convert_element_type.2, () %tuple.36, (s32[4]{0:T(128)S(1)}, f32[1800,128]{1,0:T(8,128)}, f32[1800,128]{1,0:T(8,128)}, f32[1800,128]{1,0:T(8,128)S(1)}, f32[1800,128]{1,0:T(8,128)}, ...), branch_computations={%region_0.1_spmd, %region_1.2_spmd} | conditional | flops 295912 | bytes 17989704 | solution.py:271
  58.1 9.6 %branch_1_fun.5 = (f32[128,1152]{1,0:T(8,128)S(1)}, f32[128,1152]{1,0:T(8,128)S(1)}, f32[256,1152]{1,0:T(8,128)S(1)}) custom-call(s32[4]{0:T(128)S(1)} %get-tuple-element.49.at_ref, f32[1800,128]{1,0:T(8,128)} %get-tuple-element.50.own, f32[1800,128]{1,0:T(8,128)} %get-tuple-element.51.x2, f32[1800,128]{1,0:T(8,128)S(1)} %get-tuple-element.52.cx, ...), custom_call_target="tpu_custom_call" | custom-call | flops 1000 | bytes 7372800 | tf_op jit(solution)/shard_map/cond/branch_1_fun/pallas_call | solution.py:184
  67.7 2.8 %collective-permute-done = f32[256,1152]{1,0:T(8,128)S(1)} collective-permute-done((f32[256,1152]{1,0:T(8,128)S(1)}, f32[256,1152]{1,0:T(8,128)S(1)}, u32[]{:S(2)}, u32[]{:S(2)}) %collective-permute-start) | collective-permute-done | bytes 1179680 | tf_op jit(solution)/shard_map/cond/branch_1_fun/ppermute | solution.py:214
  72.3 1.5 %collective-permute-start.15 = (f32[128,896]{1,0:T(8,128)}, f32[128,896]{1,0:T(8,128)S(1)}, u32[]{:S(2)}, u32[]{:S(2)}) collective-permute-start(f32[128,896]{1,0:T(8,128)} %copy-done.11), channel_id=1, source_target_pairs={{0,2},{1,3},{2,0},{3,1},{4,6},{5,7},{6,4},{7,5},{8,10},{9,11},{10,... | collective-permute-start | bytes 1376264 | tf_op jit(solution)/shard_map/ppermute | solution.py:214
  73.9 16.2 %conditional.3 = (f32[128,384]{1,0:T(8,128)}, bf16[512,1800]{1,0:T(8,128)(2,1)S(1)}, bf16[512,1800]{1,0:T(8,128)(2,1)S(1)}, f32[128,384]{1,0:T(8,128)S(1)}, f32[128,384]{1,0:T(8,128)S(1)}) conditional(s32[]{:T(128)} %convert_element_type.2, () %tuple.31, (s32[4]{0:T(128)S(1)}, f32[1800,128]{1,0:T(8,128)}, f32[1800,128]{1,0:T(8,128)}, ...), branch_computations={%region_2.3_spmd, %region_3.4_spmd} | conditional | flops 100000194560 | bytes 33276176 | solution.py:271
  73.9 5.5 %branch_1_fun.6 = (f32[128,384]{1,0:T(8,128)S(1)}, f32[128,384]{1,0:T(8,128)S(1)}, f32[256,384]{1,0:T(8,128)S(1)}) custom-call(s32[4]{0:T(128)S(1)} %get-tuple-element.72.at_ref, f32[1800,128]{1,0:T(8,128)} %get-tuple-element.62.e0, f32[1800,128]{1,0:T(8,128)} %get-tuple-element.63.o0, f32[1800,128]{1,0:T(8,128)} %get-tuple-element.64.e1, ...), custom_call_target="tpu_custom_call" | custom-call | flops 1000 | bytes 5529600 | tf_op jit(solution)/shard_map/cond/branch_1_fun/pallas_call | solution.py:184
  79.5 1.7 %collective-permute-done.1 = f32[256,384]{1,0:T(8,128)S(1)} collective-permute-done((f32[256,384]{1,0:T(8,128)S(1)}, f32[256,384]{1,0:T(8,128)S(1)}, u32[]{:S(2)}, u32[]{:S(2)}) %collective-permute-start.1) | collective-permute-done | bytes 393248 | tf_op jit(solution)/shard_map/cond/branch_1_fun/ppermute | solution.py:214
  82.1 3.4 %branch_1_fun.7 = (f32[128,384]{1,0:T(8,128)S(1)}, f32[128,384]{1,0:T(8,128)S(1)}, f32[256,384]{1,0:T(8,128)S(1)}) custom-call(s32[4]{0:T(128)S(1)} %get-tuple-element.72.at_ref, f32[1800,128]{1,0:T(8,128)S(1)} %copy-done.3, f32[1800,128]{1,0:T(8,128)S(1)} %copy-done.5, f32[1800,128]{1,0:T(8,128)S(1)} %get-tuple-element.74.cx, f32[1800,128]{1,0:T(8,128)S(1)} %copy-done.1, ...), custom_call_target="tpu_custom_call" | custom-call | flops 1000 | bytes 5791744 | tf_op jit(solution)/shard_map/cond/branch_1_fun/pallas_call | solution.py:184
  86.7 2.6 %collective-permute-done.2.b = f32[128,384]{1,0:T(8,128)S(1)} collective-permute-done((f32[128,384]{1,0:T(8,128)S(1)}, f32[128,384]{1,0:T(8,128)S(1)}, u32[]{:S(2)}, u32[]{:S(2)}) %collective-permute-start.2) | collective-permute-done | bytes 196640 | tf_op jit(solution)/shard_map/cond/branch_1_fun/ppermute | solution.py:214
  90.1 1.6 %collective-permute-start.17 = (f32[128,384]{1,0:T(8,128)S(1)}, f32[128,384]{1,0:T(8,128)S(1)}, u32[]{:S(2)}, u32[]{:S(2)}) collective-permute-start(f32[128,384]{1,0:T(8,128)S(1)} %get-tuple-element.137), channel_id=1, source_target_pairs={{0,2},{1,3},{2,0},{3,1},{4,6},{5,7},{6,4},{7,5},{8,10},{9,11},{10,... | collective-permute-start | bytes 589832 | tf_op jit(solution)/shard_map/ppermute | solution.py:214
  91.6 2.7 %collective-permute-start.19 = (f32[128,384]{1,0:T(8,128)}, f32[128,384]{1,0:T(8,128)S(1)}, u32[]{:S(2)}, u32[]{:S(2)}) collective-permute-start(f32[128,384]{1,0:T(8,128)} %get-tuple-element.130), channel_id=1, source_target_pairs={{0,4},{1,5},{2,6},{3,7},{4,0},{5,1},{6,2},{7,3},{8,12},{9,13},{10,... | collective-permute-start | bytes 589832 | tf_op jit(solution)/shard_map/ppermute | solution.py:222
  95.1 1.8 %shard_map.28 = (f32[128,256]{1,0:T(8,128)S(1)}, f32[128,256]{1,0:T(8,128)S(1)}, f32[256,256]{1,0:T(8,128)S(1)}) custom-call(bf16[512,1800]{1,0:T(8,128)(2,1)S(1)} %get-tuple-element.122.high, bf16[512,1800]{1,0:T(8,128)(2,1)S(1)} %get-tuple-element.123.low, f32[1800,128]{1,0:T(8,128)S(1)} %collective-permute-done.13.e3, ...), custom_call_target="tpu_custom_call" | custom-call | flops 1000 | bytes 9216000 | tf_op jit(solution)/shard_map/pallas_call | solution.py:184
  97.1 1.5 %collective-permute-done.16.c3 = f32[256,256]{1,0:T(8,128)S(1)} collective-permute-done((f32[256,256]{1,0:T(8,128)S(1)}, f32[256,256]{1,0:T(8,128)S(1)}, u32[]{:S(2)}, u32[]{:S(2)}) %collective-permute-start.16) | collective-permute-done | bytes 262176 | tf_op jit(solution)/shard_map/ppermute | solution.py:214
  99.7 1.9 %shard_map.30.band = f32[128,1920]{1,0:T(8,128)} custom-call(s32[4]{0:T(128)S(1)} %pad_add_fusion.at_ref, s32[16,8]{1,0:T(8,128)S(1)} %copy.5.pairs, f32[128,896]{1,0:T(8,128)S(1)} %copy-done.8, f32[128,896]{1,0:T(8,128)S(1)} %collective-permute-done.15.y1, f32[128,384]{1,0:T(8,128)S(1)} %get-tuple-element.140.t2, f32[128,384]{1,0:T(8,128)S(1)} %shard_map.29.y2), custom_call_target="tpu_custom_call" | custom-call | flops 1000 | bytes 1310720 | tf_op jit(solution)/shard_map/pallas_call | solution.py:184
  101.6 2.6 %collective-permute-done.18.y3 = f32[128,256]{1,0:T(8,128)S(1)} collective-permute-done((f32[128,256]{1,0:T(8,128)S(1)}, f32[128,256]{1,0:T(8,128)S(1)}, u32[]{:S(2)}, u32[]{:S(2)}) %collective-permute-start.18) | collective-permute-done | bytes 131104 | tf_op jit(solution)/shard_map/ppermute | solution.py:214
  104.2 1.5 %shard_map.31 = f32[128,1920]{1,0:T(8,128)} custom-call(s32[4]{0:T(128)S(1)} %pad_add_fusion.at_ref, s32[16,8]{1,0:T(8,128)S(1)} %copy.5.pairs, f32[128,256]{1,0:T(8,128)S(1)} %get-tuple-element.134.k3, f32[256,256]{1,0:T(8,128)S(1)} %collective-permute-done.16.c3, f32[128,256]{1,0:T(8,128)S(1)} %collective-permute-done.18.y3, ...), custom_call_target="tpu_custom_call", output_to_operand_aliasing={{}: (7, {})} | custom-call | tf_op jit(solution)/shard_map/pallas_call | solution.py:309
  (64 shorter events, 8.8 us)
Async XLA Ops:
  2.2 4.4 %collective-permute-start.4 = (f32[1800,128]{1,0:T(8,128)}, f32[1800,128]{1,0:T(8,128)S(1)}, u32[]{:S(2)}, u32[]{:S(2)}) collective-permute-start(f32[1800,128]{1,0:T(8,128)} %dynamic-slice_bitcast_fusion.3), channel_id=1, source_target_pairs={{0,1},{1,0},{2,3},{3,2},{4,5},{5,4},{6,7},{7,6},{8,9},{9,8},{10,11... | collective-permute-start | bytes 2764808 | tf_op jit(solution)/shard_map/ppermute | solution.py:214
  3.9 23.5 %collective-permute-start.7 = (f32[1800,128]{1,0:T(8,128)S(1)}, f32[1800,128]{1,0:T(8,128)S(1)}, u32[]{:S(2)}, u32[]{:S(2)}) collective-permute-start(f32[1800,128]{1,0:T(8,128)S(1)} %dynamic-slice_bitcast_fusion.1), channel_id=1, source_target_pairs={{0,3},{1,2},{2,1},{3,0},{4,7},{5,6},{6,5},{7,4},{8,11},{9,10},{10,... | collective-permute-start | bytes 2764808 | tf_op jit(solution)/shard_map/ppermute | solution.py:214
  7.9 44.2 %copy-start.2 = (f32[1800,128]{1,0:T(8,128)}, f32[1800,128]{1,0:T(8,128)S(1)}, u32[]{:S(2)}) copy-start(f32[1800,128]{1,0:T(8,128)S(1)} %get-tuple-element.128) | copy-start | bytes 2764804
  7.9 23.0 %collective-permute-start.5 = (f32[1800,128]{1,0:T(8,128)S(1)}, f32[1800,128]{1,0:T(8,128)}, u32[]{:S(2)}, u32[]{:S(2)}) collective-permute-start(f32[1800,128]{1,0:T(8,128)S(1)} %get-tuple-element.141), channel_id=1, source_target_pairs={{0,4},{1,5},{2,6},{3,7},{4,0},{5,1},{6,2},{7,3},{8,12},{9,13},{10,... | collective-permute-start | bytes 2764808 | tf_op jit(solution)/shard_map/ppermute | solution.py:222
  9.5 21.3 %collective-permute-start.6 = (f32[1800,128]{1,0:T(8,128)S(1)}, f32[1800,128]{1,0:T(8,128)S(1)}, u32[]{:S(2)}, u32[]{:S(2)}) collective-permute-start(f32[1800,128]{1,0:T(8,128)S(1)} %get-tuple-element.141), channel_id=1, source_target_pairs={{4,8},{5,9},{6,10},{7,11},{8,4},{9,5},{10,6},{11,7},{20,24},{21,25... | collective-permute-start | bytes 2764808 | tf_op jit(solution)/shard_map/ppermute | solution.py:222
  11.5 35.8 %collective-permute-start.10 = (f32[1800,128]{1,0:T(8,128)S(1)}, f32[1800,128]{1,0:T(8,128)S(1)}, u32[]{:S(2)}, u32[]{:S(2)}) collective-permute-start(f32[1800,128]{1,0:T(8,128)S(1)} %dynamic-slice_bitcast_fusion), channel_id=1, source_target_pairs={{0,2},{1,3},{2,0},{3,1},{4,6},{5,7},{6,4},{7,5},{8,10},{9,11},{10,... | collective-permute-start | bytes 2764808 | tf_op jit(solution)/shard_map/ppermute | solution.py:214
  27.4 24.7 %copy-start = (f32[1800,128]{1,0:T(8,128)}, f32[1800,128]{1,0:T(8,128)S(1)}, u32[]{:S(2)}) copy-start(f32[1800,128]{1,0:T(8,128)S(1)} %collective-permute-done.7) | copy-start | bytes 2764804
  27.6 24.5 %collective-permute-start.8 = (f32[1800,128]{1,0:T(8,128)S(1)}, f32[1800,128]{1,0:T(8,128)}, u32[]{:S(2)}, u32[]{:S(2)}) collective-permute-start(f32[1800,128]{1,0:T(8,128)S(1)} %get-tuple-element.152), channel_id=1, source_target_pairs={{0,4},{1,5},{2,6},{3,7},{4,0},{5,1},{6,2},{7,3},{8,12},{9,13},{10,... | collective-permute-start | bytes 2764808 | tf_op jit(solution)/shard_map/ppermute | solution.py:222
  29.3 22.8 %collective-permute-start.9 = (f32[1800,128]{1,0:T(8,128)S(1)}, f32[1800,128]{1,0:T(8,128)}, u32[]{:S(2)}, u32[]{:S(2)}) collective-permute-start(f32[1800,128]{1,0:T(8,128)S(1)} %get-tuple-element.151), channel_id=1, source_target_pairs={{4,8},{5,9},{6,10},{7,11},{8,4},{9,5},{10,6},{11,7},{20,24},{21,25... | collective-permute-start | bytes 2764808 | tf_op jit(solution)/shard_map/ppermute | solution.py:222
  30.9 16.5 %copy-start.6 = (f32[1800,128]{1,0:T(8,128)}, f32[1800,128]{1,0:T(8,128)S(1)}, u32[]{:S(2)}) copy-start(f32[1800,128]{1,0:T(8,128)S(1)} %collective-permute-done.6) | copy-start | bytes 2764804
  47.3 6.5 %copy-start.4 = (f32[1800,128]{1,0:T(8,128)}, f32[1800,128]{1,0:T(8,128)S(1)}, u32[]{:S(2)}) copy-start(f32[1800,128]{1,0:T(8,128)S(1)} %collective-permute-done.10) | copy-start | bytes 2764804
  48.8 25.0 %collective-permute-start.11 = (f32[1800,128]{1,0:T(8,128)}, f32[1800,128]{1,0:T(8,128)}, u32[]{:S(2)}, u32[]{:S(2)}) collective-permute-start(f32[1800,128]{1,0:T(8,128)} %get-tuple-element.154), channel_id=1, source_target_pairs={{0,4},{1,5},{2,6},{3,7},{4,0},{5,1},{6,2},{7,3},{8,12},{9,13},{10,... | collective-permute-start | bytes 2764808 | tf_op jit(solution)/shard_map/ppermute | solution.py:222
  50.5 23.3 %collective-permute-start.12 = (f32[1800,128]{1,0:T(8,128)}, f32[1800,128]{1,0:T(8,128)}, u32[]{:S(2)}, u32[]{:S(2)}) collective-permute-start(f32[1800,128]{1,0:T(8,128)} %get-tuple-element.153), channel_id=1, source_target_pairs={{4,8},{5,9},{6,10},{7,11},{8,4},{9,5},{10,6},{11,7},{20,24},{21,25... | collective-permute-start | bytes 2764808 | tf_op jit(solution)/shard_map/ppermute | solution.py:222
  53.8 41.3 %collective-permute-start.13 = (f32[1800,128]{1,0:T(8,128)}, f32[1800,128]{1,0:T(8,128)S(1)}, u32[]{:S(2)}, u32[]{:S(2)}) collective-permute-start(f32[1800,128]{1,0:T(8,128)} %get-tuple-element.150), channel_id=1, source_target_pairs={{0,4},{1,5},{2,6},{3,7},{4,0},{5,1},{6,2},{7,3},{8,12},{9,13},{10,... | collective-permute-start | bytes 2764808 | tf_op jit(solution)/shard_map/ppermute | solution.py:222
  57.3 37.8 %collective-permute-start.14 = (f32[1800,128]{1,0:T(8,128)}, f32[1800,128]{1,0:T(8,128)S(1)}, u32[]{:S(2)}, u32[]{:S(2)}) collective-permute-start(f32[1800,128]{1,0:T(8,128)} %get-tuple-element.149), channel_id=1, source_target_pairs={{4,8},{5,9},{6,10},{7,11},{8,4},{9,5},{10,6},{11,7},{20,24},{21,25... | collective-permute-start | bytes 2764808 | tf_op jit(solution)/shard_map/ppermute | solution.py:222
  67.7 2.9 %collective-permute-start = (f32[256,1152]{1,0:T(8,128)S(1)}, f32[256,1152]{1,0:T(8,128)S(1)}, u32[]{:S(2)}, u32[]{:S(2)}) collective-permute-start(f32[256,1152]{1,0:T(8,128)S(1)} %get-tuple-element.59), channel_id=1, source_target_pairs={{0,1},{1,0},{2,3},{3,2},{4,5},{5,4},{6,7},{7,6},{8,9},{9,8},{10,11... | collective-permute-start | bytes 3538952 | tf_op jit(solution)/shard_map/cond/branch_1_fun/ppermute | solution.py:214
  72.3 1.5 %copy-start.7 = (f32[128,896]{1,0:T(8,128)}, f32[128,896]{1,0:T(8,128)S(1)}, u32[]{:S(2)}) copy-start(f32[128,896]{1,0:T(8,128)S(1)} %get-tuple-element.139.t1) | copy-start | bytes 1376260
  72.3 22.1 %collective-permute-start.15 = (f32[128,896]{1,0:T(8,128)}, f32[128,896]{1,0:T(8,128)S(1)}, u32[]{:S(2)}, u32[]{:S(2)}) collective-permute-start(f32[128,896]{1,0:T(8,128)} %copy-done.11), channel_id=1, source_target_pairs={{0,2},{1,3},{2,0},{3,1},{4,6},{5,7},{6,4},{7,5},{8,10},{9,11},{10,... | collective-permute-start | bytes 1376264 | tf_op jit(solution)/shard_map/ppermute | solution.py:214
  73.9 8.2 %copy-start.1 = (f32[1800,128]{1,0:T(8,128)S(1)}, f32[1800,128]{1,0:T(8,128)}, u32[]{:S(2)}) copy-start(f32[1800,128]{1,0:T(8,128)} %get-tuple-element.75.x3) | copy-start | bytes 2764804 | tf_op jit(solution)/shard_map/cond
  73.9 8.2 %copy-start.3 = (f32[1800,128]{1,0:T(8,128)S(1)}, f32[1800,128]{1,0:T(8,128)}, u32[]{:S(2)}) copy-start(f32[1800,128]{1,0:T(8,128)} %get-tuple-element.79.own) | copy-start | bytes 2764804 | tf_op jit(solution)/shard_map/cond
  73.9 8.2 %copy-start.5 = (f32[1800,128]{1,0:T(8,128)S(1)}, f32[1800,128]{1,0:T(8,128)}, u32[]{:S(2)}) copy-start(f32[1800,128]{1,0:T(8,128)} %get-tuple-element.73.x2) | copy-start | bytes 2764804 | tf_op jit(solution)/shard_map/cond
  73.9 8.2 %copy-start.10 = (f32[128,256]{1,0:T(8,128)S(1)}, f32[128,256]{1,0:T(8,128)}, u32[]{:S(2)}) copy-start(f32[128,256]{1,0:T(8,128)} %get-tuple-element.77.early_other) | copy-start | bytes 393220 | tf_op jit(solution)/shard_map/cond
  79.5 1.8 %collective-permute-start.1 = (f32[256,384]{1,0:T(8,128)S(1)}, f32[256,384]{1,0:T(8,128)S(1)}, u32[]{:S(2)}, u32[]{:S(2)}) collective-permute-start(f32[256,384]{1,0:T(8,128)S(1)} %get-tuple-element.69), channel_id=1, source_target_pairs={{0,1},{1,0},{2,3},{3,2},{4,5},{5,4},{6,7},{7,6},{8,9},{9,8},{10,11... | collective-permute-start | bytes 1179656 | tf_op jit(solution)/shard_map/cond/branch_1_fun/ppermute | solution.py:214
  81.3 8.0 %collective-permute-start.2 = (f32[128,384]{1,0:T(8,128)S(1)}, f32[128,384]{1,0:T(8,128)S(1)}, u32[]{:S(2)}, u32[]{:S(2)}) collective-permute-start(f32[128,384]{1,0:T(8,128)S(1)} %get-tuple-element.147), channel_id=1, source_target_pairs={{0,2},{1,3},{2,0},{3,1},{4,6},{5,7},{6,4},{7,5},{8,10},{9,11},{10,... | collective-permute-start | bytes 589832 | tf_op jit(solution)/shard_map/cond/branch_1_fun/ppermute | solution.py:214
  85.5 4.5 %collective-permute-start.3 = (f32[256,384]{1,0:T(8,128)S(1)}, f32[256,384]{1,0:T(8,128)S(1)}, u32[]{:S(2)}, u32[]{:S(2)}) collective-permute-start(f32[256,384]{1,0:T(8,128)S(1)} %get-tuple-element.83), channel_id=1, source_target_pairs={{0,1},{1,0},{2,3},{3,2},{4,5},{5,4},{6,7},{7,6},{8,9},{9,8},{10,11... | collective-permute-start | bytes 1179656 | tf_op jit(solution)/shard_map/cond/branch_1_fun/ppermute | solution.py:214
  90.1 7.0 %collective-permute-start.17 = (f32[128,384]{1,0:T(8,128)S(1)}, f32[128,384]{1,0:T(8,128)S(1)}, u32[]{:S(2)}, u32[]{:S(2)}) collective-permute-start(f32[128,384]{1,0:T(8,128)S(1)} %get-tuple-element.137), channel_id=1, source_target_pairs={{0,2},{1,3},{2,0},{3,1},{4,6},{5,7},{6,4},{7,5},{8,10},{9,11},{10,... | collective-permute-start | bytes 589832 | tf_op jit(solution)/shard_map/ppermute | solution.py:214
  91.6 9.9 %collective-permute-start.19 = (f32[128,384]{1,0:T(8,128)}, f32[128,384]{1,0:T(8,128)S(1)}, u32[]{:S(2)}, u32[]{:S(2)}) collective-permute-start(f32[128,384]{1,0:T(8,128)} %get-tuple-element.130), channel_id=1, source_target_pairs={{0,4},{1,5},{2,6},{3,7},{4,0},{5,1},{6,2},{7,3},{8,12},{9,13},{10,... | collective-permute-start | bytes 589832 | tf_op jit(solution)/shard_map/ppermute | solution.py:222
  94.4 7.2 %collective-permute-start.20 = (f32[128,384]{1,0:T(8,128)}, f32[128,384]{1,0:T(8,128)S(1)}, u32[]{:S(2)}, u32[]{:S(2)}) collective-permute-start(f32[128,384]{1,0:T(8,128)} %get-tuple-element.130), channel_id=1, source_target_pairs={{4,8},{5,9},{6,10},{7,11},{8,4},{9,5},{10,6},{11,7},{20,24},{21,25... | collective-permute-start | bytes 589832 | tf_op jit(solution)/shard_map/ppermute | solution.py:222
  96.9 2.7 %copy-start.12 = (s32[16,8]{0,1:T(8,128)S(1)}, s32[16,8]{0,1:T(8,128)}, u32[]{:S(2)}) copy-start(s32[16,8]{0,1:T(8,128)} %param.7) | copy-start | bytes 1540
  96.9 2.8 %copy-start.8 = (f32[128,896]{1,0:T(8,128)S(1)}, f32[128,896]{1,0:T(8,128)}, u32[]{:S(2)}) copy-start(f32[128,896]{1,0:T(8,128)} %copy-done.7) | copy-start | bytes 1376260
  96.9 1.6 %collective-permute-start.16 = (f32[256,256]{1,0:T(8,128)S(1)}, f32[256,256]{1,0:T(8,128)S(1)}, u32[]{:S(2)}, u32[]{:S(2)}) collective-permute-start(f32[256,256]{1,0:T(8,128)S(1)} %get-tuple-element.135), channel_id=1, source_target_pairs={{0,1},{1,0},{2,3},{3,2},{4,5},{5,4},{6,7},{7,6},{8,9},{9,8},{10,11... | collective-permute-start | bytes 786440 | tf_op jit(solution)/shard_map/ppermute | solution.py:214
  98.6 5.6 %collective-permute-start.18 = (f32[128,256]{1,0:T(8,128)S(1)}, f32[128,256]{1,0:T(8,128)S(1)}, u32[]{:S(2)}, u32[]{:S(2)}) collective-permute-start(f32[128,256]{1,0:T(8,128)S(1)} %slice_add_fusion.6), channel_id=1, source_target_pairs={{0,2},{1,3},{2,0},{3,1},{4,6},{5,7},{6,4},{7,5},{8,10},{9,11},{10,... | collective-permute-start | bytes 393224 | tf_op jit(solution)/shard_map/ppermute | solution.py:214
  (2 other events, 1.4 us)

commit v5 on v4

--- a/solution.py
+++ b/solution.py
@@ -23,7 +23,9 @@
         preferred_element_type=jnp.float32,
     )
     (ah, al), (bh, bl) = halves(a), halves(b)
-    return dot(ah, bh) + (dot(ah, bl) + dot(al, bh))
+    width = b.shape[1]
+    main = dot(ah, side_by_side(bh, bl))
+    return main[:, :width] + (main[:, width:] + dot(al, bh))
 
 
 def side_by_side(*values):
@@ -56,14 +58,37 @@
         ref[:, block(index, rows)] = jnp.zeros((ref.shape[0], rows), ref.dtype)
 
 
-def first_kernel(at_ref, own, x2, cx, x3, e0, o0, e1, o1, keep, other, send):
+def early_kernel(own, cx, x3, e0, o0, out):
+    mine = side_by_side(own[...], cx[...], x3[...])
+    out[...] = product(mine, side_by_side(mine, e0[...], o0[...]))
+
+
+def first_kernel(
+    at_ref, known, own, x2, cx, x3, e0, o0, e1, o1, keep, other, early_keep, early_other, send
+):
     k, flip = at_ref[0], at_ref[2] == 1
-    mine = side_by_side(own[...], x2[...], cx[...], x3[...])
-    out = product(mine, side_by_side(mine, e0[...], o0[...], e1[...], o1[...]))
-    first = jnp.where((k == 1) | (k == 2), 8, 7)
-    even = jnp.where(flip, first, 6)
-    place_columns(out, keep, other, send, (k, k ^ 2, k ^ 1, k ^ 3, 4, 5, even, 6 + first - even))
-    clear_column(keep, other, send, 15 - first)
+    rows = own.shape[1]
+    fresh = product(
+        side_by_side(own[...], x2[...], cx[...], x3[...]), side_by_side(x2[...], e1[...], o1[...])
+    )
+    beside = product(x2[...], side_by_side(e0[...], o0[...]))
+
+    def new(i, j):
+        return fresh[block(i, rows), block(j, rows)]
+
+    def line(i, j):
+        old = [known[block(j, rows), block(c, rows)] for c in range(5)]
+        return side_by_side(old[0], new(i, 0), *old[1:], new(i, 1), new(i, 2))
+
+    second = side_by_side(new(0, 0).T, new(1, 0), new(2, 0).T, new(3, 0).T, beside, new(1, 1), new(1, 2))
+    out = jnp.concatenate([line(0, 0), second, line(2, 1), line(3, 2)], 0)
+    first = jnp.where((k == 1) | (k == 2), 2, 1)
+    even = jnp.where(flip, first, 0)
+    near, far = (k, k ^ 2, k ^ 1, k ^ 3, 4, 5), (even, first - even)
+    cut = len(near) * rows
+    place_columns(out[:, :cut], keep, other, send, near)
+    place_columns(out[:, cut:], early_keep, early_other, send.at[:, cut:], far)
+    clear_column(early_keep, early_other, send.at[:, cut:], 3 - first)
 
 
 def copy_kernel(a, out):
@@ -103,10 +128,11 @@
     k, flip = at_ref[0], at_ref[2] == 1
     mine = side_by_side(own[...], x2[...], cx[...], x3[...])
     out = product(mine, side_by_side(e2[...], o2[...]))
-    last = jnp.where((k == 1) | (k == 2), 0, 1)
-    even = jnp.where(flip, last, 2)
-    place_columns(out, keep, other, send, (even, 2 + last - even))
-    clear_column(keep, other, send, 1 - last)
+    last = jnp.where((k == 1) | (k == 2), 1, 2)
+    even = jnp.where(flip, last, 3)
+    place_columns(out, keep, other, send, (even, 3 + last - even))
+    clear_column(keep, other, send, 0)
+    clear_column(keep, other, send, 3 - last)
     early = early_keep.shape[1]
     keep[:, :early] += early_keep[...]
     other[:, :early] += early_other[...]
@@ -149,12 +175,12 @@
     here, there = jnp.where(upper, high, low), jnp.where(upper, low, high)
     near = jnp.where(upper, 2, 1)
     this, that = 5 - flip, 4 + flip
-    write(here + near, (t1, this), (y2, 2))
-    write(there + near, (t1, that), (y2, 1))
-    write(here + 3 - near, (t2, 1), (y1, this))
-    write(there + 3 - near, (t2, 2), (y1, that))
-    write(jnp.where(upper, high, low + 3), (t2, 0), (y1, 6))
-    write(jnp.where(upper, low + 3, high), (t1, 6), (y2, 0))
+    write(here + near, (t1, this), (y2, 3))
+    write(there + near, (t1, that), (y2, 2))
+    write(here + 3 - near, (t2, 2), (y1, this))
+    write(there + 3 - near, (t2, 3), (y1, that))
+    write(jnp.where(upper, high, low + 3), (t2, 1), (y2, 0))
+    write(jnp.where(upper, low + 3, high), (t2, 0), (y2, 1))
 
 
 def final_kernel(reach, at_ref, pairs, k3, c3, y3, ez, oz, band, out, parts, sems):
@@ -222,7 +248,11 @@
         return lax.ppermute(value, "blk", route)
 
     def both(to_even, to_odd):
-        return along(to_even, 0), along(to_odd, 1)
+        second = along(to_odd, 1)
+        return along(to_even, 0), second
+
+    def f32(*shape):
+        return jax.ShapeDtypeStruct(shape, jnp.float32)
 
     quarters = fitted_slab.T.reshape(PLANE, depth, rows)
 
@@ -243,7 +273,8 @@
     near_outer = jnp.where(outer, own_a, cx_a)
     e1, o1 = both(jnp.where(flip, near_outer, x3_a), jnp.where(flip, x3_a, near_outer))
 
-    own_b, cx_b, x3_b, x2_b, _, _ = lax.optimization_barrier((own_a, cx_a, x3_a, x2, e0, o0))
+    known = call(early_kernel, [f32(3 * rows, 5 * rows)], [], (), (own, cx, x3, e0, o0))[0]
+    own_b, cx_b, x3_b, x2_b, _ = lax.optimization_barrier((own_a, cx_a, x3_a, x2, known))
     far_inner = jnp.where(outer, x2_b, x3_b)
     e2, o2 = both(jnp.where(flip, far_inner, x2_b), jnp.where(flip, x2_b, far_inner))
 
@@ -252,9 +283,6 @@
     far_outer = jnp.where(outer, x3_c, x2_c)
     e3, o3 = both(jnp.where(flip, far_outer, near_outer), jnp.where(flip, near_outer, far_outer))
 
-    def f32(*shape):
-        return jax.ShapeDtypeStruct(shape, jnp.float32)
-
     def parts(n):
         return [f32(rows, n * rows), f32(rows, n * rows), f32(2 * rows, n * rows)]
 
@@ -273,11 +301,14 @@
     mine = (own, x2, cx, x3)
 
     def first_part(place, *operands):
-        total, out = core_sum(*call(first_kernel, parts(9), [], (place,), operands))
-        cut = 7 * rows
-        return total[:, :cut], out[:, :cut], total[:, cut:], out[:, cut:]
-
-    t1, out1, *early = fenced(first_part, place, *mine, e0, o0, e1, o1)
+        near, far, cut = parts(PLANE + 2), parts(3), (PLANE + 2) * rows
+        outs = near[:2] + far[:2] + [f32(2 * rows, 9 * rows)]
+        *kept, send = call(first_kernel, outs, [], (place,), operands)
+        core = xor(send, 1)
+        corner = core[:rows, :cut], core[rows:, :cut], core[:rows, cut:], core[rows:, cut:]
+        return tuple(a + b for a, b in zip(kept, corner))
+
+    t1, out1, *early = fenced(first_part, place, known, *mine, e0, o0, e1, o1)
     y1 = xor(out1, 2)
 
     def second_part(place, own, x2, cx, x3, early_keep, early_other, *arrived):
@@ -286,7 +317,7 @@
         half, out = core_sum(keep, other, send)
         far = xor(out, 2)
         place = after(place, out)
-        k2, other, send = call(second_kernel, parts(3), [], (place,), (own, x2, cx, x3, *arrived[4:], early_keep, early_other))
+        k2, other, send = call(second_kernel, parts(4), [], (place,), (own, x2, cx, x3, *arrived[4:], early_keep, early_other))
         turned = [jax.ShapeDtypeStruct((PLANE * rows, depth), jnp.bfloat16)] * 2
         high, low = call(turn_kernel, turned, [], (), (after(own, k2), x2, cx, x3))
         half = after(half, high)
@@ -300,7 +331,7 @@
     e3, o3, _, _ = lax.optimization_barrier((e3, o3, pack, y1))
     k3, other, send = call(third_kernel, parts(2), [], (), (high, low, e3, o3))
     c3 = xor(send, 1)
-    y2 = call(copy_kernel, [f32(rows, 3 * rows)], [], (), (y2,), flops=5 * 10**9)[0]
+    y2 = call(copy_kernel, [f32(rows, 4 * rows)], [], (), (y2,), flops=5 * 10**9)[0]
     y3 = xor(after(other + c3[rows:], y2), 2)
 
     whole = f32(rows, (2 * reach + 1) * rows)

time: 106 us -> 106 us (level)
  waiting for transfers between devices: 42.3 us -> 37.9 us
  starting transfers between devices: 26.1 us -> 27.9 us
  Pallas kernels: 25.5 us -> 26.6 us
    ppermute x11, waiting for transfers between devices: 42.3 us -> 36.8 us  [xor(): return lax.ppermute(value, 'blk', [(i, i ^ t) for i in devices])]
    pallas_call x8 -> x9, Pallas kernels: 24 us -> 25.2 us  [call(): pl.pallas_call(kernel, cost_estimate=pl.CostEstimate(flops=flops, bytes_a...]
    ppermute x10, waiting for transfers between devices: 0.03 us -> 1.15 us  [along(): return lax.ppermute(value, 'blk', route)]
    ppermute x10, starting transfers between devices: 16.4 us -> 17.5 us  [along(): return lax.ppermute(value, 'blk', route)]
  transfers between devices with their start and end apart: 21 -> 21, of which waited for: 7 -> 9; matrix products, arithmetic and copies ran while one was open for 7% -> 8% of each run, Pallas kernels for 23% -> 24%
where the time goes in v5:
time: 106 us; the launch traced here: 105 us
  waiting for transfers between devices  37.9 us (36%)
  starting transfers between devices  27.9 us (26%)
  Pallas kernels  26.6 us (25%)
  local copies, waits for them, and re-layouts  6.28 us (6%)
  other arithmetic  5.86 us (6%)
    ppermute x11, waiting for transfers between devices, xor(): return lax.ppermute(value, 'blk', [(i, i ^ t) for i in devices])  36.8 us
    pallas_call x9, Pallas kernels, call(): pl.pallas_call(kernel, cost_estimate=pl.CostEstimate(flops=flops, bytes_a...  25.2 us
    ppermute x10, starting transfers between devices, along(): return lax.ppermute(value, 'blk', route)  17.5 us
    ppermute x11, starting transfers between devices, xor(): return lax.ppermute(value, 'blk', [(i, i ^ t) for i in devices])  10.4 us
    squeeze x3, local copies, waits for them, and re-layouts, quarter(): lax.dynamic_index_in_dim(after(quarters, *others), index, 0, keepdims=False)  4.65 us
  transfers between devices with their start and end apart: 21, of which 9 were waited for; matrix products, arithmetic and copies ran while one was open for 8% of the time, Pallas kernels for 24%

profile of v5, /device:TPU:0, one launch (start us, length us, event | category | flops | bytes accessed | tf_op | source)
XLA Modules:
  0.0 105.1 jit_solution(1785112806547680587)
XLA Ops:
  0.0 2.2 %dynamic-slice_bitcast_fusion.3 = f32[1800,128]{1,0:T(8,128)} fusion(f32[4,1800,128]{2,1,0:T(8,128)} %bitcast.16, s32[]{:T(128)S(6)} %select_n.82), kind=kLoop, calls=%fused_computation.13 | loop fusion | bytes 1843204 | tf_op jit(solution)/shard_map/jit(dynamic_index_in_dim)/squeeze | solution.py:260
  2.6 1.2 %dynamic-slice_bitcast_fusion.1 = f32[1800,128]{1,0:T(8,128)S(1)} fusion(f32[4,1800,128]{2,1,0:T(8,128)} %bitcast.17, s32[]{:T(128)S(6)} %select_n.86), kind=kLoop, calls=%fused_computation.11 | loop fusion | bytes 1843204 | tf_op jit(solution)/shard_map/jit(dynamic_index_in_dim)/squeeze | solution.py:260
  3.9 2.7 %collective-permute-start.7 = (f32[1800,128]{1,0:T(8,128)S(1)}, f32[1800,128]{1,0:T(8,128)S(1)}, u32[]{:S(2)}, u32[]{:S(2)}) collective-permute-start(f32[1800,128]{1,0:T(8,128)S(1)} %dynamic-slice_bitcast_fusion.1), channel_id=1, source_target_pairs={{0,3},{1,2},{2,1},{3,0},{4,7},{5,6},{6,5},{7,4},{8,11},{9,10},{10,... | collective-permute-start | bytes 2764808 | tf_op jit(solution)/shard_map/ppermute | solution.py:240
  6.6 1.3 %broadcast_select_fusion.7 = (f32[1800,128]{1,0:T(8,128)S(1)}, f32[1800,128]{1,0:T(8,128)S(1)}) fusion(f32[1800,128]{1,0:T(8,128)S(1)} %collective-permute-done.4.cx, pred[]{:T(512)S(6)} %or.3, f32[4,1800,128]{2,1,0:T(8,128)} %bitcast.18, s32[]{:T(128)S(6)} %select_n.83), kind=kLoop, calls=%fused_computation.21 | loop fusion | flops 230400 | bytes 3686405 | tf_op jit(solution)/shard_map/jit(_where)/select_n | solution.py:267
  7.9 1.6 %collective-permute-start.5 = (f32[1800,128]{1,0:T(8,128)S(1)}, f32[1800,128]{1,0:T(8,128)S(1)}, u32[]{:S(2)}, u32[]{:S(2)}) collective-permute-start(f32[1800,128]{1,0:T(8,128)S(1)} %get-tuple-element.146), channel_id=1, source_target_pairs={{0,4},{1,5},{2,6},{3,7},{4,0},{5,1},{6,2},{7,3},{8,12},{9,13},{10,... | collective-permute-start | bytes 2764808 | tf_op jit(solution)/shard_map/ppermute | solution.py:248
  10.2 1.2 %dynamic-slice_bitcast_fusion = f32[1800,128]{1,0:T(8,128)S(1)} fusion(f32[4,1800,128]{2,1,0:T(8,128)} %bitcast.19, s32[]{:T(128)S(6)} %select_n.87), kind=kLoop, calls=%fused_computation.10 | loop fusion | bytes 1843204 | tf_op jit(solution)/shard_map/jit(dynamic_index_in_dim)/squeeze | solution.py:260
  11.5 1.3 %collective-permute-start.10 = (f32[1800,128]{1,0:T(8,128)S(1)}, f32[1800,128]{1,0:T(8,128)S(1)}, u32[]{:S(2)}, u32[]{:S(2)}) collective-permute-start(f32[1800,128]{1,0:T(8,128)S(1)} %dynamic-slice_bitcast_fusion), channel_id=1, source_target_pairs={{0,2},{1,3},{2,0},{3,1},{4,6},{5,7},{6,4},{7,5},{8,10},{9,11},{10,... | collective-permute-start | bytes 2764808 | tf_op jit(solution)/shard_map/ppermute | solution.py:240
  12.8 14.6 %collective-permute-done.7.x3 = f32[1800,128]{1,0:T(8,128)S(1)} collective-permute-done((f32[1800,128]{1,0:T(8,128)S(1)}, f32[1800,128]{1,0:T(8,128)S(1)}, u32[]{:S(2)}, u32[]{:S(2)}) %collective-permute-start.7) | collective-permute-done | bytes 921632 | tf_op jit(solution)/shard_map/ppermute | solution.py:240
  27.6 1.6 %collective-permute-start.8 = (f32[1800,128]{1,0:T(8,128)S(1)}, f32[1800,128]{1,0:T(8,128)S(1)}, u32[]{:S(2)}, u32[]{:S(2)}) collective-permute-start(f32[1800,128]{1,0:T(8,128)S(1)} %get-tuple-element.159), channel_id=1, source_target_pairs={{0,4},{1,5},{2,6},{3,7},{4,0},{5,1},{6,2},{7,3},{8,12},{9,13},{10,... | collective-permute-start | bytes 2764808 | tf_op jit(solution)/shard_map/ppermute | solution.py:248
  30.3 4.5 %shard_map.28 = f32[384,640]{1,0:T(8,128)} custom-call(f32[1800,128]{1,0:T(8,128)S(1)} %get-tuple-element.133.own, f32[1800,128]{1,0:T(8,128)S(1)} %collective-permute-done.4.cx, f32[1800,128]{1,0:T(8,128)S(1)} %collective-permute-done.7.x3, f32[1800,128]{1,0:T(8,128)S(1)} %collective-permute-done.5.e0, f32[1800,128]{1,0:T(8,128)S(1)} %collective-permute-done.6.o0), custom_call_target="tpu_custom_call" | custom-call | flops 1000 | bytes 4608000 | tf_op jit(solution)/shard_map/pallas_call | solution.py:210
  34.8 12.5 %collective-permute-done.10 = f32[1800,128]{1,0:T(8,128)S(1)} collective-permute-done((f32[1800,128]{1,0:T(8,128)S(1)}, f32[1800,128]{1,0:T(8,128)S(1)}, u32[]{:S(2)}, u32[]{:S(2)}) %collective-permute-start.10) | collective-permute-done | bytes 921632 | tf_op jit(solution)/shard_map/ppermute | solution.py:240
  47.3 1.5 %select_select_fusion = (f32[1800,128]{1,0:T(8,128)}, f32[1800,128]{1,0:T(8,128)}) fusion(f32[1800,128]{1,0:T(8,128)S(1)} %collective-permute-done.10, f32[1800,128]{1,0:T(8,128)S(1)} %collective-permute-done.7.x3, pred[]{:T(512)S(6)} %xor.12, pred[]{:T(512)S(6)} %or.3), kind=kLoop, calls=%fused_computation.8 | loop fusion | flops 691200 | bytes 3686402 | tf_op jit(solution)/shard_map/jit(_where)/select_n | solution.py:279
  48.8 1.7 %collective-permute-start.11 = (f32[1800,128]{1,0:T(8,128)}, f32[1800,128]{1,0:T(8,128)}, u32[]{:S(2)}, u32[]{:S(2)}) collective-permute-start(f32[1800,128]{1,0:T(8,128)} %get-tuple-element.161), channel_id=1, source_target_pairs={{0,4},{1,5},{2,6},{3,7},{4,0},{5,1},{6,2},{7,3},{8,12},{9,13},{10,... | collective-permute-start | bytes 2764808 | tf_op jit(solution)/shard_map/ppermute | solution.py:248
  50.5 1.6 %collective-permute-start.12 = (f32[1800,128]{1,0:T(8,128)}, f32[1800,128]{1,0:T(8,128)}, u32[]{:S(2)}, u32[]{:S(2)}) collective-permute-start(f32[1800,128]{1,0:T(8,128)} %get-tuple-element.160), channel_id=1, source_target_pairs={{4,8},{5,9},{6,10},{7,11},{8,4},{9,5},{10,6},{11,7},{20,24},{21,25... | collective-permute-start | bytes 2764808 | tf_op jit(solution)/shard_map/ppermute | solution.py:248
  52.1 1.7 %broadcast_select_fusion = (f32[1800,128]{1,0:T(8,128)}, f32[1800,128]{1,0:T(8,128)}) fusion(pred[]{:T(512)S(6)} %xor.12, f32[1800,128]{1,0:T(8,128)S(1)} %collective-permute-done.7.x3, f32[1800,128]{1,0:T(8,128)S(1)} %collective-permute-done.10, pred[]{:T(512)S(6)} %or.3, f32[1800,128]{1,0:T(8,128)S(1)} %get-tuple-element.133.own, ...), kind=kLoop, calls=%fused_computation.14 | loop fusion | flops 921600 | bytes 5529602 | tf_op jit(solution)/shard_map/jit(_where)/select_n | solution.py:284
  54.0 3.4 %collective-permute-start.13 = (f32[1800,128]{1,0:T(8,128)}, f32[1800,128]{1,0:T(8,128)S(1)}, u32[]{:S(2)}, u32[]{:S(2)}) collective-permute-start(f32[1800,128]{1,0:T(8,128)} %get-tuple-element.157), channel_id=1, source_target_pairs={{0,4},{1,5},{2,6},{3,7},{4,0},{5,1},{6,2},{7,3},{8,12},{9,13},{10,... | collective-permute-start | bytes 2764808 | tf_op jit(solution)/shard_map/ppermute | solution.py:248
  58.4 10.4 %conditional.2 = (f32[128,768]{1,0:T(8,128)S(1)}, f32[128,768]{1,0:T(8,128)}, f32[128,384]{1,0:T(8,128)S(1)}, f32[128,384]{1,0:T(8,128)S(1)}) conditional(s32[]{:T(128)} %convert_element_type.2, () %tuple.36, (s32[4]{0:T(128)S(1)}, f32[384,640]{1,0:T(8,128)}, f32[1800,128]{1,0:T(8,128)}, f32[1800,128]{1,0:T(8,128)}, f32[1800,128]{1,0:T(8,128)S(1)}, ...), branch_computations={%region_0.1_spmd, %region_1.2_spmd} | conditional | flops 295912 | bytes 16613448 | solution.py:299
  58.4 6.5 %branch_1_fun.5 = (f32[128,768]{1,0:T(8,128)S(1)}, f32[128,768]{1,0:T(8,128)S(1)}, f32[128,384]{1,0:T(8,128)S(1)}, f32[128,384]{1,0:T(8,128)S(1)}, f32[256,1152]{1,0:T(8,128)S(1)}) custom-call(s32[4]{0:T(128)S(1)} %get-tuple-element.51.at_ref, f32[384,640]{1,0:T(8,128)} %get-tuple-element.52.known, f32[1800,128]{1,0:T(8,128)} %get-tuple-element.53.own, ...), custom_call_target="tpu_custom_call" | custom-call | flops 1000 | bytes 8355840 | tf_op jit(solution)/shard_map/cond/branch_1_fun/pallas_call | solution.py:210
  65.0 2.8 %collective-permute-done = f32[256,1152]{1,0:T(8,128)S(1)} collective-permute-done((f32[256,1152]{1,0:T(8,128)S(1)}, f32[256,1152]{1,0:T(8,128)S(1)}, u32[]{:S(2)}, u32[]{:S(2)}) %collective-permute-start) | collective-permute-done | bytes 1179680 | tf_op jit(solution)/shard_map/cond/branch_1_fun/ppermute | solution.py:240
  70.1 1.5 %collective-permute-start.15 = (f32[128,768]{1,0:T(8,128)}, f32[128,768]{1,0:T(8,128)S(1)}, u32[]{:S(2)}, u32[]{:S(2)}) collective-permute-start(f32[128,768]{1,0:T(8,128)} %get-tuple-element.136), channel_id=1, source_target_pairs={{0,2},{1,3},{2,0},{3,1},{4,6},{5,7},{6,4},{7,5},{8,10},{9,11},{10,... | collective-permute-start | bytes 1179656 | tf_op jit(solution)/shard_map/ppermute | solution.py:240
  72.4 14.9 %conditional.3 = (f32[128,384]{1,0:T(8,128)}, bf16[512,1800]{1,0:T(8,128)(2,1)S(1)}, bf16[512,1800]{1,0:T(8,128)(2,1)S(1)}, f32[128,512]{1,0:T(8,128)S(1)}, f32[128,512]{1,0:T(8,128)S(1)}) conditional(s32[]{:T(128)} %convert_element_type.2, () %tuple.31, (s32[4]{0:T(128)S(1)}, f32[1800,128]{1,0:T(8,128)}, f32[1800,128]{1,0:T(8,128)}, ...), branch_computations={%region_2.3_spmd, %region_3.4_spmd} | conditional | flops 100000227328 | bytes 35373356 | solution.py:299
  72.4 5.2 %branch_1_fun.6 = (f32[128,384]{1,0:T(8,128)S(1)}, f32[128,384]{1,0:T(8,128)S(1)}, f32[256,384]{1,0:T(8,128)S(1)}) custom-call(s32[4]{0:T(128)S(1)} %get-tuple-element.77.at_ref, f32[1800,128]{1,0:T(8,128)} %get-tuple-element.67.e0, f32[1800,128]{1,0:T(8,128)} %get-tuple-element.68.o0, f32[1800,128]{1,0:T(8,128)} %get-tuple-element.69.e1, ...), custom_call_target="tpu_custom_call" | custom-call | flops 1000 | bytes 5529600 | tf_op jit(solution)/shard_map/cond/branch_1_fun/pallas_call | solution.py:210
  77.7 1.7 %collective-permute-done.1 = f32[256,384]{1,0:T(8,128)S(1)} collective-permute-done((f32[256,384]{1,0:T(8,128)S(1)}, f32[256,384]{1,0:T(8,128)S(1)}, u32[]{:S(2)}, u32[]{:S(2)}) %collective-permute-start.1) | collective-permute-done | bytes 393248 | tf_op jit(solution)/shard_map/cond/branch_1_fun/ppermute | solution.py:240
  79.5 1.8 %collective-permute-start.2 = (f32[128,384]{1,0:T(8,128)S(1)}, f32[128,384]{1,0:T(8,128)S(1)}, u32[]{:S(2)}, u32[]{:S(2)}) collective-permute-start(f32[128,384]{1,0:T(8,128)S(1)} %get-tuple-element.154), channel_id=1, source_target_pairs={{0,2},{1,3},{2,0},{3,1},{4,6},{5,7},{6,4},{7,5},{8,10},{9,11},{10,... | collective-permute-start | bytes 589832 | tf_op jit(solution)/shard_map/cond/branch_1_fun/ppermute | solution.py:240
  81.3 3.4 %branch_1_fun.7 = (f32[128,512]{1,0:T(8,128)S(1)}, f32[128,512]{1,0:T(8,128)S(1)}, f32[256,512]{1,0:T(8,128)S(1)}) custom-call(s32[4]{0:T(128)S(1)} %get-tuple-element.77.at_ref, f32[1800,128]{1,0:T(8,128)S(1)} %copy-done.3, f32[1800,128]{1,0:T(8,128)S(1)} %copy-done.5, f32[1800,128]{1,0:T(8,128)S(1)} %get-tuple-element.79.cx, f32[1800,128]{1,0:T(8,128)S(1)} %copy-done.1, ...), custom_call_target="tpu_custom_call" | custom-call | flops 1000 | bytes 5922816 | tf_op jit(solution)/shard_map/cond/branch_1_fun/pallas_call | solution.py:210
  87.3 1.8 %collective-permute-start.17 = (f32[128,512]{1,0:T(8,128)S(1)}, f32[128,512]{1,0:T(8,128)S(1)}, u32[]{:S(2)}, u32[]{:S(2)}) collective-permute-start(f32[128,512]{1,0:T(8,128)S(1)} %get-tuple-element.142), channel_id=1, source_target_pairs={{0,2},{1,3},{2,0},{3,1},{4,6},{5,7},{6,4},{7,5},{8,10},{9,11},{10,... | collective-permute-start | bytes 786440 | tf_op jit(solution)/shard_map/ppermute | solution.py:240
  89.1 4.6 %collective-permute-start.19 = (f32[128,384]{1,0:T(8,128)}, f32[128,384]{1,0:T(8,128)S(1)}, u32[]{:S(2)}, u32[]{:S(2)}) collective-permute-start(f32[128,384]{1,0:T(8,128)} %get-tuple-element.135), channel_id=1, source_target_pairs={{0,4},{1,5},{2,6},{3,7},{4,0},{5,1},{6,2},{7,3},{8,12},{9,13},{10,... | collective-permute-start | bytes 589832 | tf_op jit(solution)/shard_map/ppermute | solution.py:248
  94.3 1.8 %shard_map.29 = (f32[128,256]{1,0:T(8,128)S(1)}, f32[128,256]{1,0:T(8,128)S(1)}, f32[256,256]{1,0:T(8,128)S(1)}) custom-call(bf16[512,1800]{1,0:T(8,128)(2,1)S(1)} %get-tuple-element.127.high, bf16[512,1800]{1,0:T(8,128)(2,1)S(1)} %get-tuple-element.128.low, f32[1800,128]{1,0:T(8,128)S(1)} %collective-permute-done.13.e3, ...), custom_call_target="tpu_custom_call" | custom-call | flops 1000 | bytes 9216000 | tf_op jit(solution)/shard_map/pallas_call | solution.py:210
  96.3 1.5 %collective-permute-done.16.c3 = f32[256,256]{1,0:T(8,128)S(1)} collective-permute-done((f32[256,256]{1,0:T(8,128)S(1)}, f32[256,256]{1,0:T(8,128)S(1)}, u32[]{:S(2)}, u32[]{:S(2)}) %collective-permute-start.16) | collective-permute-done | bytes 262176 | tf_op jit(solution)/shard_map/ppermute | solution.py:240
  98.5 1.9 %shard_map.31.band = f32[128,1920]{1,0:T(8,128)} custom-call(s32[4]{0:T(128)S(1)} %pad_add_fusion.at_ref, s32[16,8]{1,0:T(8,128)S(1)} %copy.5.pairs, f32[128,768]{1,0:T(8,128)S(1)} %get-tuple-element.144.t1, f32[128,768]{1,0:T(8,128)S(1)} %collective-permute-done.15.y1, f32[128,512]{1,0:T(8,128)S(1)} %copy-done.11, f32[128,512]{1,0:T(8,128)S(1)} %shard_map.30.y2), custom_call_target="tpu_custom_call" | custom-call | flops 1000 | bytes 1310720 | tf_op jit(solution)/shard_map/pallas_call | solution.py:210
  100.4 3.1 %collective-permute-done.18.y3 = f32[128,256]{1,0:T(8,128)S(1)} collective-permute-done((f32[128,256]{1,0:T(8,128)S(1)}, f32[128,256]{1,0:T(8,128)S(1)}, u32[]{:S(2)}, u32[]{:S(2)}) %collective-permute-start.18) | collective-permute-done | bytes 131104 | tf_op jit(solution)/shard_map/ppermute | solution.py:240
  103.4 1.5 %shard_map.32 = f32[128,1920]{1,0:T(8,128)} custom-call(s32[4]{0:T(128)S(1)} %pad_add_fusion.at_ref, s32[16,8]{1,0:T(8,128)S(1)} %copy.5.pairs, f32[128,256]{1,0:T(8,128)S(1)} %get-tuple-element.139.k3, f32[256,256]{1,0:T(8,128)S(1)} %collective-permute-done.16.c3, f32[128,256]{1,0:T(8,128)S(1)} %collective-permute-done.18.y3, ...), custom_call_target="tpu_custom_call", output_to_operand_aliasing={{}: (7, {})} | custom-call | tf_op jit(solution)/shard_map/pallas_call | solution.py:340
  (70 shorter events, 10.8 us)
Async XLA Ops:
  2.2 4.4 %collective-permute-start.4 = (f32[1800,128]{1,0:T(8,128)}, f32[1800,128]{1,0:T(8,128)S(1)}, u32[]{:S(2)}, u32[]{:S(2)}) collective-permute-start(f32[1800,128]{1,0:T(8,128)} %dynamic-slice_bitcast_fusion.3), channel_id=1, source_target_pairs={{0,1},{1,0},{2,3},{3,2},{4,5},{5,4},{6,7},{7,6},{8,9},{9,8},{10,11... | collective-permute-start | bytes 2764808 | tf_op jit(solution)/shard_map/ppermute | solution.py:240
  3.9 23.5 %collective-permute-start.7 = (f32[1800,128]{1,0:T(8,128)S(1)}, f32[1800,128]{1,0:T(8,128)S(1)}, u32[]{:S(2)}, u32[]{:S(2)}) collective-permute-start(f32[1800,128]{1,0:T(8,128)S(1)} %dynamic-slice_bitcast_fusion.1), channel_id=1, source_target_pairs={{0,3},{1,2},{2,1},{3,0},{4,7},{5,6},{6,5},{7,4},{8,11},{9,10},{10,... | collective-permute-start | bytes 2764808 | tf_op jit(solution)/shard_map/ppermute | solution.py:240
  7.9 44.2 %copy-start.2 = (f32[1800,128]{1,0:T(8,128)}, f32[1800,128]{1,0:T(8,128)S(1)}, u32[]{:S(2)}) copy-start(f32[1800,128]{1,0:T(8,128)S(1)} %get-tuple-element.133.own) | copy-start | bytes 2764804
  7.9 22.4 %collective-permute-start.5 = (f32[1800,128]{1,0:T(8,128)S(1)}, f32[1800,128]{1,0:T(8,128)S(1)}, u32[]{:S(2)}, u32[]{:S(2)}) collective-permute-start(f32[1800,128]{1,0:T(8,128)S(1)} %get-tuple-element.146), channel_id=1, source_target_pairs={{0,4},{1,5},{2,6},{3,7},{4,0},{5,1},{6,2},{7,3},{8,12},{9,13},{10,... | collective-permute-start | bytes 2764808 | tf_op jit(solution)/shard_map/ppermute | solution.py:248
  9.5 20.8 %collective-permute-start.6 = (f32[1800,128]{1,0:T(8,128)S(1)}, f32[1800,128]{1,0:T(8,128)S(1)}, u32[]{:S(2)}, u32[]{:S(2)}) collective-permute-start(f32[1800,128]{1,0:T(8,128)S(1)} %get-tuple-element.146), channel_id=1, source_target_pairs={{4,8},{5,9},{6,10},{7,11},{8,4},{9,5},{10,6},{11,7},{20,24},{21,25... | collective-permute-start | bytes 2764808 | tf_op jit(solution)/shard_map/ppermute | solution.py:248
  11.5 35.8 %collective-permute-start.10 = (f32[1800,128]{1,0:T(8,128)S(1)}, f32[1800,128]{1,0:T(8,128)S(1)}, u32[]{:S(2)}, u32[]{:S(2)}) collective-permute-start(f32[1800,128]{1,0:T(8,128)S(1)} %dynamic-slice_bitcast_fusion), channel_id=1, source_target_pairs={{0,2},{1,3},{2,0},{3,1},{4,6},{5,7},{6,4},{7,5},{8,10},{9,11},{10,... | collective-permute-start | bytes 2764808 | tf_op jit(solution)/shard_map/ppermute | solution.py:240
  27.4 24.7 %copy-start = (f32[1800,128]{1,0:T(8,128)}, f32[1800,128]{1,0:T(8,128)S(1)}, u32[]{:S(2)}) copy-start(f32[1800,128]{1,0:T(8,128)S(1)} %collective-permute-done.7.x3) | copy-start | bytes 2764804
  27.6 24.5 %collective-permute-start.8 = (f32[1800,128]{1,0:T(8,128)S(1)}, f32[1800,128]{1,0:T(8,128)S(1)}, u32[]{:S(2)}, u32[]{:S(2)}) collective-permute-start(f32[1800,128]{1,0:T(8,128)S(1)} %get-tuple-element.159), channel_id=1, source_target_pairs={{0,4},{1,5},{2,6},{3,7},{4,0},{5,1},{6,2},{7,3},{8,12},{9,13},{10,... | collective-permute-start | bytes 2764808 | tf_op jit(solution)/shard_map/ppermute | solution.py:248
  29.2 22.9 %collective-permute-start.9 = (f32[1800,128]{1,0:T(8,128)S(1)}, f32[1800,128]{1,0:T(8,128)S(1)}, u32[]{:S(2)}, u32[]{:S(2)}) collective-permute-start(f32[1800,128]{1,0:T(8,128)S(1)} %get-tuple-element.158), channel_id=1, source_target_pairs={{4,8},{5,9},{6,10},{7,11},{8,4},{9,5},{10,6},{11,7},{20,24},{21,25... | collective-permute-start | bytes 2764808 | tf_op jit(solution)/shard_map/ppermute | solution.py:248
  30.3 4.5 %copy-start.6 = (f32[1800,128]{1,0:T(8,128)}, f32[1800,128]{1,0:T(8,128)S(1)}, u32[]{:S(2)}) copy-start(f32[1800,128]{1,0:T(8,128)S(1)} %collective-permute-done.5.e0) | copy-start | bytes 2764804
  30.3 4.5 %copy-start.7 = (f32[1800,128]{1,0:T(8,128)}, f32[1800,128]{1,0:T(8,128)S(1)}, u32[]{:S(2)}) copy-start(f32[1800,128]{1,0:T(8,128)S(1)} %collective-permute-done.6.o0) | copy-start | bytes 2764804
  47.3 6.5 %copy-start.4 = (f32[1800,128]{1,0:T(8,128)}, f32[1800,128]{1,0:T(8,128)S(1)}, u32[]{:S(2)}) copy-start(f32[1800,128]{1,0:T(8,128)S(1)} %collective-permute-done.10) | copy-start | bytes 2764804
  48.8 23.6 %collective-permute-start.11 = (f32[1800,128]{1,0:T(8,128)}, f32[1800,128]{1,0:T(8,128)}, u32[]{:S(2)}, u32[]{:S(2)}) collective-permute-start(f32[1800,128]{1,0:T(8,128)} %get-tuple-element.161), channel_id=1, source_target_pairs={{0,4},{1,5},{2,6},{3,7},{4,0},{5,1},{6,2},{7,3},{8,12},{9,13},{10,... | collective-permute-start | bytes 2764808 | tf_op jit(solution)/shard_map/ppermute | solution.py:248
  50.5 21.9 %collective-permute-start.12 = (f32[1800,128]{1,0:T(8,128)}, f32[1800,128]{1,0:T(8,128)}, u32[]{:S(2)}, u32[]{:S(2)}) collective-permute-start(f32[1800,128]{1,0:T(8,128)} %get-tuple-element.160), channel_id=1, source_target_pairs={{4,8},{5,9},{6,10},{7,11},{8,4},{9,5},{10,6},{11,7},{20,24},{21,25... | collective-permute-start | bytes 2764808 | tf_op jit(solution)/shard_map/ppermute | solution.py:248
  54.0 40.3 %collective-permute-start.13 = (f32[1800,128]{1,0:T(8,128)}, f32[1800,128]{1,0:T(8,128)S(1)}, u32[]{:S(2)}, u32[]{:S(2)}) collective-permute-start(f32[1800,128]{1,0:T(8,128)} %get-tuple-element.157), channel_id=1, source_target_pairs={{0,4},{1,5},{2,6},{3,7},{4,0},{5,1},{6,2},{7,3},{8,12},{9,13},{10,... | collective-permute-start | bytes 2764808 | tf_op jit(solution)/shard_map/ppermute | solution.py:248
  57.4 36.9 %collective-permute-start.14 = (f32[1800,128]{1,0:T(8,128)}, f32[1800,128]{1,0:T(8,128)S(1)}, u32[]{:S(2)}, u32[]{:S(2)}) collective-permute-start(f32[1800,128]{1,0:T(8,128)} %get-tuple-element.156), channel_id=1, source_target_pairs={{4,8},{5,9},{6,10},{7,11},{8,4},{9,5},{10,6},{11,7},{20,24},{21,25... | collective-permute-start | bytes 2764808 | tf_op jit(solution)/shard_map/ppermute | solution.py:248
  64.9 2.9 %collective-permute-start = (f32[256,1152]{1,0:T(8,128)S(1)}, f32[256,1152]{1,0:T(8,128)S(1)}, u32[]{:S(2)}, u32[]{:S(2)}) collective-permute-start(f32[256,1152]{1,0:T(8,128)S(1)} %get-tuple-element.62), channel_id=1, source_target_pairs={{0,1},{1,0},{2,3},{3,2},{4,5},{5,4},{6,7},{7,6},{8,9},{9,8},{10,11... | collective-permute-start | bytes 3538952 | tf_op jit(solution)/shard_map/cond/branch_1_fun/ppermute | solution.py:240
  70.1 23.5 %collective-permute-start.15 = (f32[128,768]{1,0:T(8,128)}, f32[128,768]{1,0:T(8,128)S(1)}, u32[]{:S(2)}, u32[]{:S(2)}) collective-permute-start(f32[128,768]{1,0:T(8,128)} %get-tuple-element.136), channel_id=1, source_target_pairs={{0,2},{1,3},{2,0},{3,1},{4,6},{5,7},{6,4},{7,5},{8,10},{9,11},{10,... | collective-permute-start | bytes 1179656 | tf_op jit(solution)/shard_map/ppermute | solution.py:240
  72.4 8.8 %copy-start.1 = (f32[1800,128]{1,0:T(8,128)S(1)}, f32[1800,128]{1,0:T(8,128)}, u32[]{:S(2)}) copy-start(f32[1800,128]{1,0:T(8,128)} %get-tuple-element.80.x3) | copy-start | bytes 2764804 | tf_op jit(solution)/shard_map/cond
  72.4 8.8 %copy-start.3 = (f32[1800,128]{1,0:T(8,128)S(1)}, f32[1800,128]{1,0:T(8,128)}, u32[]{:S(2)}) copy-start(f32[1800,128]{1,0:T(8,128)} %get-tuple-element.84.own) | copy-start | bytes 2764804 | tf_op jit(solution)/shard_map/cond
  72.4 8.8 %copy-start.5 = (f32[1800,128]{1,0:T(8,128)S(1)}, f32[1800,128]{1,0:T(8,128)}, u32[]{:S(2)}) copy-start(f32[1800,128]{1,0:T(8,128)} %get-tuple-element.78.x2) | copy-start | bytes 2764804 | tf_op jit(solution)/shard_map/cond
  72.4 8.8 %copy-start.13 = (f32[128,384]{1,0:T(8,128)S(1)}, f32[128,384]{1,0:T(8,128)}, u32[]{:S(2)}) copy-start(f32[128,384]{1,0:T(8,128)} %get-tuple-element.81.early_keep) | copy-start | bytes 589828 | tf_op jit(solution)/shard_map/cond
  72.4 8.8 %copy-start.15 = (f32[128,384]{1,0:T(8,128)S(1)}, f32[128,384]{1,0:T(8,128)}, u32[]{:S(2)}) copy-start(f32[128,384]{1,0:T(8,128)} %get-tuple-element.82.early_other) | copy-start | bytes 589828 | tf_op jit(solution)/shard_map/cond
  77.7 1.8 %collective-permute-start.1 = (f32[256,384]{1,0:T(8,128)S(1)}, f32[256,384]{1,0:T(8,128)S(1)}, u32[]{:S(2)}, u32[]{:S(2)}) collective-permute-start(f32[256,384]{1,0:T(8,128)S(1)} %get-tuple-element.74), channel_id=1, source_target_pairs={{0,1},{1,0},{2,3},{3,2},{4,5},{5,4},{6,7},{7,6},{8,9},{9,8},{10,11... | collective-permute-start | bytes 1179656 | tf_op jit(solution)/shard_map/cond/branch_1_fun/ppermute | solution.py:240
  79.5 7.0 %collective-permute-start.2 = (f32[128,384]{1,0:T(8,128)S(1)}, f32[128,384]{1,0:T(8,128)S(1)}, u32[]{:S(2)}, u32[]{:S(2)}) collective-permute-start(f32[128,384]{1,0:T(8,128)S(1)} %get-tuple-element.154), channel_id=1, source_target_pairs={{0,2},{1,3},{2,0},{3,1},{4,6},{5,7},{6,4},{7,5},{8,10},{9,11},{10,... | collective-permute-start | bytes 589832 | tf_op jit(solution)/shard_map/cond/branch_1_fun/ppermute | solution.py:240
  84.7 2.5 %collective-permute-start.3 = (f32[256,512]{1,0:T(8,128)S(1)}, f32[256,512]{1,0:T(8,128)S(1)}, u32[]{:S(2)}, u32[]{:S(2)}) collective-permute-start(f32[256,512]{1,0:T(8,128)S(1)} %get-tuple-element.88), channel_id=1, source_target_pairs={{0,1},{1,0},{2,3},{3,2},{4,5},{5,4},{6,7},{7,6},{8,9},{9,8},{10,11... | collective-permute-start | bytes 1572872 | tf_op jit(solution)/shard_map/cond/branch_1_fun/ppermute | solution.py:240
  87.3 8.9 %copy-start.10 = (f32[128,512]{1,0:T(8,128)}, f32[128,512]{1,0:T(8,128)S(1)}, u32[]{:S(2)}) copy-start(f32[128,512]{1,0:T(8,128)S(1)} %get-tuple-element.145.t2) | copy-start | bytes 786436
  87.3 9.0 %collective-permute-start.17 = (f32[128,512]{1,0:T(8,128)S(1)}, f32[128,512]{1,0:T(8,128)S(1)}, u32[]{:S(2)}, u32[]{:S(2)}) collective-permute-start(f32[128,512]{1,0:T(8,128)S(1)} %get-tuple-element.142), channel_id=1, source_target_pairs={{0,2},{1,3},{2,0},{3,1},{4,6},{5,7},{6,4},{7,5},{8,10},{9,11},{10,... | collective-permute-start | bytes 786440 | tf_op jit(solution)/shard_map/ppermute | solution.py:240
  89.1 11.3 %collective-permute-start.19 = (f32[128,384]{1,0:T(8,128)}, f32[128,384]{1,0:T(8,128)S(1)}, u32[]{:S(2)}, u32[]{:S(2)}) collective-permute-start(f32[128,384]{1,0:T(8,128)} %get-tuple-element.135), channel_id=1, source_target_pairs={{0,4},{1,5},{2,6},{3,7},{4,0},{5,1},{6,2},{7,3},{8,12},{9,13},{10,... | collective-permute-start | bytes 589832 | tf_op jit(solution)/shard_map/ppermute | solution.py:248
  93.6 6.7 %collective-permute-start.20 = (f32[128,384]{1,0:T(8,128)}, f32[128,384]{1,0:T(8,128)S(1)}, u32[]{:S(2)}, u32[]{:S(2)}) collective-permute-start(f32[128,384]{1,0:T(8,128)} %get-tuple-element.135), channel_id=1, source_target_pairs={{4,8},{5,9},{6,10},{7,11},{8,4},{9,5},{10,6},{11,7},{20,24},{21,25... | collective-permute-start | bytes 589832 | tf_op jit(solution)/shard_map/ppermute | solution.py:248
  96.2 1.6 %collective-permute-start.16 = (f32[256,256]{1,0:T(8,128)S(1)}, f32[256,256]{1,0:T(8,128)S(1)}, u32[]{:S(2)}, u32[]{:S(2)}) collective-permute-start(f32[256,256]{1,0:T(8,128)S(1)} %get-tuple-element.140), channel_id=1, source_target_pairs={{0,1},{1,0},{2,3},{3,2},{4,5},{5,4},{6,7},{7,6},{8,9},{9,8},{10,11... | collective-permute-start | bytes 786440 | tf_op jit(solution)/shard_map/ppermute | solution.py:240
  97.8 5.6 %collective-permute-start.18 = (f32[128,256]{1,0:T(8,128)S(1)}, f32[128,256]{1,0:T(8,128)S(1)}, u32[]{:S(2)}, u32[]{:S(2)}) collective-permute-start(f32[128,256]{1,0:T(8,128)S(1)} %slice_add_fusion.8), channel_id=1, source_target_pairs={{0,2},{1,3},{2,0},{3,1},{4,6},{5,7},{6,4},{7,5},{8,10},{9,11},{10,... | collective-permute-start | bytes 393224 | tf_op jit(solution)/shard_map/ppermute | solution.py:240
  (6 other events, 9.5 us)

commit v6 on v5

--- a/solution.py
+++ b/solution.py
@@ -99,10 +99,17 @@
     out[...] = a[...] + b[...]
 
 
-def cross_kernel(at_ref, e0, o0, e1, o1, e2, o2, keep, other, send, cross, packs):
+def part_kernel(e0, o0, e1, o1, out):
+    out[...] = product(side_by_side(e0[...], e1[...]), side_by_side(o0[...], o1[...]))
+
+
+def cross_kernel(at_ref, known, e0, o0, e1, o1, e2, o2, keep, other, send, cross, packs):
     k, odd = at_ref[0], at_ref[1] == 1
     rows = e0.shape[1]
-    cross[...] = product(side_by_side(e0[...], e1[...], e2[...]), side_by_side(o0[...], o1[...], o2[...]))
+    two = known.shape[0]
+    cross[:two, :two] = known[...]
+    cross[two:] = product(e2[...], side_by_side(o0[...], o1[...], o2[...]))
+    cross[:two, two:] = product(side_by_side(e0[...], e1[...]), o2[...])
     upper = k >= 2
     low_2 = jnp.where(upper, 0, jnp.where(k == 1, 1, 2))
     low = (None, jnp.where(upper, 2, 0), low_2, jnp.where(k == 1, 2, 1))
@@ -304,16 +311,17 @@
         near, far, cut = parts(PLANE + 2), parts(3), (PLANE + 2) * rows
         outs = near[:2] + far[:2] + [f32(2 * rows, 9 * rows)]
         *kept, send = call(first_kernel, outs, [], (place,), operands)
+        crossed = call(part_kernel, [f32(2 * rows, 2 * rows)], [], (), (after(operands[5], send), *operands[6:]))[0]
         core = xor(send, 1)
         corner = core[:rows, :cut], core[rows:, :cut], core[:rows, cut:], core[rows:, cut:]
-        return tuple(a + b for a, b in zip(kept, corner))
-
-    t1, out1, *early = fenced(first_part, place, known, *mine, e0, o0, e1, o1)
+        return crossed, *(a + b for a, b in zip(kept, corner))
+
+    crossed, t1, out1, *early = fenced(first_part, place, known, *mine, e0, o0, e1, o1)
     y1 = xor(out1, 2)
 
-    def second_part(place, own, x2, cx, x3, early_keep, early_other, *arrived):
+    def second_part(place, crossed, own, x2, cx, x3, early_keep, early_other, *arrived):
         square, tall = (pltpu.VMEM((n * rows, 3 * rows), jnp.float32) for n in (PLANE - 1, PLANE))
-        keep, other, send = call(cross_kernel, parts(3), [square, tall], (place,), arrived)
+        keep, other, send = call(cross_kernel, parts(3), [square, tall], (place,), (crossed, *arrived))
         half, out = core_sum(keep, other, send)
         far = xor(out, 2)
         place = after(place, out)
@@ -324,7 +332,7 @@
         pack = call(add_kernel, [f32(rows, 3 * rows)], [], (), (half, far), flops=10**11)[0]
         return pack, high, low, *core_sum(k2, other, send)
 
-    pack, high, low, t2, out2 = fenced(second_part, place, *mine, *early, e0, o0, e1, o1, e2, o2)
+    pack, high, low, t2, out2 = fenced(second_part, place, crossed, *mine, *early, e0, o0, e1, o1, e2, o2)
     ez, oz = both(pack, pack)
     y2 = xor(out2, 2)
 

time: 106 us -> 105 us (level)
    ppermute x11, waiting for transfers between devices: 36.8 us -> 32.9 us  [xor(): return lax.ppermute(value, 'blk', [(i, i ^ t) for i in devices])]
    ppermute x10, waiting for transfers between devices: 1.15 us -> 4.44 us  [along(): return lax.ppermute(value, 'blk', route)]
    pallas_call x9 -> x10, Pallas kernels: 25.2 us -> 25.7 us  [call(): pl.pallas_call(kernel, cost_estimate=pl.CostEstimate(flops=flops, bytes_a...]
  transfers between devices with their start and end apart: 21 -> 21, of which waited for: 9 -> 10; matrix products, arithmetic and copies ran while one was open for 8% -> 8% of each run, Pallas kernels for 24% -> 25%
where the time goes in v6:
time: 105 us; the launch traced here: 104 us
  waiting for transfers between devices  37.4 us (36%)
  starting transfers between devices  28 us (27%)
  Pallas kernels  27.2 us (26%)
  other arithmetic  5.83 us (6%)
  local copies, waits for them, and re-layouts  5.5 us (5%)
    ppermute x11, waiting for transfers between devices, xor(): return lax.ppermute(value, 'blk', [(i, i ^ t) for i in devices])  32.9 us
    pallas_call x10, Pallas kernels, call(): pl.pallas_call(kernel, cost_estimate=pl.CostEstimate(flops=flops, bytes_a...  25.7 us
    ppermute x10, starting transfers between devices, along(): return lax.ppermute(value, 'blk', route)  17.8 us
    ppermute x11, starting transfers between devices, xor(): return lax.ppermute(value, 'blk', [(i, i ^ t) for i in devices])  10.2 us
    squeeze x3, local copies, waits for them, and re-layouts, quarter(): lax.dynamic_index_in_dim(after(quarters, *others), index, 0, keepdims=False)  4.65 us
    ppermute x10, waiting for transfers between devices, along(): return lax.ppermute(value, 'blk', route)  4.44 us
  transfers between devices with their start and end apart: 21, of which 10 were waited for; matrix products, arithmetic and copies ran while one was open for 8% of the time, Pallas kernels for 25%

profile of v6, /device:TPU:0, one launch (start us, length us, event | category | flops | bytes accessed | tf_op | source)
XLA Modules:
  0.0 104.3 jit_solution(9239060446636250021)
XLA Ops:
  0.0 2.2 %dynamic-slice_bitcast_fusion.3 = f32[1800,128]{1,0:T(8,128)} fusion(f32[4,1800,128]{2,1,0:T(8,128)} %bitcast.16, s32[]{:T(128)S(6)} %select_n.81), kind=kLoop, calls=%fused_computation.13 | loop fusion | bytes 1843204 | tf_op jit(solution)/shard_map/jit(dynamic_index_in_dim)/squeeze | solution.py:267
  3.9 2.7 %collective-permute-start.5 = (f32[1800,128]{1,0:T(8,128)S(1)}, f32[1800,128]{1,0:T(8,128)S(1)}, u32[]{:S(2)}, u32[]{:S(2)}) collective-permute-start(f32[1800,128]{1,0:T(8,128)S(1)} %dynamic-slice_bitcast_fusion.1), channel_id=1, source_target_pairs={{0,3},{1,2},{2,1},{3,0},{4,7},{5,6},{6,5},{7,4},{8,11},{9,10},{10,... | collective-permute-start | bytes 2764808 | tf_op jit(solution)/shard_map/ppermute | solution.py:247
  6.6 1.3 %broadcast_select_fusion.7 = (f32[1800,128]{1,0:T(8,128)S(1)}, f32[1800,128]{1,0:T(8,128)S(1)}) fusion(f32[1800,128]{1,0:T(8,128)S(1)} %collective-permute-done.4.cx, pred[]{:T(512)S(6)} %or.3, f32[4,1800,128]{2,1,0:T(8,128)} %bitcast.18, s32[]{:T(128)S(6)} %select_n.82), kind=kLoop, calls=%fused_computation.21 | loop fusion | flops 230400 | bytes 3686405 | tf_op jit(solution)/shard_map/jit(_where)/select_n | solution.py:274
  7.9 1.6 %collective-permute-start.6 = (f32[1800,128]{1,0:T(8,128)S(1)}, f32[1800,128]{1,0:T(8,128)S(1)}, u32[]{:S(2)}, u32[]{:S(2)}) collective-permute-start(f32[1800,128]{1,0:T(8,128)S(1)} %get-tuple-element.152), channel_id=1, source_target_pairs={{0,4},{1,5},{2,6},{3,7},{4,0},{5,1},{6,2},{7,3},{8,12},{9,13},{10,... | collective-permute-start | bytes 2764808 | tf_op jit(solution)/shard_map/ppermute | solution.py:255
  10.2 1.2 %dynamic-slice_bitcast_fusion = f32[1800,128]{1,0:T(8,128)S(1)} fusion(f32[4,1800,128]{2,1,0:T(8,128)} %bitcast.19, s32[]{:T(128)S(6)} %select_n.86), kind=kLoop, calls=%fused_computation.10 | loop fusion | bytes 1843204 | tf_op jit(solution)/shard_map/jit(dynamic_index_in_dim)/squeeze | solution.py:267
  11.5 1.3 %collective-permute-start.8 = (f32[1800,128]{1,0:T(8,128)S(1)}, f32[1800,128]{1,0:T(8,128)S(1)}, u32[]{:S(2)}, u32[]{:S(2)}) collective-permute-start(f32[1800,128]{1,0:T(8,128)S(1)} %dynamic-slice_bitcast_fusion), channel_id=1, source_target_pairs={{0,2},{1,3},{2,0},{3,1},{4,6},{5,7},{6,4},{7,5},{8,10},{9,11},{10,... | collective-permute-start | bytes 2764808 | tf_op jit(solution)/shard_map/ppermute | solution.py:247
  12.8 14.6 %collective-permute-done.5.x3 = f32[1800,128]{1,0:T(8,128)S(1)} collective-permute-done((f32[1800,128]{1,0:T(8,128)S(1)}, f32[1800,128]{1,0:T(8,128)S(1)}, u32[]{:S(2)}, u32[]{:S(2)}) %collective-permute-start.5) | collective-permute-done | bytes 921632 | tf_op jit(solution)/shard_map/ppermute | solution.py:247
  28.4 4.4 %collective-permute-start.9 = (f32[1800,128]{1,0:T(8,128)S(1)}, f32[1800,128]{1,0:T(8,128)S(1)}, u32[]{:S(2)}, u32[]{:S(2)}) collective-permute-start(f32[1800,128]{1,0:T(8,128)S(1)} %get-tuple-element.165), channel_id=1, source_target_pairs={{0,4},{1,5},{2,6},{3,7},{4,0},{5,1},{6,2},{7,3},{8,12},{9,13},{10,... | collective-permute-start | bytes 2764808 | tf_op jit(solution)/shard_map/ppermute | solution.py:255
  32.8 4.5 %shard_map.28 = f32[384,640]{1,0:T(8,128)} custom-call(f32[1800,128]{1,0:T(8,128)S(1)} %get-tuple-element.139.own, f32[1800,128]{1,0:T(8,128)S(1)} %collective-permute-done.4.cx, f32[1800,128]{1,0:T(8,128)S(1)} %collective-permute-done.5.x3, f32[1800,128]{1,0:T(8,128)S(1)} %collective-permute-done.6.e0, f32[1800,128]{1,0:T(8,128)S(1)} %collective-permute-done.7.o0), custom_call_target="tpu_custom_call" | custom-call | flops 1000 | bytes 4608000 | tf_op jit(solution)/shard_map/pallas_call | solution.py:217
  37.3 10.0 %collective-permute-done.8 = f32[1800,128]{1,0:T(8,128)S(1)} collective-permute-done((f32[1800,128]{1,0:T(8,128)S(1)}, f32[1800,128]{1,0:T(8,128)S(1)}, u32[]{:S(2)}, u32[]{:S(2)}) %collective-permute-start.8) | collective-permute-done | bytes 921632 | tf_op jit(solution)/shard_map/ppermute | solution.py:247
  47.3 1.5 %select_select_fusion = (f32[1800,128]{1,0:T(8,128)}, f32[1800,128]{1,0:T(8,128)}) fusion(f32[1800,128]{1,0:T(8,128)S(1)} %collective-permute-done.8, f32[1800,128]{1,0:T(8,128)S(1)} %collective-permute-done.5.x3, pred[]{:T(512)S(6)} %xor.12, pred[]{:T(512)S(6)} %or.3), kind=kLoop, calls=%fused_computation.8 | loop fusion | flops 691200 | bytes 3686402 | tf_op jit(solution)/shard_map/jit(_where)/select_n | solution.py:286
  48.8 1.7 %collective-permute-start.11 = (f32[1800,128]{1,0:T(8,128)}, f32[1800,128]{1,0:T(8,128)}, u32[]{:S(2)}, u32[]{:S(2)}) collective-permute-start(f32[1800,128]{1,0:T(8,128)} %get-tuple-element.167), channel_id=1, source_target_pairs={{0,4},{1,5},{2,6},{3,7},{4,0},{5,1},{6,2},{7,3},{8,12},{9,13},{10,... | collective-permute-start | bytes 2764808 | tf_op jit(solution)/shard_map/ppermute | solution.py:255
  50.5 1.6 %collective-permute-start.12 = (f32[1800,128]{1,0:T(8,128)}, f32[1800,128]{1,0:T(8,128)}, u32[]{:S(2)}, u32[]{:S(2)}) collective-permute-start(f32[1800,128]{1,0:T(8,128)} %get-tuple-element.166), channel_id=1, source_target_pairs={{4,8},{5,9},{6,10},{7,11},{8,4},{9,5},{10,6},{11,7},{20,24},{21,25... | collective-permute-start | bytes 2764808 | tf_op jit(solution)/shard_map/ppermute | solution.py:255
  52.1 1.9 %collective-permute-done.9 = f32[1800,128]{1,0:T(8,128)S(1)} collective-permute-done((f32[1800,128]{1,0:T(8,128)S(1)}, f32[1800,128]{1,0:T(8,128)S(1)}, u32[]{:S(2)}, u32[]{:S(2)}) %collective-permute-start.9) | collective-permute-done | bytes 921632 | tf_op jit(solution)/shard_map/ppermute | solution.py:255
  53.9 1.7 %broadcast_select_fusion = (f32[1800,128]{1,0:T(8,128)}, f32[1800,128]{1,0:T(8,128)}) fusion(pred[]{:T(512)S(6)} %xor.12, f32[1800,128]{1,0:T(8,128)S(1)} %collective-permute-done.5.x3, f32[1800,128]{1,0:T(8,128)S(1)} %collective-permute-done.8, pred[]{:T(512)S(6)} %or.3, f32[1800,128]{1,0:T(8,128)S(1)} %get-tuple-element.139.own, ...), kind=kLoop, calls=%fused_computation.14 | loop fusion | flops 921600 | bytes 5529602 | tf_op jit(solution)/shard_map/jit(_where)/select_n | solution.py:291
  55.6 2.2 %collective-permute-start.13 = (f32[1800,128]{1,0:T(8,128)}, f32[1800,128]{1,0:T(8,128)S(1)}, u32[]{:S(2)}, u32[]{:S(2)}) collective-permute-start(f32[1800,128]{1,0:T(8,128)} %get-tuple-element.163), channel_id=1, source_target_pairs={{0,4},{1,5},{2,6},{3,7},{4,0},{5,1},{6,2},{7,3},{8,12},{9,13},{10,... | collective-permute-start | bytes 2764808 | tf_op jit(solution)/shard_map/ppermute | solution.py:255
  58.8 10.5 %conditional.2 = (f32[256,256]{1,0:T(8,128)S(1)}, f32[128,768]{1,0:T(8,128)S(1)}, f32[128,768]{1,0:T(8,128)}, f32[128,384]{1,0:T(8,128)S(1)}, f32[128,384]{1,0:T(8,128)S(1)}) conditional(s32[]{:T(128)} %convert_element_type.2, () %tuple.33, (s32[4]{0:T(128)S(1)}, f32[384,640]{1,0:T(8,128)}, f32[1800,128]{1,0:T(8,128)}, f32[1800,128]{1,0:T(8,128)}, ...), branch_computations={%region_0.1_spmd, %region_1.2_spmd} | conditional | flops 296912 | bytes 35045568 | solution.py:306
  58.8 6.7 %branch_1_fun.6 = (f32[128,768]{1,0:T(8,128)S(1)}, f32[128,768]{1,0:T(8,128)S(1)}, f32[128,384]{1,0:T(8,128)S(1)}, f32[128,384]{1,0:T(8,128)S(1)}, f32[256,1152]{1,0:T(8,128)S(1)}) custom-call(s32[4]{0:T(128)S(1)} %get-tuple-element.54.at_ref, f32[384,640]{1,0:T(8,128)} %get-tuple-element.55.known, f32[1800,128]{1,0:T(8,128)} %get-tuple-element.56.own, ...), custom_call_target="tpu_custom_call" | custom-call | flops 1000 | bytes 8355840 | tf_op jit(solution)/shard_map/cond/branch_1_fun/pallas_call | solution.py:217
  66.7 1.7 %collective-permute-done = f32[256,1152]{1,0:T(8,128)S(1)} collective-permute-done((f32[256,1152]{1,0:T(8,128)S(1)}, f32[256,1152]{1,0:T(8,128)S(1)}, u32[]{:S(2)}, u32[]{:S(2)}) %collective-permute-start) | collective-permute-done | bytes 1179680 | tf_op jit(solution)/shard_map/cond/branch_1_fun/ppermute | solution.py:247
  71.2 2.6 %collective-permute-done.11 = f32[1800,128]{1,0:T(8,128)} collective-permute-done((f32[1800,128]{1,0:T(8,128)}, f32[1800,128]{1,0:T(8,128)}, u32[]{:S(2)}, u32[]{:S(2)}) %collective-permute-start.11) | collective-permute-done | bytes 921632 | tf_op jit(solution)/shard_map/ppermute | solution.py:255
  73.8 14.2 %conditional.3 = (f32[128,384]{1,0:T(8,128)}, bf16[512,1800]{1,0:T(8,128)(2,1)S(1)}, bf16[512,1800]{1,0:T(8,128)(2,1)S(1)}, f32[128,512]{1,0:T(8,128)S(1)}, f32[128,512]{1,0:T(8,128)S(1)}) conditional(s32[]{:T(128)} %convert_element_type.2, () %tuple.32, (s32[4]{0:T(128)S(1)}, f32[256,256]{1,0:T(8,128)}, f32[1800,128]{1,0:T(8,128)}, ...), branch_computations={%region_2.3_spmd, %region_3.4_spmd} | conditional | flops 100000227328 | bytes 34062580 | solution.py:306
  73.8 4.5 %branch_1_fun.8 = (f32[128,384]{1,0:T(8,128)S(1)}, f32[128,384]{1,0:T(8,128)S(1)}, f32[256,384]{1,0:T(8,128)S(1)}) custom-call(s32[4]{0:T(128)S(1)} %get-tuple-element.81.at_ref, f32[256,256]{1,0:T(8,128)} %get-tuple-element.70.known, f32[1800,128]{1,0:T(8,128)} %get-tuple-element.71.e0, f32[1800,128]{1,0:T(8,128)} %get-tuple-element.72.o0, ...), custom_call_target="tpu_custom_call" | custom-call | flops 1000 | bytes 5791744 | tf_op jit(solution)/shard_map/cond/branch_1_fun/pallas_call | solution.py:217
  78.6 1.5 %collective-permute-done.1 = f32[256,384]{1,0:T(8,128)S(1)} collective-permute-done((f32[256,384]{1,0:T(8,128)S(1)}, f32[256,384]{1,0:T(8,128)S(1)}, u32[]{:S(2)}, u32[]{:S(2)}) %collective-permute-start.1) | collective-permute-done | bytes 393248 | tf_op jit(solution)/shard_map/cond/branch_1_fun/ppermute | solution.py:247
  80.1 1.4 %collective-permute-start.2 = (f32[128,384]{1,0:T(8,128)S(1)}, f32[128,384]{1,0:T(8,128)S(1)}, u32[]{:S(2)}, u32[]{:S(2)}) collective-permute-start(f32[128,384]{1,0:T(8,128)S(1)} %get-tuple-element.160), channel_id=1, source_target_pairs={{0,2},{1,3},{2,0},{3,1},{4,6},{5,7},{6,4},{7,5},{8,10},{9,11},{10,... | collective-permute-start | bytes 589832 | tf_op jit(solution)/shard_map/cond/branch_1_fun/ppermute | solution.py:247
  81.5 3.4 %branch_1_fun.9 = (f32[128,512]{1,0:T(8,128)S(1)}, f32[128,512]{1,0:T(8,128)S(1)}, f32[256,512]{1,0:T(8,128)S(1)}) custom-call(s32[4]{0:T(128)S(1)} %get-tuple-element.81.at_ref, f32[1800,128]{1,0:T(8,128)S(1)} %copy-done.3, f32[1800,128]{1,0:T(8,128)S(1)} %copy-done.5, f32[1800,128]{1,0:T(8,128)S(1)} %get-tuple-element.83.cx, f32[1800,128]{1,0:T(8,128)S(1)} %copy-done.1, ...), custom_call_target="tpu_custom_call" | custom-call | flops 1000 | bytes 5922816 | tf_op jit(solution)/shard_map/cond/branch_1_fun/pallas_call | solution.py:217
  88.0 1.5 %collective-permute-start.17 = (f32[128,512]{1,0:T(8,128)S(1)}, f32[128,512]{1,0:T(8,128)S(1)}, u32[]{:S(2)}, u32[]{:S(2)}) collective-permute-start(f32[128,512]{1,0:T(8,128)S(1)} %get-tuple-element.148), channel_id=1, source_target_pairs={{0,2},{1,3},{2,0},{3,1},{4,6},{5,7},{6,4},{7,5},{8,10},{9,11},{10,... | collective-permute-start | bytes 786440 | tf_op jit(solution)/shard_map/ppermute | solution.py:247
  89.5 3.4 %collective-permute-start.19 = (f32[128,384]{1,0:T(8,128)}, f32[128,384]{1,0:T(8,128)S(1)}, u32[]{:S(2)}, u32[]{:S(2)}) collective-permute-start(f32[128,384]{1,0:T(8,128)} %get-tuple-element.141), channel_id=1, source_target_pairs={{0,4},{1,5},{2,6},{3,7},{4,0},{5,1},{6,2},{7,3},{8,12},{9,13},{10,... | collective-permute-start | bytes 589832 | tf_op jit(solution)/shard_map/ppermute | solution.py:255
  93.6 1.9 %shard_map.29 = (f32[128,256]{1,0:T(8,128)S(1)}, f32[128,256]{1,0:T(8,128)S(1)}, f32[256,256]{1,0:T(8,128)S(1)}) custom-call(bf16[512,1800]{1,0:T(8,128)(2,1)S(1)} %get-tuple-element.133.high, bf16[512,1800]{1,0:T(8,128)(2,1)S(1)} %get-tuple-element.134.low, f32[1800,128]{1,0:T(8,128)S(1)} %collective-permute-done.13.e3, ...), custom_call_target="tpu_custom_call" | custom-call | flops 1000 | bytes 9216000 | tf_op jit(solution)/shard_map/pallas_call | solution.py:217
  95.7 1.4 %collective-permute-done.16.c3 = f32[256,256]{1,0:T(8,128)S(1)} collective-permute-done((f32[256,256]{1,0:T(8,128)S(1)}, f32[256,256]{1,0:T(8,128)S(1)}, u32[]{:S(2)}, u32[]{:S(2)}) %collective-permute-start.16) | collective-permute-done | bytes 262176 | tf_op jit(solution)/shard_map/ppermute | solution.py:247
  98.2 1.9 %shard_map.31.band = f32[128,1920]{1,0:T(8,128)} custom-call(s32[4]{0:T(128)S(1)} %pad_add_fusion.at_ref, s32[16,8]{1,0:T(8,128)S(1)} %copy.5.pairs, f32[128,768]{1,0:T(8,128)S(1)} %get-tuple-element.150.t1, f32[128,768]{1,0:T(8,128)S(1)} %collective-permute-done.15.y1, f32[128,512]{1,0:T(8,128)S(1)} %copy-done.16, f32[128,512]{1,0:T(8,128)S(1)} %shard_map.30.y2), custom_call_target="tpu_custom_call" | custom-call | flops 1000 | bytes 1310720 | tf_op jit(solution)/shard_map/pallas_call | solution.py:217
  100.0 2.7 %collective-permute-done.18.y3 = f32[128,256]{1,0:T(8,128)S(1)} collective-permute-done((f32[128,256]{1,0:T(8,128)S(1)}, f32[128,256]{1,0:T(8,128)S(1)}, u32[]{:S(2)}, u32[]{:S(2)}) %collective-permute-start.18) | collective-permute-done | bytes 131104 | tf_op jit(solution)/shard_map/ppermute | solution.py:247
  102.7 1.5 %shard_map.32 = f32[128,1920]{1,0:T(8,128)} custom-call(s32[4]{0:T(128)S(1)} %pad_add_fusion.at_ref, s32[16,8]{1,0:T(8,128)S(1)} %copy.5.pairs, f32[128,256]{1,0:T(8,128)S(1)} %get-tuple-element.145.k3, f32[256,256]{1,0:T(8,128)S(1)} %collective-permute-done.16.c3, f32[128,256]{1,0:T(8,128)S(1)} %collective-permute-done.18.y3, ...), custom_call_target="tpu_custom_call", output_to_operand_aliasing={{}: (7, {})} | custom-call | tf_op jit(solution)/shard_map/pallas_call | solution.py:348
  (73 shorter events, 13.8 us)
Async XLA Ops:
  2.2 4.4 %collective-permute-start.4 = (f32[1800,128]{1,0:T(8,128)}, f32[1800,128]{1,0:T(8,128)S(1)}, u32[]{:S(2)}, u32[]{:S(2)}) collective-permute-start(f32[1800,128]{1,0:T(8,128)} %dynamic-slice_bitcast_fusion.3), channel_id=1, source_target_pairs={{0,1},{1,0},{2,3},{3,2},{4,5},{5,4},{6,7},{7,6},{8,9},{9,8},{10,11... | collective-permute-start | bytes 2764808 | tf_op jit(solution)/shard_map/ppermute | solution.py:247
  3.9 23.5 %collective-permute-start.5 = (f32[1800,128]{1,0:T(8,128)S(1)}, f32[1800,128]{1,0:T(8,128)S(1)}, u32[]{:S(2)}, u32[]{:S(2)}) collective-permute-start(f32[1800,128]{1,0:T(8,128)S(1)} %dynamic-slice_bitcast_fusion.1), channel_id=1, source_target_pairs={{0,3},{1,2},{2,1},{3,0},{4,7},{5,6},{6,5},{7,4},{8,11},{9,10},{10,... | collective-permute-start | bytes 2764808 | tf_op jit(solution)/shard_map/ppermute | solution.py:247
  7.9 46.1 %copy-start.2 = (f32[1800,128]{1,0:T(8,128)}, f32[1800,128]{1,0:T(8,128)S(1)}, u32[]{:S(2)}) copy-start(f32[1800,128]{1,0:T(8,128)S(1)} %get-tuple-element.139.own) | copy-start | bytes 2764804
  7.9 24.9 %collective-permute-start.6 = (f32[1800,128]{1,0:T(8,128)S(1)}, f32[1800,128]{1,0:T(8,128)S(1)}, u32[]{:S(2)}, u32[]{:S(2)}) collective-permute-start(f32[1800,128]{1,0:T(8,128)S(1)} %get-tuple-element.152), channel_id=1, source_target_pairs={{0,4},{1,5},{2,6},{3,7},{4,0},{5,1},{6,2},{7,3},{8,12},{9,13},{10,... | collective-permute-start | bytes 2764808 | tf_op jit(solution)/shard_map/ppermute | solution.py:255
  9.5 23.2 %collective-permute-start.7 = (f32[1800,128]{1,0:T(8,128)S(1)}, f32[1800,128]{1,0:T(8,128)S(1)}, u32[]{:S(2)}, u32[]{:S(2)}) collective-permute-start(f32[1800,128]{1,0:T(8,128)S(1)} %get-tuple-element.152), channel_id=1, source_target_pairs={{4,8},{5,9},{6,10},{7,11},{8,4},{9,5},{10,6},{11,7},{20,24},{21,25... | collective-permute-start | bytes 2764808 | tf_op jit(solution)/shard_map/ppermute | solution.py:255
  11.5 35.8 %collective-permute-start.8 = (f32[1800,128]{1,0:T(8,128)S(1)}, f32[1800,128]{1,0:T(8,128)S(1)}, u32[]{:S(2)}, u32[]{:S(2)}) collective-permute-start(f32[1800,128]{1,0:T(8,128)S(1)} %dynamic-slice_bitcast_fusion), channel_id=1, source_target_pairs={{0,2},{1,3},{2,0},{3,1},{4,6},{5,7},{6,4},{7,5},{8,10},{9,11},{10,... | collective-permute-start | bytes 2764808 | tf_op jit(solution)/shard_map/ppermute | solution.py:247
  27.4 26.6 %copy-start = (f32[1800,128]{1,0:T(8,128)}, f32[1800,128]{1,0:T(8,128)S(1)}, u32[]{:S(2)}) copy-start(f32[1800,128]{1,0:T(8,128)S(1)} %collective-permute-done.5.x3) | copy-start | bytes 2764804
  27.6 24.4 %collective-permute-start.10 = (f32[1800,128]{1,0:T(8,128)S(1)}, f32[1800,128]{1,0:T(8,128)S(1)}, u32[]{:S(2)}, u32[]{:S(2)}) collective-permute-start(f32[1800,128]{1,0:T(8,128)S(1)} %get-tuple-element.164), channel_id=1, source_target_pairs={{4,8},{5,9},{6,10},{7,11},{8,4},{9,5},{10,6},{11,7},{20,24},{21,25... | collective-permute-start | bytes 2764808 | tf_op jit(solution)/shard_map/ppermute | solution.py:255
  28.4 25.6 %collective-permute-start.9 = (f32[1800,128]{1,0:T(8,128)S(1)}, f32[1800,128]{1,0:T(8,128)S(1)}, u32[]{:S(2)}, u32[]{:S(2)}) collective-permute-start(f32[1800,128]{1,0:T(8,128)S(1)} %get-tuple-element.165), channel_id=1, source_target_pairs={{0,4},{1,5},{2,6},{3,7},{4,0},{5,1},{6,2},{7,3},{8,12},{9,13},{10,... | collective-permute-start | bytes 2764808 | tf_op jit(solution)/shard_map/ppermute | solution.py:255
  47.3 8.3 %copy-start.4 = (f32[1800,128]{1,0:T(8,128)}, f32[1800,128]{1,0:T(8,128)S(1)}, u32[]{:S(2)}) copy-start(f32[1800,128]{1,0:T(8,128)S(1)} %collective-permute-done.8) | copy-start | bytes 2764804
  48.8 25.0 %collective-permute-start.11 = (f32[1800,128]{1,0:T(8,128)}, f32[1800,128]{1,0:T(8,128)}, u32[]{:S(2)}, u32[]{:S(2)}) collective-permute-start(f32[1800,128]{1,0:T(8,128)} %get-tuple-element.167), channel_id=1, source_target_pairs={{0,4},{1,5},{2,6},{3,7},{4,0},{5,1},{6,2},{7,3},{8,12},{9,13},{10,... | collective-permute-start | bytes 2764808 | tf_op jit(solution)/shard_map/ppermute | solution.py:255
  50.5 23.3 %collective-permute-start.12 = (f32[1800,128]{1,0:T(8,128)}, f32[1800,128]{1,0:T(8,128)}, u32[]{:S(2)}, u32[]{:S(2)}) collective-permute-start(f32[1800,128]{1,0:T(8,128)} %get-tuple-element.166), channel_id=1, source_target_pairs={{4,8},{5,9},{6,10},{7,11},{8,4},{9,5},{10,6},{11,7},{20,24},{21,25... | collective-permute-start | bytes 2764808 | tf_op jit(solution)/shard_map/ppermute | solution.py:255
  55.6 37.9 %collective-permute-start.13 = (f32[1800,128]{1,0:T(8,128)}, f32[1800,128]{1,0:T(8,128)S(1)}, u32[]{:S(2)}, u32[]{:S(2)}) collective-permute-start(f32[1800,128]{1,0:T(8,128)} %get-tuple-element.163), channel_id=1, source_target_pairs={{0,4},{1,5},{2,6},{3,7},{4,0},{5,1},{6,2},{7,3},{8,12},{9,13},{10,... | collective-permute-start | bytes 2764808 | tf_op jit(solution)/shard_map/ppermute | solution.py:255
  57.8 35.8 %collective-permute-start.14 = (f32[1800,128]{1,0:T(8,128)}, f32[1800,128]{1,0:T(8,128)S(1)}, u32[]{:S(2)}, u32[]{:S(2)}) collective-permute-start(f32[1800,128]{1,0:T(8,128)} %get-tuple-element.162), channel_id=1, source_target_pairs={{4,8},{5,9},{6,10},{7,11},{8,4},{9,5},{10,6},{11,7},{20,24},{21,25... | collective-permute-start | bytes 2764808 | tf_op jit(solution)/shard_map/ppermute | solution.py:255
  58.8 6.8 %copy-start.7 = (f32[1800,128]{1,0:T(8,128)S(1)}, f32[1800,128]{1,0:T(8,128)}, u32[]{:S(2)}) copy-start(f32[1800,128]{1,0:T(8,128)} %get-tuple-element.64.e0) | copy-start | bytes 2764804 | tf_op jit(solution)/shard_map/cond
  58.8 6.8 %copy-start.9 = (f32[1800,128]{1,0:T(8,128)S(1)}, f32[1800,128]{1,0:T(8,128)}, u32[]{:S(2)}) copy-start(f32[1800,128]{1,0:T(8,128)} %get-tuple-element.60.o0) | copy-start | bytes 2764804 | tf_op jit(solution)/shard_map/cond
  58.8 6.8 %copy-start.11 = (f32[1800,128]{1,0:T(8,128)S(1)}, f32[1800,128]{1,0:T(8,128)}, u32[]{:S(2)}) copy-start(f32[1800,128]{1,0:T(8,128)} %get-tuple-element.62.o1) | copy-start | bytes 2764804 | tf_op jit(solution)/shard_map/cond
  58.8 6.8 %copy-start.13 = (f32[1800,128]{1,0:T(8,128)S(1)}, f32[1800,128]{1,0:T(8,128)}, u32[]{:S(2)}) copy-start(f32[1800,128]{1,0:T(8,128)} %get-tuple-element.61.e1) | copy-start | bytes 2764804 | tf_op jit(solution)/shard_map/cond
  65.5 2.9 %collective-permute-start = (f32[256,1152]{1,0:T(8,128)S(1)}, f32[256,1152]{1,0:T(8,128)S(1)}, u32[]{:S(2)}, u32[]{:S(2)}) collective-permute-start(f32[256,1152]{1,0:T(8,128)S(1)} %get-tuple-element.63), channel_id=1, source_target_pairs={{0,1},{1,0},{2,3},{3,2},{4,5},{5,4},{6,7},{7,6},{8,9},{9,8},{10,11... | collective-permute-start | bytes 3538952 | tf_op jit(solution)/shard_map/cond/branch_1_fun/ppermute | solution.py:247
  70.0 22.9 %collective-permute-start.15 = (f32[128,768]{1,0:T(8,128)}, f32[128,768]{1,0:T(8,128)S(1)}, u32[]{:S(2)}, u32[]{:S(2)}) collective-permute-start(f32[128,768]{1,0:T(8,128)} %get-tuple-element.142), channel_id=1, source_target_pairs={{0,2},{1,3},{2,0},{3,1},{4,6},{5,7},{6,4},{7,5},{8,10},{9,11},{10,... | collective-permute-start | bytes 1179656 | tf_op jit(solution)/shard_map/ppermute | solution.py:247
  73.8 7.7 %copy-start.1 = (f32[1800,128]{1,0:T(8,128)S(1)}, f32[1800,128]{1,0:T(8,128)}, u32[]{:S(2)}) copy-start(f32[1800,128]{1,0:T(8,128)} %get-tuple-element.84.x3) | copy-start | bytes 2764804 | tf_op jit(solution)/shard_map/cond
  73.8 7.7 %copy-start.3 = (f32[1800,128]{1,0:T(8,128)S(1)}, f32[1800,128]{1,0:T(8,128)}, u32[]{:S(2)}) copy-start(f32[1800,128]{1,0:T(8,128)} %get-tuple-element.88.own) | copy-start | bytes 2764804 | tf_op jit(solution)/shard_map/cond
  73.8 7.7 %copy-start.5 = (f32[1800,128]{1,0:T(8,128)S(1)}, f32[1800,128]{1,0:T(8,128)}, u32[]{:S(2)}) copy-start(f32[1800,128]{1,0:T(8,128)} %get-tuple-element.82.x2) | copy-start | bytes 2764804 | tf_op jit(solution)/shard_map/cond
  78.3 1.8 %collective-permute-start.1 = (f32[256,384]{1,0:T(8,128)S(1)}, f32[256,384]{1,0:T(8,128)S(1)}, u32[]{:S(2)}, u32[]{:S(2)}) collective-permute-start(f32[256,384]{1,0:T(8,128)S(1)} %get-tuple-element.78), channel_id=1, source_target_pairs={{0,1},{1,0},{2,3},{3,2},{4,5},{5,4},{6,7},{7,6},{8,9},{9,8},{10,11... | collective-permute-start | bytes 1179656 | tf_op jit(solution)/shard_map/cond/branch_1_fun/ppermute | solution.py:247
  80.1 7.1 %collective-permute-start.2 = (f32[128,384]{1,0:T(8,128)S(1)}, f32[128,384]{1,0:T(8,128)S(1)}, u32[]{:S(2)}, u32[]{:S(2)}) collective-permute-start(f32[128,384]{1,0:T(8,128)S(1)} %get-tuple-element.160), channel_id=1, source_target_pairs={{0,2},{1,3},{2,0},{3,1},{4,6},{5,7},{6,4},{7,5},{8,10},{9,11},{10,... | collective-permute-start | bytes 589832 | tf_op jit(solution)/shard_map/cond/branch_1_fun/ppermute | solution.py:247
  84.9 3.0 %collective-permute-start.3 = (f32[256,512]{1,0:T(8,128)S(1)}, f32[256,512]{1,0:T(8,128)S(1)}, u32[]{:S(2)}, u32[]{:S(2)}) collective-permute-start(f32[256,512]{1,0:T(8,128)S(1)} %get-tuple-element.92), channel_id=1, source_target_pairs={{0,1},{1,0},{2,3},{3,2},{4,5},{5,4},{6,7},{7,6},{8,9},{9,8},{10,11... | collective-permute-start | bytes 1572872 | tf_op jit(solution)/shard_map/cond/branch_1_fun/ppermute | solution.py:247
  88.0 7.4 %copy-start.15 = (f32[128,512]{1,0:T(8,128)}, f32[128,512]{1,0:T(8,128)S(1)}, u32[]{:S(2)}) copy-start(f32[128,512]{1,0:T(8,128)S(1)} %get-tuple-element.151.t2) | copy-start | bytes 786436
  88.0 7.7 %collective-permute-start.17 = (f32[128,512]{1,0:T(8,128)S(1)}, f32[128,512]{1,0:T(8,128)S(1)}, u32[]{:S(2)}, u32[]{:S(2)}) collective-permute-start(f32[128,512]{1,0:T(8,128)S(1)} %get-tuple-element.148), channel_id=1, source_target_pairs={{0,2},{1,3},{2,0},{3,1},{4,6},{5,7},{6,4},{7,5},{8,10},{9,11},{10,... | collective-permute-start | bytes 786440 | tf_op jit(solution)/shard_map/ppermute | solution.py:247
  89.5 10.5 %collective-permute-start.19 = (f32[128,384]{1,0:T(8,128)}, f32[128,384]{1,0:T(8,128)S(1)}, u32[]{:S(2)}, u32[]{:S(2)}) collective-permute-start(f32[128,384]{1,0:T(8,128)} %get-tuple-element.141), channel_id=1, source_target_pairs={{0,4},{1,5},{2,6},{3,7},{4,0},{5,1},{6,2},{7,3},{8,12},{9,13},{10,... | collective-permute-start | bytes 589832 | tf_op jit(solution)/shard_map/ppermute | solution.py:255
  92.9 7.1 %collective-permute-start.20 = (f32[128,384]{1,0:T(8,128)}, f32[128,384]{1,0:T(8,128)S(1)}, u32[]{:S(2)}, u32[]{:S(2)}) collective-permute-start(f32[128,384]{1,0:T(8,128)} %get-tuple-element.141), channel_id=1, source_target_pairs={{4,8},{5,9},{6,10},{7,11},{8,4},{9,5},{10,6},{11,7},{20,24},{21,25... | collective-permute-start | bytes 589832 | tf_op jit(solution)/shard_map/ppermute | solution.py:255
  95.5 1.6 %collective-permute-start.16 = (f32[256,256]{1,0:T(8,128)S(1)}, f32[256,256]{1,0:T(8,128)S(1)}, u32[]{:S(2)}, u32[]{:S(2)}) collective-permute-start(f32[256,256]{1,0:T(8,128)S(1)} %get-tuple-element.146), channel_id=1, source_target_pairs={{0,1},{1,0},{2,3},{3,2},{4,5},{5,4},{6,7},{7,6},{8,9},{9,8},{10,11... | collective-permute-start | bytes 786440 | tf_op jit(solution)/shard_map/ppermute | solution.py:247
  97.1 5.6 %collective-permute-start.18 = (f32[128,256]{1,0:T(8,128)S(1)}, f32[128,256]{1,0:T(8,128)S(1)}, u32[]{:S(2)}, u32[]{:S(2)}) collective-permute-start(f32[128,256]{1,0:T(8,128)S(1)} %slice_add_fusion.8), channel_id=1, source_target_pairs={{0,2},{1,3},{2,0},{3,1},{4,6},{5,7},{6,4},{7,5},{8,10},{9,11},{10,... | collective-permute-start | bytes 393224 | tf_op jit(solution)/shard_map/ppermute | solution.py:247
  (7 other events, 20.3 us)

commit v7 on v6

--- a/solution.py
+++ b/solution.py
@@ -99,17 +99,28 @@
     out[...] = a[...] + b[...]
 
 
-def part_kernel(e0, o0, e1, o1, out):
-    out[...] = product(side_by_side(e0[...], e1[...]), side_by_side(o0[...], o1[...]))
-
-
-def cross_kernel(at_ref, known, e0, o0, e1, o1, e2, o2, keep, other, send, cross, packs):
+def turned_product(high, low, columns):
+    ch, cl = halves(columns)
+    dot = functools.partial(jnp.dot, preferred_element_type=jnp.float32)
+    width = columns.shape[1]
+    main = dot(high[...], side_by_side(ch, cl))
+    return main[:, :width] + (main[:, width:] + dot(low[...], ch))
+
+
+def part_kernel(e0, o0, e1, o1, out, high, low):
+    rows = e0.shape[1]
+    for i, ref in enumerate((e0, e1)):
+        high[block(i, rows)], low[block(i, rows)] = halves(ref[...].T)
+    out[...] = turned_product(high, low, side_by_side(o0[...], o1[...]))
+
+
+def cross_kernel(at_ref, known, turned_high, turned_low, o0, o1, e2, o2, keep, other, send, cross, packs):
     k, odd = at_ref[0], at_ref[1] == 1
-    rows = e0.shape[1]
+    rows = e2.shape[1]
     two = known.shape[0]
     cross[:two, :two] = known[...]
     cross[two:] = product(e2[...], side_by_side(o0[...], o1[...], o2[...]))
-    cross[:two, two:] = product(side_by_side(e0[...], e1[...]), o2[...])
+    cross[:two, two:] = turned_product(turned_high, turned_low, o2[...])
     upper = k >= 2
     low_2 = jnp.where(upper, 0, jnp.where(k == 1, 1, 2))
     low = (None, jnp.where(upper, 2, 0), low_2, jnp.where(k == 1, 2, 1))
@@ -236,7 +247,7 @@
     reach = pair_list.shape[1] - 1
     me = lax.axis_index("blk").astype(jnp.int32)
     k = me % PLANE
-    odd = (me // PLANE) % 2
+    odd = (me // PLANE + 1) % 2
     upper = k >= 2
     outer = (k == 0) | (k == 3)
     flip = upper ^ (odd == 1)
@@ -249,7 +260,7 @@
     def along(value, parity):
         route = []
         for i in devices:
-            j = i + (PLANE if i // PLANE % 2 == parity else -PLANE)
+            j = i + (PLANE if (i // PLANE + 1) % 2 == parity else -PLANE)
             if j in devices:
                 route.append((i, j))
         return lax.ppermute(value, "blk", route)
@@ -311,28 +322,30 @@
         near, far, cut = parts(PLANE + 2), parts(3), (PLANE + 2) * rows
         outs = near[:2] + far[:2] + [f32(2 * rows, 9 * rows)]
         *kept, send = call(first_kernel, outs, [], (place,), operands)
-        crossed = call(part_kernel, [f32(2 * rows, 2 * rows)], [], (), (after(operands[5], send), *operands[6:]))[0]
+        turned = [jax.ShapeDtypeStruct((2 * rows, depth), jnp.bfloat16)] * 2
+        arrived = (after(operands[5], send), *operands[6:])
+        crossed = call(part_kernel, [f32(2 * rows, 2 * rows), *turned], [], (), arrived)
         core = xor(send, 1)
         corner = core[:rows, :cut], core[rows:, :cut], core[:rows, cut:], core[rows:, cut:]
-        return crossed, *(a + b for a, b in zip(kept, corner))
-
-    crossed, t1, out1, *early = fenced(first_part, place, known, *mine, e0, o0, e1, o1)
+        return *crossed, *(a + b for a, b in zip(kept, corner))
+
+    *crossed, t1, out1, early_keep, early_other = fenced(first_part, place, known, *mine, e0, o0, e1, o1)
     y1 = xor(out1, 2)
 
     def second_part(place, crossed, own, x2, cx, x3, early_keep, early_other, *arrived):
         square, tall = (pltpu.VMEM((n * rows, 3 * rows), jnp.float32) for n in (PLANE - 1, PLANE))
-        keep, other, send = call(cross_kernel, parts(3), [square, tall], (place,), (crossed, *arrived))
+        keep, other, send = call(cross_kernel, parts(3), [square, tall], (place,), (*crossed, *arrived))
         half, out = core_sum(keep, other, send)
         far = xor(out, 2)
         place = after(place, out)
-        k2, other, send = call(second_kernel, parts(4), [], (place,), (own, x2, cx, x3, *arrived[4:], early_keep, early_other))
+        k2, other, send = call(second_kernel, parts(4), [], (place,), (own, x2, cx, x3, *arrived[2:], early_keep, early_other))
         turned = [jax.ShapeDtypeStruct((PLANE * rows, depth), jnp.bfloat16)] * 2
         high, low = call(turn_kernel, turned, [], (), (after(own, k2), x2, cx, x3))
         half = after(half, high)
         pack = call(add_kernel, [f32(rows, 3 * rows)], [], (), (half, far), flops=10**11)[0]
         return pack, high, low, *core_sum(k2, other, send)
 
-    pack, high, low, t2, out2 = fenced(second_part, place, crossed, *mine, *early, e0, o0, e1, o1, e2, o2)
+    pack, high, low, t2, out2 = fenced(second_part, place, tuple(crossed), *mine, early_keep, early_other, o0, o1, e2, o2)
     ez, oz = both(pack, pack)
     y2 = xor(out2, 2)
 

time: 105 us -> 104 us (level)
    ppermute x10, waiting for transfers between devices: 4.44 us -> 1.56 us  [along(): return lax.ppermute(value, 'blk', route)]
    ppermute x11, waiting for transfers between devices: 32.9 us -> 35.7 us  [xor(): return lax.ppermute(value, 'blk', [(i, i ^ t) for i in devices])]
  transfers between devices with their start and end apart: 21 -> 21, of which waited for: 10 -> 10; matrix products, arithmetic and copies ran while one was open for 8% -> 8% of each run, Pallas kernels for 25% -> 24%
where the time goes in v7:
time: 104 us
  waiting for transfers between devices  37.2 us (36%)
  starting transfers between devices  27.8 us (27%)
  Pallas kernels  26.8 us (26%)
  other arithmetic  5.99 us (6%)
  local copies, waits for them, and re-layouts  5.49 us (5%)
    ppermute x11, waiting for transfers between devices, xor(): return lax.ppermute(value, 'blk', [(i, i ^ t) for i in devices])  35.7 us
    pallas_call x10, Pallas kernels, call(): pl.pallas_call(kernel, cost_estimate=pl.CostEstimate(flops=flops, bytes_a...  25.3 us
    ppermute x10, starting transfers between devices, along(): return lax.ppermute(value, 'blk', route)  17.6 us
    ppermute x11, starting transfers between devices, xor(): return lax.ppermute(value, 'blk', [(i, i ^ t) for i in devices])  10.2 us
    squeeze x3, local copies, waits for them, and re-layouts, quarter(): lax.dynamic_index_in_dim(after(quarters, *others), index, 0, keepdims=False)  4.65 us
  transfers between devices with their start and end apart: 21, of which 10 were waited for; matrix products, arithmetic and copies ran while one was open for 8% of the time, Pallas kernels for 24%

profile of v7, /device:TPU:0, one launch (start us, length us, event | category | flops | bytes accessed | tf_op | source)
XLA Modules:
  0.0 103.8 jit_solution(17191934856920414623)
XLA Ops:
  0.0 2.2 %dynamic-slice_bitcast_fusion.3 = f32[1800,128]{1,0:T(8,128)} fusion(f32[4,1800,128]{2,1,0:T(8,128)} %bitcast.16, s32[]{:T(128)S(6)} %select_n.81), kind=kLoop, calls=%fused_computation.13 | loop fusion | bytes 1843204 | tf_op jit(solution)/shard_map/jit(dynamic_index_in_dim)/squeeze | solution.py:278
  2.6 1.2 %dynamic-slice_bitcast_fusion.1 = f32[1800,128]{1,0:T(8,128)S(1)} fusion(f32[4,1800,128]{2,1,0:T(8,128)} %bitcast.17, s32[]{:T(128)S(6)} %select_n.83), kind=kLoop, calls=%fused_computation.11 | loop fusion | bytes 1843204 | tf_op jit(solution)/shard_map/jit(dynamic_index_in_dim)/squeeze | solution.py:278
  3.9 2.7 %collective-permute-start.5 = (f32[1800,128]{1,0:T(8,128)S(1)}, f32[1800,128]{1,0:T(8,128)S(1)}, u32[]{:S(2)}, u32[]{:S(2)}) collective-permute-start(f32[1800,128]{1,0:T(8,128)S(1)} %dynamic-slice_bitcast_fusion.1), channel_id=1, source_target_pairs={{0,3},{1,2},{2,1},{3,0},{4,7},{5,6},{6,5},{7,4},{8,11},{9,10},{10,... | collective-permute-start | bytes 2764808 | tf_op jit(solution)/shard_map/ppermute | solution.py:258
  6.6 1.3 %broadcast_select_fusion.7 = (f32[1800,128]{1,0:T(8,128)S(1)}, f32[1800,128]{1,0:T(8,128)S(1)}) fusion(f32[1800,128]{1,0:T(8,128)S(1)} %collective-permute-done.4.cx, pred[]{:T(512)S(6)} %or.3, f32[4,1800,128]{2,1,0:T(8,128)} %bitcast.18, s32[]{:T(128)S(6)} %select_n.82), kind=kLoop, calls=%fused_computation.21 | loop fusion | flops 230400 | bytes 3686405 | tf_op jit(solution)/shard_map/jit(_where)/select_n | solution.py:285
  7.9 1.6 %collective-permute-start.7 = (f32[1800,128]{1,0:T(8,128)S(1)}, f32[1800,128]{1,0:T(8,128)S(1)}, u32[]{:S(2)}, u32[]{:S(2)}) collective-permute-start(f32[1800,128]{1,0:T(8,128)S(1)} %get-tuple-element.159), channel_id=1, source_target_pairs={{0,4},{1,5},{2,6},{3,7},{4,0},{5,1},{6,2},{7,3},{8,12},{9,13},{10,... | collective-permute-start | bytes 2764808 | tf_op jit(solution)/shard_map/ppermute | solution.py:266
  10.2 1.2 %dynamic-slice_bitcast_fusion = f32[1800,128]{1,0:T(8,128)S(1)} fusion(f32[4,1800,128]{2,1,0:T(8,128)} %bitcast.19, s32[]{:T(128)S(6)} %select_n.86), kind=kLoop, calls=%fused_computation.10 | loop fusion | bytes 1843204 | tf_op jit(solution)/shard_map/jit(dynamic_index_in_dim)/squeeze | solution.py:278
  11.5 1.3 %collective-permute-start.8 = (f32[1800,128]{1,0:T(8,128)S(1)}, f32[1800,128]{1,0:T(8,128)S(1)}, u32[]{:S(2)}, u32[]{:S(2)}) collective-permute-start(f32[1800,128]{1,0:T(8,128)S(1)} %dynamic-slice_bitcast_fusion), channel_id=1, source_target_pairs={{0,2},{1,3},{2,0},{3,1},{4,6},{5,7},{6,4},{7,5},{8,10},{9,11},{10,... | collective-permute-start | bytes 2764808 | tf_op jit(solution)/shard_map/ppermute | solution.py:258
  12.8 14.6 %collective-permute-done.5.x3 = f32[1800,128]{1,0:T(8,128)S(1)} collective-permute-done((f32[1800,128]{1,0:T(8,128)S(1)}, f32[1800,128]{1,0:T(8,128)S(1)}, u32[]{:S(2)}, u32[]{:S(2)}) %collective-permute-start.5) | collective-permute-done | bytes 921632 | tf_op jit(solution)/shard_map/ppermute | solution.py:258
  27.6 1.6 %collective-permute-start.10 = (f32[1800,128]{1,0:T(8,128)S(1)}, f32[1800,128]{1,0:T(8,128)S(1)}, u32[]{:S(2)}, u32[]{:S(2)}) collective-permute-start(f32[1800,128]{1,0:T(8,128)S(1)} %get-tuple-element.171), channel_id=1, source_target_pairs={{0,4},{1,5},{2,6},{3,7},{4,0},{5,1},{6,2},{7,3},{8,12},{9,13},{10,... | collective-permute-start | bytes 2764808 | tf_op jit(solution)/shard_map/ppermute | solution.py:266
  30.3 4.5 %shard_map.28 = f32[384,640]{1,0:T(8,128)} custom-call(f32[1800,128]{1,0:T(8,128)S(1)} %get-tuple-element.146.own, f32[1800,128]{1,0:T(8,128)S(1)} %collective-permute-done.4.cx, f32[1800,128]{1,0:T(8,128)S(1)} %collective-permute-done.5.x3, f32[1800,128]{1,0:T(8,128)S(1)} %collective-permute-done.6.e0, f32[1800,128]{1,0:T(8,128)S(1)} %collective-permute-done.7.o0), custom_call_target="tpu_custom_call" | custom-call | flops 1000 | bytes 4608000 | tf_op jit(solution)/shard_map/pallas_call | solution.py:228
  34.8 12.5 %collective-permute-done.8 = f32[1800,128]{1,0:T(8,128)S(1)} collective-permute-done((f32[1800,128]{1,0:T(8,128)S(1)}, f32[1800,128]{1,0:T(8,128)S(1)}, u32[]{:S(2)}, u32[]{:S(2)}) %collective-permute-start.8) | collective-permute-done | bytes 921632 | tf_op jit(solution)/shard_map/ppermute | solution.py:258
  47.3 1.5 %select_select_fusion = (f32[1800,128]{1,0:T(8,128)}, f32[1800,128]{1,0:T(8,128)}) fusion(f32[1800,128]{1,0:T(8,128)S(1)} %collective-permute-done.8, f32[1800,128]{1,0:T(8,128)S(1)} %collective-permute-done.5.x3, pred[]{:T(512)S(6)} %xor.12, pred[]{:T(512)S(6)} %or.3), kind=kLoop, calls=%fused_computation.8 | loop fusion | flops 691200 | bytes 3686402 | tf_op jit(solution)/shard_map/jit(_where)/select_n | solution.py:297
  48.8 1.7 %collective-permute-start.12 = (f32[1800,128]{1,0:T(8,128)}, f32[1800,128]{1,0:T(8,128)}, u32[]{:S(2)}, u32[]{:S(2)}) collective-permute-start(f32[1800,128]{1,0:T(8,128)} %get-tuple-element.173), channel_id=1, source_target_pairs={{0,4},{1,5},{2,6},{3,7},{4,0},{5,1},{6,2},{7,3},{8,12},{9,13},{10,... | collective-permute-start | bytes 2764808 | tf_op jit(solution)/shard_map/ppermute | solution.py:266
  50.5 1.6 %collective-permute-start.11 = (f32[1800,128]{1,0:T(8,128)}, f32[1800,128]{1,0:T(8,128)}, u32[]{:S(2)}, u32[]{:S(2)}) collective-permute-start(f32[1800,128]{1,0:T(8,128)} %get-tuple-element.174), channel_id=1, source_target_pairs={{4,8},{5,9},{6,10},{7,11},{8,4},{9,5},{10,6},{11,7},{20,24},{21,25... | collective-permute-start | bytes 2764808 | tf_op jit(solution)/shard_map/ppermute | solution.py:266
  52.1 1.8 %broadcast_select_fusion = (f32[1800,128]{1,0:T(8,128)}, f32[1800,128]{1,0:T(8,128)}) fusion(pred[]{:T(512)S(6)} %xor.12, f32[1800,128]{1,0:T(8,128)S(1)} %collective-permute-done.5.x3, f32[1800,128]{1,0:T(8,128)S(1)} %collective-permute-done.8, pred[]{:T(512)S(6)} %or.3, f32[1800,128]{1,0:T(8,128)S(1)} %get-tuple-element.146.own, ...), kind=kLoop, calls=%fused_computation.14 | loop fusion | flops 921600 | bytes 5529602 | tf_op jit(solution)/shard_map/jit(_where)/select_n | solution.py:302
  53.9 3.5 %collective-permute-start.14 = (f32[1800,128]{1,0:T(8,128)}, f32[1800,128]{1,0:T(8,128)S(1)}, u32[]{:S(2)}, u32[]{:S(2)}) collective-permute-start(f32[1800,128]{1,0:T(8,128)} %get-tuple-element.169), channel_id=1, source_target_pairs={{0,4},{1,5},{2,6},{3,7},{4,0},{5,1},{6,2},{7,3},{8,12},{9,13},{10,... | collective-permute-start | bytes 2764808 | tf_op jit(solution)/shard_map/ppermute | solution.py:266
  58.4 10.5 %conditional.2 = (f32[256,256]{1,0:T(8,128)S(1)}, bf16[256,1800]{1,0:T(8,128)(2,1)S(1)}, bf16[256,1800]{1,0:T(8,128)(2,1)S(1)}, f32[128,768]{1,0:T(8,128)S(1)}, ...) conditional(s32[]{:T(128)} %convert_element_type.2, () %tuple.33, (s32[4]{0:T(128)S(1)}, ...), branch_computations={%region_0.1_spmd, %region_1.2_spmd} | conditional | flops 296912 | bytes 35045584 | solution.py:317
  58.5 6.7 %branch_1_fun.6 = (f32[128,768]{1,0:T(8,128)S(1)}, f32[128,768]{1,0:T(8,128)S(1)}, f32[128,384]{1,0:T(8,128)S(1)}, f32[128,384]{1,0:T(8,128)S(1)}, f32[256,1152]{1,0:T(8,128)S(1)}) custom-call(s32[4]{0:T(128)S(1)} %get-tuple-element.54.at_ref, f32[384,640]{1,0:T(8,128)} %get-tuple-element.55.known, f32[1800,128]{1,0:T(8,128)} %get-tuple-element.56.own, ...), custom_call_target="tpu_custom_call" | custom-call | flops 1000 | bytes 8355840 | tf_op jit(solution)/shard_map/cond/branch_1_fun/pallas_call | solution.py:228
  65.2 1.3 %branch_1_fun.7 = (f32[256,256]{1,0:T(8,128)S(1)}, bf16[256,1800]{1,0:T(8,128)(2,1)S(1)}, bf16[256,1800]{1,0:T(8,128)(2,1)S(1)}) custom-call(f32[1800,128]{1,0:T(8,128)S(1)} %copy-done.11, f32[1800,128]{1,0:T(8,128)S(1)} %copy-done.7, f32[1800,128]{1,0:T(8,128)S(1)} %copy-done.13, f32[1800,128]{1,0:T(8,128)S(1)} %copy-done.9), custom_call_target="tpu_custom_call" | custom-call | flops 1000 | bytes 3686400 | tf_op jit(solution)/shard_map/cond/branch_1_fun/pallas_call | solution.py:228
  66.6 1.5 %collective-permute-done = f32[256,1152]{1,0:T(8,128)S(1)} collective-permute-done((f32[256,1152]{1,0:T(8,128)S(1)}, f32[256,1152]{1,0:T(8,128)S(1)}, u32[]{:S(2)}, u32[]{:S(2)}) %collective-permute-start) | collective-permute-done | bytes 1179680 | tf_op jit(solution)/shard_map/cond/branch_1_fun/ppermute | solution.py:258
  69.7 1.5 %collective-permute-start.15 = (f32[128,768]{1,0:T(8,128)}, f32[128,768]{1,0:T(8,128)S(1)}, u32[]{:S(2)}, u32[]{:S(2)}) collective-permute-start(f32[128,768]{1,0:T(8,128)} %get-tuple-element.149), channel_id=1, source_target_pairs={{0,2},{1,3},{2,0},{3,1},{4,6},{5,7},{6,4},{7,5},{8,10},{9,11},{10,... | collective-permute-start | bytes 1179656 | tf_op jit(solution)/shard_map/ppermute | solution.py:258
  72.4 14.1 %conditional.3 = (f32[128,384]{1,0:T(8,128)}, bf16[512,1800]{1,0:T(8,128)(2,1)S(1)}, bf16[512,1800]{1,0:T(8,128)(2,1)S(1)}, f32[128,512]{1,0:T(8,128)S(1)}, f32[128,512]{1,0:T(8,128)S(1)}) conditional(s32[]{:T(128)} %convert_element_type.2, () %tuple.32, (s32[4]{0:T(128)S(1)}, f32[256,256]{1,0:T(8,128)}, bf16[256,1800]{1,0:T(8,128)(2,1)S(1)}, ...), branch_computations={%region_2.3_spmd, %region_3.4_spmd} | conditional | flops 100000227328 | bytes 35905780 | solution.py:317
  72.4 3.9 %branch_1_fun.8 = (f32[128,384]{1,0:T(8,128)S(1)}, f32[128,384]{1,0:T(8,128)S(1)}, f32[256,384]{1,0:T(8,128)S(1)}) custom-call(s32[4]{0:T(128)S(1)} %get-tuple-element.84.at_ref, f32[256,256]{1,0:T(8,128)} %get-tuple-element.73.known, bf16[256,1800]{1,0:T(8,128)(2,1)S(1)} %get-tuple-element.74.turned_high, ...), custom_call_target="tpu_custom_call" | custom-call | flops 1000 | bytes 7634944 | tf_op jit(solution)/shard_map/cond/branch_1_fun/pallas_call | solution.py:228
  76.4 1.7 %collective-permute-done.1 = f32[256,384]{1,0:T(8,128)S(1)} collective-permute-done((f32[256,384]{1,0:T(8,128)S(1)}, f32[256,384]{1,0:T(8,128)S(1)}, u32[]{:S(2)}, u32[]{:S(2)}) %collective-permute-start.1) | collective-permute-done | bytes 393248 | tf_op jit(solution)/shard_map/cond/branch_1_fun/ppermute | solution.py:258
  78.2 1.8 %collective-permute-start.2 = (f32[128,384]{1,0:T(8,128)S(1)}, f32[128,384]{1,0:T(8,128)S(1)}, u32[]{:S(2)}, u32[]{:S(2)}) collective-permute-start(f32[128,384]{1,0:T(8,128)S(1)} %get-tuple-element.167), channel_id=1, source_target_pairs={{0,2},{1,3},{2,0},{3,1},{4,6},{5,7},{6,4},{7,5},{8,10},{9,11},{10,... | collective-permute-start | bytes 589832 | tf_op jit(solution)/shard_map/cond/branch_1_fun/ppermute | solution.py:258
  80.0 3.4 %branch_1_fun.9 = (f32[128,512]{1,0:T(8,128)S(1)}, f32[128,512]{1,0:T(8,128)S(1)}, f32[256,512]{1,0:T(8,128)S(1)}) custom-call(s32[4]{0:T(128)S(1)} %get-tuple-element.84.at_ref, f32[1800,128]{1,0:T(8,128)S(1)} %copy-done.3, f32[1800,128]{1,0:T(8,128)S(1)} %copy-done.5, f32[1800,128]{1,0:T(8,128)S(1)} %get-tuple-element.86.cx, f32[1800,128]{1,0:T(8,128)S(1)} %copy-done.1, ...), custom_call_target="tpu_custom_call" | custom-call | flops 1000 | bytes 5922816 | tf_op jit(solution)/shard_map/cond/branch_1_fun/pallas_call | solution.py:228
  87.8 4.6 %collective-permute-start.20 = (f32[128,384]{1,0:T(8,128)}, f32[128,384]{1,0:T(8,128)S(1)}, u32[]{:S(2)}, u32[]{:S(2)}) collective-permute-start(f32[128,384]{1,0:T(8,128)} %get-tuple-element.148), channel_id=1, source_target_pairs={{0,4},{1,5},{2,6},{3,7},{4,0},{5,1},{6,2},{7,3},{8,12},{9,13},{10,... | collective-permute-start | bytes 589832 | tf_op jit(solution)/shard_map/ppermute | solution.py:266
  93.0 1.9 %shard_map.29 = (f32[128,256]{1,0:T(8,128)S(1)}, f32[128,256]{1,0:T(8,128)S(1)}, f32[256,256]{1,0:T(8,128)S(1)}) custom-call(bf16[512,1800]{1,0:T(8,128)(2,1)S(1)} %get-tuple-element.140.high, bf16[512,1800]{1,0:T(8,128)(2,1)S(1)} %get-tuple-element.141.low, f32[1800,128]{1,0:T(8,128)S(1)} %collective-permute-done.13.e3, ...), custom_call_target="tpu_custom_call" | custom-call | flops 1000 | bytes 9216000 | tf_op jit(solution)/shard_map/pallas_call | solution.py:228
  95.1 1.5 %collective-permute-done.16.c3 = f32[256,256]{1,0:T(8,128)S(1)} collective-permute-done((f32[256,256]{1,0:T(8,128)S(1)}, f32[256,256]{1,0:T(8,128)S(1)}, u32[]{:S(2)}, u32[]{:S(2)}) %collective-permute-start.16) | collective-permute-done | bytes 262176 | tf_op jit(solution)/shard_map/ppermute | solution.py:258
  97.6 1.9 %shard_map.31.band = f32[128,1920]{1,0:T(8,128)} custom-call(s32[4]{0:T(128)S(1)} %pad_add_fusion.at_ref, s32[16,8]{1,0:T(8,128)S(1)} %copy.5.pairs, f32[128,768]{1,0:T(8,128)S(1)} %get-tuple-element.157.t1, f32[128,768]{1,0:T(8,128)S(1)} %collective-permute-done.15.y1, f32[128,512]{1,0:T(8,128)S(1)} %copy-done.16, f32[128,512]{1,0:T(8,128)S(1)} %shard_map.30.y2), custom_call_target="tpu_custom_call" | custom-call | flops 1000 | bytes 1310720 | tf_op jit(solution)/shard_map/pallas_call | solution.py:228
  99.5 2.7 %collective-permute-done.18.y3 = f32[128,256]{1,0:T(8,128)S(1)} collective-permute-done((f32[128,256]{1,0:T(8,128)S(1)}, f32[128,256]{1,0:T(8,128)S(1)}, u32[]{:S(2)}, u32[]{:S(2)}) %collective-permute-start.18) | collective-permute-done | bytes 131104 | tf_op jit(solution)/shard_map/ppermute | solution.py:258
  102.2 1.5 %shard_map.32 = f32[128,1920]{1,0:T(8,128)} custom-call(s32[4]{0:T(128)S(1)} %pad_add_fusion.at_ref, s32[16,8]{1,0:T(8,128)S(1)} %copy.5.pairs, f32[128,256]{1,0:T(8,128)S(1)} %get-tuple-element.152.k3, f32[256,256]{1,0:T(8,128)S(1)} %collective-permute-done.16.c3, f32[128,256]{1,0:T(8,128)S(1)} %collective-permute-done.18.y3, ...), custom_call_target="tpu_custom_call", output_to_operand_aliasing={{}: (7, {})} | custom-call | tf_op jit(solution)/shard_map/pallas_call | solution.py:361
  (73 shorter events, 12.7 us)
Async XLA Ops:
  2.2 4.4 %collective-permute-start.4 = (f32[1800,128]{1,0:T(8,128)}, f32[1800,128]{1,0:T(8,128)S(1)}, u32[]{:S(2)}, u32[]{:S(2)}) collective-permute-start(f32[1800,128]{1,0:T(8,128)} %dynamic-slice_bitcast_fusion.3), channel_id=1, source_target_pairs={{0,1},{1,0},{2,3},{3,2},{4,5},{5,4},{6,7},{7,6},{8,9},{9,8},{10,11... | collective-permute-start | bytes 2764808 | tf_op jit(solution)/shard_map/ppermute | solution.py:258
  3.9 23.5 %collective-permute-start.5 = (f32[1800,128]{1,0:T(8,128)S(1)}, f32[1800,128]{1,0:T(8,128)S(1)}, u32[]{:S(2)}, u32[]{:S(2)}) collective-permute-start(f32[1800,128]{1,0:T(8,128)S(1)} %dynamic-slice_bitcast_fusion.1), channel_id=1, source_target_pairs={{0,3},{1,2},{2,1},{3,0},{4,7},{5,6},{6,5},{7,4},{8,11},{9,10},{10,... | collective-permute-start | bytes 2764808 | tf_op jit(solution)/shard_map/ppermute | solution.py:258
  7.9 44.2 %copy-start.2 = (f32[1800,128]{1,0:T(8,128)}, f32[1800,128]{1,0:T(8,128)S(1)}, u32[]{:S(2)}) copy-start(f32[1800,128]{1,0:T(8,128)S(1)} %get-tuple-element.146.own) | copy-start | bytes 2764804
  7.9 22.4 %collective-permute-start.7 = (f32[1800,128]{1,0:T(8,128)S(1)}, f32[1800,128]{1,0:T(8,128)S(1)}, u32[]{:S(2)}, u32[]{:S(2)}) collective-permute-start(f32[1800,128]{1,0:T(8,128)S(1)} %get-tuple-element.159), channel_id=1, source_target_pairs={{0,4},{1,5},{2,6},{3,7},{4,0},{5,1},{6,2},{7,3},{8,12},{9,13},{10,... | collective-permute-start | bytes 2764808 | tf_op jit(solution)/shard_map/ppermute | solution.py:266
  9.5 20.8 %collective-permute-start.6 = (f32[1800,128]{1,0:T(8,128)S(1)}, f32[1800,128]{1,0:T(8,128)S(1)}, u32[]{:S(2)}, u32[]{:S(2)}) collective-permute-start(f32[1800,128]{1,0:T(8,128)S(1)} %get-tuple-element.159), channel_id=1, source_target_pairs={{4,8},{5,9},{6,10},{7,11},{8,4},{9,5},{10,6},{11,7},{20,24},{21,25... | collective-permute-start | bytes 2764808 | tf_op jit(solution)/shard_map/ppermute | solution.py:266
  11.5 35.8 %collective-permute-start.8 = (f32[1800,128]{1,0:T(8,128)S(1)}, f32[1800,128]{1,0:T(8,128)S(1)}, u32[]{:S(2)}, u32[]{:S(2)}) collective-permute-start(f32[1800,128]{1,0:T(8,128)S(1)} %dynamic-slice_bitcast_fusion), channel_id=1, source_target_pairs={{0,2},{1,3},{2,0},{3,1},{4,6},{5,7},{6,4},{7,5},{8,10},{9,11},{10,... | collective-permute-start | bytes 2764808 | tf_op jit(solution)/shard_map/ppermute | solution.py:258
  27.4 24.7 %copy-start = (f32[1800,128]{1,0:T(8,128)}, f32[1800,128]{1,0:T(8,128)S(1)}, u32[]{:S(2)}) copy-start(f32[1800,128]{1,0:T(8,128)S(1)} %collective-permute-done.5.x3) | copy-start | bytes 2764804
  27.6 24.4 %collective-permute-start.10 = (f32[1800,128]{1,0:T(8,128)S(1)}, f32[1800,128]{1,0:T(8,128)S(1)}, u32[]{:S(2)}, u32[]{:S(2)}) collective-permute-start(f32[1800,128]{1,0:T(8,128)S(1)} %get-tuple-element.171), channel_id=1, source_target_pairs={{0,4},{1,5},{2,6},{3,7},{4,0},{5,1},{6,2},{7,3},{8,12},{9,13},{10,... | collective-permute-start | bytes 2764808 | tf_op jit(solution)/shard_map/ppermute | solution.py:266
  29.3 22.8 %collective-permute-start.9 = (f32[1800,128]{1,0:T(8,128)S(1)}, f32[1800,128]{1,0:T(8,128)S(1)}, u32[]{:S(2)}, u32[]{:S(2)}) collective-permute-start(f32[1800,128]{1,0:T(8,128)S(1)} %get-tuple-element.172), channel_id=1, source_target_pairs={{4,8},{5,9},{6,10},{7,11},{8,4},{9,5},{10,6},{11,7},{20,24},{21,25... | collective-permute-start | bytes 2764808 | tf_op jit(solution)/shard_map/ppermute | solution.py:266
  47.3 6.6 %copy-start.4 = (f32[1800,128]{1,0:T(8,128)}, f32[1800,128]{1,0:T(8,128)S(1)}, u32[]{:S(2)}) copy-start(f32[1800,128]{1,0:T(8,128)S(1)} %collective-permute-done.8) | copy-start | bytes 2764804
  48.8 23.6 %collective-permute-start.12 = (f32[1800,128]{1,0:T(8,128)}, f32[1800,128]{1,0:T(8,128)}, u32[]{:S(2)}, u32[]{:S(2)}) collective-permute-start(f32[1800,128]{1,0:T(8,128)} %get-tuple-element.173), channel_id=1, source_target_pairs={{0,4},{1,5},{2,6},{3,7},{4,0},{5,1},{6,2},{7,3},{8,12},{9,13},{10,... | collective-permute-start | bytes 2764808 | tf_op jit(solution)/shard_map/ppermute | solution.py:266
  50.5 21.9 %collective-permute-start.11 = (f32[1800,128]{1,0:T(8,128)}, f32[1800,128]{1,0:T(8,128)}, u32[]{:S(2)}, u32[]{:S(2)}) collective-permute-start(f32[1800,128]{1,0:T(8,128)} %get-tuple-element.174), channel_id=1, source_target_pairs={{4,8},{5,9},{6,10},{7,11},{8,4},{9,5},{10,6},{11,7},{20,24},{21,25... | collective-permute-start | bytes 2764808 | tf_op jit(solution)/shard_map/ppermute | solution.py:266
  53.9 39.1 %collective-permute-start.14 = (f32[1800,128]{1,0:T(8,128)}, f32[1800,128]{1,0:T(8,128)S(1)}, u32[]{:S(2)}, u32[]{:S(2)}) collective-permute-start(f32[1800,128]{1,0:T(8,128)} %get-tuple-element.169), channel_id=1, source_target_pairs={{0,4},{1,5},{2,6},{3,7},{4,0},{5,1},{6,2},{7,3},{8,12},{9,13},{10,... | collective-permute-start | bytes 2764808 | tf_op jit(solution)/shard_map/ppermute | solution.py:266
  57.5 35.6 %collective-permute-start.13 = (f32[1800,128]{1,0:T(8,128)}, f32[1800,128]{1,0:T(8,128)S(1)}, u32[]{:S(2)}, u32[]{:S(2)}) collective-permute-start(f32[1800,128]{1,0:T(8,128)} %get-tuple-element.170), channel_id=1, source_target_pairs={{4,8},{5,9},{6,10},{7,11},{8,4},{9,5},{10,6},{11,7},{20,24},{21,25... | collective-permute-start | bytes 2764808 | tf_op jit(solution)/shard_map/ppermute | solution.py:266
  58.4 6.8 %copy-start.7 = (f32[1800,128]{1,0:T(8,128)S(1)}, f32[1800,128]{1,0:T(8,128)}, u32[]{:S(2)}) copy-start(f32[1800,128]{1,0:T(8,128)} %get-tuple-element.60.o0) | copy-start | bytes 2764804 | tf_op jit(solution)/shard_map/cond
  58.4 6.8 %copy-start.9 = (f32[1800,128]{1,0:T(8,128)S(1)}, f32[1800,128]{1,0:T(8,128)}, u32[]{:S(2)}) copy-start(f32[1800,128]{1,0:T(8,128)} %get-tuple-element.62.o1) | copy-start | bytes 2764804 | tf_op jit(solution)/shard_map/cond
  58.4 6.8 %copy-start.11 = (f32[1800,128]{1,0:T(8,128)S(1)}, f32[1800,128]{1,0:T(8,128)}, u32[]{:S(2)}) copy-start(f32[1800,128]{1,0:T(8,128)} %get-tuple-element.64.e0) | copy-start | bytes 2764804 | tf_op jit(solution)/shard_map/cond
  58.4 6.8 %copy-start.13 = (f32[1800,128]{1,0:T(8,128)S(1)}, f32[1800,128]{1,0:T(8,128)}, u32[]{:S(2)}) copy-start(f32[1800,128]{1,0:T(8,128)} %get-tuple-element.61.e1) | copy-start | bytes 2764804 | tf_op jit(solution)/shard_map/cond
  65.1 2.9 %collective-permute-start = (f32[256,1152]{1,0:T(8,128)S(1)}, f32[256,1152]{1,0:T(8,128)S(1)}, u32[]{:S(2)}, u32[]{:S(2)}) collective-permute-start(f32[256,1152]{1,0:T(8,128)S(1)} %get-tuple-element.63), channel_id=1, source_target_pairs={{0,1},{1,0},{2,3},{3,2},{4,5},{5,4},{6,7},{7,6},{8,9},{9,8},{10,11... | collective-permute-start | bytes 3538952 | tf_op jit(solution)/shard_map/cond/branch_1_fun/ppermute | solution.py:258
  69.7 22.7 %collective-permute-start.15 = (f32[128,768]{1,0:T(8,128)}, f32[128,768]{1,0:T(8,128)S(1)}, u32[]{:S(2)}, u32[]{:S(2)}) collective-permute-start(f32[128,768]{1,0:T(8,128)} %get-tuple-element.149), channel_id=1, source_target_pairs={{0,2},{1,3},{2,0},{3,1},{4,6},{5,7},{6,4},{7,5},{8,10},{9,11},{10,... | collective-permute-start | bytes 1179656 | tf_op jit(solution)/shard_map/ppermute | solution.py:258
  72.4 7.5 %copy-start.1 = (f32[1800,128]{1,0:T(8,128)S(1)}, f32[1800,128]{1,0:T(8,128)}, u32[]{:S(2)}) copy-start(f32[1800,128]{1,0:T(8,128)} %get-tuple-element.87.x3) | copy-start | bytes 2764804 | tf_op jit(solution)/shard_map/cond
  72.4 7.5 %copy-start.3 = (f32[1800,128]{1,0:T(8,128)S(1)}, f32[1800,128]{1,0:T(8,128)}, u32[]{:S(2)}) copy-start(f32[1800,128]{1,0:T(8,128)} %get-tuple-element.91.own) | copy-start | bytes 2764804 | tf_op jit(solution)/shard_map/cond
  72.4 7.5 %copy-start.5 = (f32[1800,128]{1,0:T(8,128)S(1)}, f32[1800,128]{1,0:T(8,128)}, u32[]{:S(2)}) copy-start(f32[1800,128]{1,0:T(8,128)} %get-tuple-element.85.x2) | copy-start | bytes 2764804 | tf_op jit(solution)/shard_map/cond
  76.4 1.8 %collective-permute-start.1 = (f32[256,384]{1,0:T(8,128)S(1)}, f32[256,384]{1,0:T(8,128)S(1)}, u32[]{:S(2)}, u32[]{:S(2)}) collective-permute-start(f32[256,384]{1,0:T(8,128)S(1)} %get-tuple-element.81), channel_id=1, source_target_pairs={{0,1},{1,0},{2,3},{3,2},{4,5},{5,4},{6,7},{7,6},{8,9},{9,8},{10,11... | collective-permute-start | bytes 1179656 | tf_op jit(solution)/shard_map/cond/branch_1_fun/ppermute | solution.py:258
  78.2 7.0 %collective-permute-start.2 = (f32[128,384]{1,0:T(8,128)S(1)}, f32[128,384]{1,0:T(8,128)S(1)}, u32[]{:S(2)}, u32[]{:S(2)}) collective-permute-start(f32[128,384]{1,0:T(8,128)S(1)} %get-tuple-element.167), channel_id=1, source_target_pairs={{0,2},{1,3},{2,0},{3,1},{4,6},{5,7},{6,4},{7,5},{8,10},{9,11},{10,... | collective-permute-start | bytes 589832 | tf_op jit(solution)/shard_map/cond/branch_1_fun/ppermute | solution.py:258
  84.5 2.0 %collective-permute-start.3 = (f32[256,512]{1,0:T(8,128)S(1)}, f32[256,512]{1,0:T(8,128)S(1)}, u32[]{:S(2)}, u32[]{:S(2)}) collective-permute-start(f32[256,512]{1,0:T(8,128)S(1)} %get-tuple-element.95), channel_id=1, source_target_pairs={{0,1},{1,0},{2,3},{3,2},{4,5},{5,4},{6,7},{7,6},{8,9},{9,8},{10,11... | collective-permute-start | bytes 1572872 | tf_op jit(solution)/shard_map/cond/branch_1_fun/ppermute | solution.py:258
  86.5 8.4 %copy-start.15 = (f32[128,512]{1,0:T(8,128)}, f32[128,512]{1,0:T(8,128)S(1)}, u32[]{:S(2)}) copy-start(f32[128,512]{1,0:T(8,128)S(1)} %get-tuple-element.158.t2) | copy-start | bytes 786436
  86.6 8.5 %collective-permute-start.17 = (f32[128,512]{1,0:T(8,128)S(1)}, f32[128,512]{1,0:T(8,128)S(1)}, u32[]{:S(2)}, u32[]{:S(2)}) collective-permute-start(f32[128,512]{1,0:T(8,128)S(1)} %get-tuple-element.155), channel_id=1, source_target_pairs={{0,2},{1,3},{2,0},{3,1},{4,6},{5,7},{6,4},{7,5},{8,10},{9,11},{10,... | collective-permute-start | bytes 786440 | tf_op jit(solution)/shard_map/ppermute | solution.py:258
  87.8 11.7 %collective-permute-start.20 = (f32[128,384]{1,0:T(8,128)}, f32[128,384]{1,0:T(8,128)S(1)}, u32[]{:S(2)}, u32[]{:S(2)}) collective-permute-start(f32[128,384]{1,0:T(8,128)} %get-tuple-element.148), channel_id=1, source_target_pairs={{0,4},{1,5},{2,6},{3,7},{4,0},{5,1},{6,2},{7,3},{8,12},{9,13},{10,... | collective-permute-start | bytes 589832 | tf_op jit(solution)/shard_map/ppermute | solution.py:266
  92.4 7.1 %collective-permute-start.19 = (f32[128,384]{1,0:T(8,128)}, f32[128,384]{1,0:T(8,128)S(1)}, u32[]{:S(2)}, u32[]{:S(2)}) collective-permute-start(f32[128,384]{1,0:T(8,128)} %get-tuple-element.148), channel_id=1, source_target_pairs={{4,8},{5,9},{6,10},{7,11},{8,4},{9,5},{10,6},{11,7},{20,24},{21,25... | collective-permute-start | bytes 589832 | tf_op jit(solution)/shard_map/ppermute | solution.py:266
  95.0 1.6 %collective-permute-start.16 = (f32[256,256]{1,0:T(8,128)S(1)}, f32[256,256]{1,0:T(8,128)S(1)}, u32[]{:S(2)}, u32[]{:S(2)}) collective-permute-start(f32[256,256]{1,0:T(8,128)S(1)} %get-tuple-element.153), channel_id=1, source_target_pairs={{0,1},{1,0},{2,3},{3,2},{4,5},{5,4},{6,7},{7,6},{8,9},{9,8},{10,11... | collective-permute-start | bytes 786440 | tf_op jit(solution)/shard_map/ppermute | solution.py:258
  96.6 5.6 %collective-permute-start.18 = (f32[128,256]{1,0:T(8,128)S(1)}, f32[128,256]{1,0:T(8,128)S(1)}, u32[]{:S(2)}, u32[]{:S(2)}) collective-permute-start(f32[128,256]{1,0:T(8,128)S(1)} %slice_add_fusion.8), channel_id=1, source_target_pairs={{0,2},{1,3},{2,0},{3,1},{4,6},{5,7},{6,4},{7,5},{8,10},{9,11},{10,... | collective-permute-start | bytes 393224 | tf_op jit(solution)/shard_map/ppermute | solution.py:258
  (7 other events, 18.6 us)
